TPU v7x, 256 devices: a whole 4x4x8 slice. The times are simulated.
256 devices in a mesh: row: 8 (over z), col: 32 (over y, x, core).
Axes of the slice: x: 4, y: 4, z: 8, core: 2. Of those that a mesh axis runs over, the one named last changes fastest.
Arguments:
- image_embed: bfloat16 [8192, 768], P(('row', 'col')), may hold values from -64 to 64
- text_embed: bfloat16 [8192, 768], P(('col', 'row')), may hold values from -16 to 16
- partner: int32 [8192], P(('row', 'col')), may hold values from 0 to 8191, as said below
Outputs:
- loss: float32 [], replicated
- image_grad: float32 [8192, 768], P(('row', 'col'))
- text_grad: float32 [8192, 768], P(('col', 'row'))
Inputs may be any that keep to these rules, and one draw needn't show every extreme that they name: partner is a permutation: every text matches exactly one image.
All inputs are finite; a program needn't handle non-finite values.
Results may differ from a plain program's by a relative error of at most 0.0075.
Values may be sent and summed in bfloat16 or wider, within the bound.
No kernel may reach another device: no remote copies, remote signals or barrier semaphores. Data moves between devices by JAX's collectives and lax.ppermute only.
A program may use at most 64 MiB of HBM per device.

v0:
```python
import functools

import jax
import jax.numpy as jnp
from jax import lax
from jax.experimental import pallas as pl
from jax.experimental.pallas import tpu as pltpu
from jax.sharding import Mesh, PartitionSpec as P

sharpness = 1.0 / 0.07
f32 = jnp.float32
bf16 = jnp.bfloat16
NT = (((1,), (1,)), ((), ()))
PLANE, LINE = ("y", "x"), "z"
EXTRA = 16


def normalize(embed):
    flat = embed.astype(f32)
    factor = lax.rsqrt(jnp.sum(flat * flat, axis=1, keepdims=True) + 1e-06)
    return flat * factor, factor


def pack(dst, b, value):
    rows = value.shape[0]
    for k in range(value.shape[1] // 128):
        dst[b, k * rows : (k + 1) * rows, :] = value[:, k * 128 : (k + 1) * 128]


def unpack(ref, first, count, rows, width):
    return jnp.concatenate(
        [
            ref[first : first + count, k * rows : (k + 1) * rows, :].reshape(count * rows, 128)
            for k in range(width // 128)
        ],
        axis=1,
    )


def rows_tile(values):
    row = lax.broadcasted_iota(jnp.int32, (EXTRA, 128), 0)
    tile = jnp.zeros((EXTRA, 128), f32)
    for i, v in enumerate(values):
        tile = jnp.where(row == i, v, tile)
    return tile.astype(bf16)


def start_kernel(place_ref, img_hbm, txt_hbm, partner_hbm, keep_ref, send_ref, img, txt, partner, sems):
    copies = [
        pltpu.make_async_copy(src, dst, sems.at[i])
        for i, (src, dst) in enumerate(((img_hbm, img), (txt_hbm, txt), (partner_hbm, partner)))
    ]
    for c in copies:
        c.start()
    for c in copies:
        c.wait()
    image_core = place_ref[0] == 0
    half, size = img.shape
    a, b = img[...].astype(f32), txt[...].astype(f32)
    keep_ref[:half] = jnp.where(image_core, a, b).astype(bf16)
    send_ref[:half] = jnp.where(image_core, b, a).astype(bf16)
    p = jnp.concatenate([partner[...]] * (size // half), axis=1)
    hi = p // 128
    row = lax.broadcasted_iota(jnp.int32, (EXTRA, size), 0)
    tile = jnp.where(row == 0, hi, jnp.where(row == 1, p - hi * 128, 0)).astype(f32).astype(bf16)
    keep_ref[half:] = tile
    send_ref[half:] = tile


def prep_kernel(images, first, second, out):
    half = first.shape[0] - EXTRA
    unit = [normalize(src[:half, :])[0] for src in (first, second)]
    unit = jnp.concatenate(unit, axis=0).astype(bf16)
    size = unit.size // 128
    tile = jnp.zeros((EXTRA, 128), bf16)
    if images:
        lane = lax.broadcasted_iota(jnp.int32, (EXTRA, 128), 1)
        a, b = (src[half:, :128].astype(f32) for src in (first, second))
        tile = jnp.where(lane // half % 2 == 0, a, b).astype(bf16)
    for b in range(out.shape[0]):
        pack(out, b, unit)
        out[b, size:, :] = tile


def scores_kernel(images, rows, place_ref, x_ref, y_ref, e_ref, pay_ref):
    packed = x_ref.shape[1]
    width = (packed - EXTRA) // rows * 128
    per, half = 128 // rows, rows // 2
    texts = x_ref.shape[0] // 2
    nx, ny = x_ref.shape[0] // per, y_ref.shape[0] // per
    if images:
        ny = texts // per
    else:
        nx = texts // per
    lane = lax.broadcasted_iota(jnp.int32, (1, 128), 1)
    tail = (x_ref if images else y_ref)[:, packed - EXTRA :, :].astype(f32)
    partner = tail[:, 0, :] * 128.0 + tail[:, 1, :]

    def partners(t):
        p = partner[per * t : per * t + 1]
        for q in range(1, per):
            p = jnp.where(lane >= q * rows, partner[per * t + q : per * t + q + 1], p)
        return p

    def ids(t):
        i = (lane % rows) // half * (texts * half) + (per * t + lane // rows) * half
        return (place_ref[1] * (texts * rows) + i + lane % half).astype(f32)

    xs, ys = (partners, ids) if images else (ids, partners)
    y = unpack(y_ref, 0, ny * per, rows, width)
    targets = [ys(t) for t in range(ny)]
    sums = []
    positive = jnp.zeros((128, 128), f32)
    for r in range(nx):
        x = unpack(x_ref, r * per, per, rows, width)
        s = lax.dot_general(x, y, NT, preferred_element_type=f32) * f32(sharpness)
        own = jnp.broadcast_to(xs(r), (128, 128)).T
        lanes = jnp.zeros((128, 128), f32)
        for t in range(ny):
            piece = s[:, t * 128 : (t + 1) * 128]
            match = own == targets[t]
            if not images:
                positive += jnp.where(match, piece, f32(0.0))
            e = jnp.exp(piece)
            lanes += e
            e_ref[r * ny + t] = jnp.where(match, -e, e)
        sums.append(jnp.sum(lanes.T, axis=0, keepdims=True))
    if not images:
        positive = jnp.sum(jnp.sum(positive, axis=0, keepdims=True), axis=1, keepdims=True)
        sums += [jnp.broadcast_to(positive, (1, 128)), jnp.zeros((7 - nx, 128), f32)]
    pay = jnp.concatenate(sums, axis=0)
    for b in range(pay_ref.shape[0]):
        pay_ref[b] = pay


def grads_kernel(images, rows, y_ref, e_ref, mine_ref, other_ref, out_ref):
    blocks, packed, _ = out_ref.shape
    width = (packed - EXTRA) // rows * 128
    per = 128 // rows
    nx = blocks // per
    ny = e_ref.shape[0] // nx
    row_inv = f32(1.0) / mine_ref[:nx]
    col_total = other_ref[:ny]
    col_inv = f32(1.0) / col_total
    share = jnp.sum(jnp.log(col_total), axis=0, keepdims=True)
    share = jnp.broadcast_to(jnp.sum(share, axis=1, keepdims=True), (1, 128))
    if images:
        share -= 2.0 * other_ref[ny : ny + 1]
    hi = share.astype(bf16).astype(f32)
    mid = (share - hi).astype(bf16).astype(f32)
    tile = rows_tile([hi, mid, share - hi - mid])
    y = unpack(y_ref, 0, ny * per, rows, width)
    for r in range(nx):
        ri = jnp.broadcast_to(row_inv[r : r + 1], (128, 128)).T
        d = []
        for t in range(ny):
            e = e_ref[r * ny + t]
            v = jnp.abs(e) * (ri + col_inv[t : t + 1]) - jnp.where(e < 0.0, f32(2.0), f32(0.0))
            d.append(v.astype(bf16))
        g = jnp.dot(jnp.concatenate(d, axis=1), y, preferred_element_type=f32).astype(bf16)
        for q in range(per):
            pack(out_ref, r * per + q, g[q * rows : (q + 1) * rows])
            out_ref[r * per + q, packed - EXTRA :, :] = tile


def finish_kernel(scale, keep_first, first, second, parts, keep_ref, send_ref, share_ref):
    half, size = keep_ref.shape
    rows = 2 * half
    body = rows * (size // 128)
    total = parts[0, :body, :].astype(f32)
    for b in range(1, parts.shape[0]):
        total += parts[b, :body, :].astype(f32)
    total = total * f32(scale)
    total = jnp.concatenate(
        [total[k * rows : (k + 1) * rows] for k in range(size // 128)], axis=1
    )
    grads = []
    for i, src in enumerate((first, second)):
        unit, factor = normalize(src[:half, :])
        g = total[i * half : (i + 1) * half]
        grads.append(factor * (g - unit * jnp.sum(unit * g, axis=1, keepdims=True)))
    keep, send = grads if keep_first else grads[::-1]
    keep_ref[...] = keep
    send_ref[:half] = send
    share = parts[:, body:, :].astype(f32)
    share = jnp.sum(jnp.sum(share, axis=0), axis=0, keepdims=True)
    share_ref[...] = jnp.broadcast_to(share, share_ref.shape)
    send_ref[half:] = jnp.broadcast_to(share[:, :1], (send_ref.shape[0] - half, size))


def output_kernel(batch, place_ref, keep_ref, share_ref, recv_ref, img_ref, txt_ref, loss_ref):
    image_core = place_ref[0] == 0
    half = keep_ref.shape[0]
    keep, recv = keep_ref[...], recv_ref[:half]
    img_ref[...] = jnp.where(image_core, keep, recv)
    txt_ref[...] = jnp.where(image_core, recv, keep)
    loss_ref[...] = (share_ref[:1, :1] + recv_ref[half : half + 1, :1]) / (2.0 * batch)


def call(kernel, outs, scalars=False, **kw):
    if scalars:
        kw["in_specs"] = [pl.BlockSpec(memory_space=pltpu.SMEM)]
        kw["in_specs"] += [pl.BlockSpec(memory_space=pltpu.VMEM)] * (scalars - 1)
    return pl.pallas_call(
        kernel,
        out_shape=[jax.ShapeDtypeStruct(s, d) for s, d in outs],
        compiler_params=pltpu.CompilerParams(vmem_limit_bytes=48 * 1024 * 1024),
        **kw,
    )


def exchange(x, axes):
    return lax.all_to_all(x, axes, 0, 0)


def swap(x):
    return lax.ppermute(x, "c", [(0, 1), (1, 0)])


def local(image_embed, text_embed, partner):
    half, size = image_embed.shape
    rows = 2 * half
    n_plane = lax.axis_size("y") * lax.axis_size("x")
    n_line = lax.axis_size("z")
    batch = rows * n_plane * n_line
    chip = lax.axis_index("y") * lax.axis_size("x") + lax.axis_index("x")
    core = lax.axis_index("c")
    image_core = core == 0
    place = jnp.stack([core, chip]).astype(jnp.int32)
    packed = rows * (size // 128) + EXTRA
    tiles = n_plane * n_line * rows * rows // (128 * 128)

    own, send = call(
        start_kernel,
        [((half + EXTRA, size), bf16)] * 2,
        in_specs=[pl.BlockSpec(memory_space=pltpu.SMEM)] + [pl.BlockSpec(memory_space=pl.ANY)] * 3,
        scratch_shapes=[
            pltpu.VMEM((half, size), bf16),
            pltpu.VMEM((half, size), bf16),
            pltpu.VMEM((1, half), jnp.int32),
            pltpu.SemaphoreType.DMA((3,)),
        ],
    )(place, image_embed, text_embed, partner.reshape(1, half))
    off = swap(send)

    def gather_images():
        kernel = functools.partial(prep_kernel, True)
        return exchange(call(kernel, [((n_plane, packed, 128), bf16)])(own, off)[0], PLANE)

    def gather_texts():
        kernel = functools.partial(prep_kernel, False)
        every = exchange(call(kernel, [((n_line, packed, 128), bf16)])(off, own)[0], LINE)
        return jnp.pad(every, ((0, n_plane - n_line), (0, 0), (0, 0)))

    x = lax.cond(image_core, gather_images, gather_texts)
    y = swap(x)

    def sums(images, count, axes):
        e, pay = call(
            functools.partial(scores_kernel, images, rows),
            [((tiles, 128, 128), f32), ((count, 8, 128), f32)],
            scalars=3,
        )(place, x, y)
        return e, jnp.sum(exchange(pay, axes), axis=0)

    e, mine = lax.cond(
        image_core,
        functools.partial(sums, True, n_plane, PLANE),
        functools.partial(sums, False, n_line, LINE),
    )
    other = swap(mine)

    def grads(images, count, axes):
        pay = call(
            functools.partial(grads_kernel, images, rows), [((count, packed, 128), bf16)]
        )(y, e, mine, other)[0]
        return call(
            functools.partial(finish_kernel, sharpness / (2.0 * batch), images),
            [((half, size), f32), ((half + 8, size), f32), ((8, 128), f32)],
        )(*((own, off) if images else (off, own)), exchange(pay, axes))

    keep, send, share = lax.cond(
        image_core,
        functools.partial(grads, True, n_plane, PLANE),
        functools.partial(grads, False, n_line, LINE),
    )
    image_grad, text_grad, loss = call(
        functools.partial(output_kernel, batch),
        [((half, size), f32), ((half, size), f32), ((1, 1), f32)],
        scalars=4,
    )(place, keep, share, swap(send))
    return loss.reshape(()), image_grad, text_grad


def solution(mesh):
    shape = (mesh.shape["row"], 4, mesh.shape["col"] // 8, 2)
    fine = Mesh(mesh.devices.reshape(shape), ("z", "y", "x", "c"))
    by_image, by_text = P(("z", "y", "x", "c")), P(("y", "x", "c", "z"))
    return jax.shard_map(
        local,
        mesh=fine,
        in_specs=(by_image, by_text, by_image),
        out_specs=(P(), by_image, by_text),
        check_vma=False,
    )
```

profile of v0, /device:TPU:1, one launch (start us, length us, event | category | flops | bytes accessed | tf_op | source)
XLA Modules:
  0.0 78.1 jit_solution(17400676829067454218)
XLA Ops:
  0.6 0.1 pad_add_fusion.place_ref
  0.7 0.0 copy-start
  0.7 0.8 %copy-done = bf16[32,768]{1,0:T(8,128)(2,1)S(1)} copy-done((bf16[32,768]{1,0:T(8,128)(2,1)S(1)}, bf16[32,768]{1,0:T(8,128)(2,1)}, u32[]{:S(2)}) %copy-start) | copy-done | bytes 49176
  1.5 0.0 copy-start.1
  1.5 0.8 %copy-done.1 = bf16[32,768]{1,0:T(8,128)(2,1)S(1)} copy-done((bf16[32,768]{1,0:T(8,128)(2,1)S(1)}, bf16[32,768]{1,0:T(8,128)(2,1)}, u32[]{:S(2)}) %copy-start.1) | copy-done | bytes 49176
  2.3 0.0 copy-start.2
  2.3 0.7 copy-done.2
  3.0 0.8 %shard_map.58 = (bf16[48,768]{1,0:T(8,128)(2,1)S(1)}, bf16[48,768]{1,0:T(8,128)(2,1)S(1)}) custom-call(s32[2]{0:T(128)S(1)} %pad_add_fusion.place_ref, bf16[32,768]{1,0:T(8,128)(2,1)S(1)} %copy-done, bf16[32,768]{1,0:T(8,128)(2,1)S(1)} %copy-done.1, s32[1,32]{1,0:T(1,128)S(1)} %bitcast.4), custom_call_target="tpu_custom_call" | custom-call | tf_op jit(solution)/shard_map/pallas_call | solution.py:233
  3.8 3.3 %collective-permute-start = (bf16[48,768]{1,0:T(8,128)(2,1)S(1)}, bf16[48,768]{1,0:T(8,128)(2,1)S(1)}, u32[]{:S(2)}, u32[]{:S(2)}) collective-permute-start(bf16[48,768]{1,0:T(8,128)(2,1)S(1)} %get-tuple-element.86), channel_id=1, source_target_pairs={{0,1},{1,0},{2,3},{3,2},{4,5},{5,4},{6,7},{7,6},{8,9},{9,8},{10,11... | collective-permute-start | bytes 221192 | tf_op jit(solution)/shard_map/ppermute | solution.py:217
  7.1 0.9 %collective-permute-done = bf16[48,768]{1,0:T(8,128)(2,1)S(1)} collective-permute-done((bf16[48,768]{1,0:T(8,128)(2,1)S(1)}, bf16[48,768]{1,0:T(8,128)(2,1)S(1)}, u32[]{:S(2)}, u32[]{:S(2)}) %collective-permute-start) | collective-permute-done | bytes 73760 | tf_op jit(solution)/shard_map/ppermute | solution.py:217
  8.0 21.9 %conditional.3 = (bf16[16,400,128]{2,1,0:T(8,128)(2,1)S(1)}) conditional(s32[]{:T(128)} %convert_element_type.4, (bf16[48,768]{1,0:T(8,128)(2,1)S(1)}, bf16[48,768]{1,0:T(8,128)(2,1)S(1)}) %tuple.28, (bf16[48,768]{1,0:T(8,128)(2,1)S(1)}, bf16[48,768]{1,0:T(8,128)(2,1)S(1)}) %tuple.29), branch_computations={%region_0.1_spmd, %region_1.2_spmd} | conditional | bytes 4096010 | solution.py:255
  8.0 0.1 branch_0_fun.4
  8.2 21.6 %all_to_all.24 = bf16[8,400,128]{2,1,0:T(8,128)(2,1)S(1)} all-to-all(bf16[8,400,128]{2,1,0:T(8,128)(2,1)S(1)} %branch_0_fun.4), channel_id=1, replica_groups=mesh['z'=8,'y'=4,'x'=4,'c'=2] {'z'}, dimensions={0} | all-to-all | bytes 1638400 | tf_op jit(solution)/shard_map/cond/branch_0_fun/all_to_all | solution.py:213
  29.7 0.2 pad.3
  29.9 0.1 collective-permute-start.1
  30.0 3.5 %collective-permute-done.1 = bf16[16,400,128]{2,1,0:T(8,128)(2,1)S(1)} collective-permute-done((bf16[16,400,128]{2,1,0:T(8,128)(2,1)S(1)}, bf16[16,400,128]{2,1,0:T(8,128)(2,1)S(1)}, u32[]{:S(2)}, u32[]{:S(2)}) %collective-permute-start.1) | collective-permute-done | bytes 1638432 | tf_op jit(solution)/shard_map/ppermute | solution.py:217
  33.5 18.6 %conditional.4 = (f32[32,128,128]{2,1,0:T(8,128)}, f32[8,128]{1,0:T(8,128)S(1)}) conditional(s32[]{:T(128)} %convert_element_type.4, (s32[2]{0:T(128)S(1)}, bf16[16,400,128]{2,1,0:T(8,128)(2,1)S(1)}, bf16[16,400,128]{2,1,0:T(8,128)(2,1)S(1)}) %tuple.30, (s32[2]{0:T(128)S(1)}, bf16[16,400,128]{2,1,0:T(8,128)(2,1)S(1)}, ...), branch_computations={%region_2.4_spmd, %region_4.6_spmd} | conditional | flops 15360 | bytes 200724 | solution.py:266
  33.5 4.2 %branch_0_fun.5 = (f32[32,128,128]{2,1,0:T(8,128)}, f32[8,8,128]{2,1,0:T(8,128)S(1)}) custom-call(s32[2]{0:T(128)S(1)} %get-tuple-element.51.place_ref, bf16[16,400,128]{2,1,0:T(8,128)(2,1)S(1)} %get-tuple-element.52.x_ref, bf16[16,400,128]{2,1,0:T(8,128)(2,1)S(1)} %get-tuple-element.53.y_ref), custom_call_target="tpu_custom_call" | custom-call | tf_op jit(solution)/shard_map/cond/branch_0_fun/pallas_call | solution.py:259
  37.6 14.4 %all_to_all.26 = f32[8,8,128]{2,1,0:T(8,128)S(1)} all-to-all(f32[8,8,128]{2,1,0:T(8,128)S(1)} %get-tuple-element.55), channel_id=1, replica_groups=mesh['z'=8,'y'=4,'x'=4,'c'=2] {'z'}, dimensions={0} | all-to-all | bytes 65536 | tf_op jit(solution)/shard_map/cond/branch_0_fun/all_to_all | solution.py:213
  52.0 0.3 collective-permute-start.2
  52.3 1.0 %collective-permute-done.2 = f32[8,128]{1,0:T(8,128)S(1)} collective-permute-done((f32[8,128]{1,0:T(8,128)S(1)}, f32[8,128]{1,0:T(8,128)S(1)}, u32[]{:S(2)}, u32[]{:S(2)}) %collective-permute-start.2) | collective-permute-done | bytes 4128 | tf_op jit(solution)/shard_map/ppermute | solution.py:217
  53.3 22.1 %conditional.5 = ((f32[32,768]{1,0:T(8,128)S(1)}, f32[40,768]{1,0:T(8,128)S(1)}, f32[8,128]{1,0:T(8,128)S(1)})) conditional(s32[]{:T(128)} %convert_element_type.4, (bf16[16,400,128]{2,1,0:T(8,128)(2,1)S(1)}, f32[32,128,128]{2,1,0:T(8,128)}, f32[8,128]{1,0:T(8,128)S(1)}, f32[8,128]{1,0:T(8,128)S(1)}, bf16[48,768]{1,0:T(8,128)(2,1)S(1)}, ...), branch_computations={%region_6.7_spmd, %region_7.8_spmd} | conditional | bytes 3276808 | solution.py:282
  53.3 2.6 %branch_0_fun.6 = bf16[8,400,128]{2,1,0:T(8,128)(2,1)S(1)} custom-call(bf16[16,400,128]{2,1,0:T(8,128)(2,1)S(1)} %get-tuple-element.63.y_ref, f32[32,128,128]{2,1,0:T(8,128)} %get-tuple-element.64.e_ref, f32[8,128]{1,0:T(8,128)S(1)} %get-tuple-element.65.mine_ref, f32[8,128]{1,0:T(8,128)S(1)} %get-tuple-element.66.other_ref), custom_call_target="tpu_custom_call" | custom-call | tf_op jit(solution)/shard_map/cond/branch_0_fun/pallas_call | solution.py:274
  55.9 19.2 %all_to_all.28.parts = bf16[8,400,128]{2,1,0:T(8,128)(2,1)S(1)} all-to-all(bf16[8,400,128]{2,1,0:T(8,128)(2,1)S(1)} %branch_0_fun.6), channel_id=1, replica_groups=mesh['z'=8,'y'=4,'x'=4,'c'=2] {'z'}, dimensions={0} | all-to-all | bytes 1638400 | tf_op jit(solution)/shard_map/cond/branch_0_fun/all_to_all | solution.py:213
  75.1 0.2 branch_0_fun.7
  75.4 0.5 collective-permute-start.3
  75.9 1.0 %collective-permute-done.3.recv_ref = f32[40,768]{1,0:T(8,128)S(1)} collective-permute-done((f32[40,768]{1,0:T(8,128)S(1)}, f32[40,768]{1,0:T(8,128)S(1)}, u32[]{:S(2)}, u32[]{:S(2)}) %collective-permute-start.3) | collective-permute-done | bytes 122912 | tf_op jit(solution)/shard_map/ppermute | solution.py:217
  76.9 1.2 %shard_map.59 = (f32[32,768]{1,0:T(8,128)}, f32[32,768]{1,0:T(8,128)}, f32[1,1]{1,0:T(1,128)}) custom-call(s32[2]{0:T(128)S(1)} %pad_add_fusion.place_ref, f32[32,768]{1,0:T(8,128)S(1)} %get-tuple-element.90.keep_ref, f32[8,128]{1,0:T(8,128)S(1)} %get-tuple-element.91.share_ref, f32[40,768]{1,0:T(8,128)S(1)} %collective-permute-done.3.recv_ref), custom_call_target="tpu_custom_call" | custom-call | tf_op jit(solution)/shard_map/pallas_call | solution.py:287
  (1 shorter events, 0.0 us)
Async XLA Ops:
  0.7 0.8 %copy-start = (bf16[32,768]{1,0:T(8,128)(2,1)S(1)}, bf16[32,768]{1,0:T(8,128)(2,1)}, u32[]{:S(2)}) copy-start(bf16[32,768]{1,0:T(8,128)(2,1)} %img_hbm.1) | copy-start | bytes 147460
  1.5 0.8 %copy-start.1 = (bf16[32,768]{1,0:T(8,128)(2,1)S(1)}, bf16[32,768]{1,0:T(8,128)(2,1)}, u32[]{:S(2)}) copy-start(bf16[32,768]{1,0:T(8,128)(2,1)} %txt_hbm.1) | copy-start | bytes 147460
  2.3 0.7 copy-start.2
  3.8 4.2 %collective-permute-start = (bf16[48,768]{1,0:T(8,128)(2,1)S(1)}, bf16[48,768]{1,0:T(8,128)(2,1)S(1)}, u32[]{:S(2)}, u32[]{:S(2)}) collective-permute-start(bf16[48,768]{1,0:T(8,128)(2,1)S(1)} %get-tuple-element.86), channel_id=1, source_target_pairs={{0,1},{1,0},{2,3},{3,2},{4,5},{5,4},{6,7},{7,6},{8,9},{9,8},{10,11... | collective-permute-start | bytes 221192 | tf_op jit(solution)/shard_map/ppermute | solution.py:217
  29.9 3.6 %collective-permute-start.1 = (bf16[16,400,128]{2,1,0:T(8,128)(2,1)S(1)}, bf16[16,400,128]{2,1,0:T(8,128)(2,1)S(1)}, u32[]{:S(2)}, u32[]{:S(2)}) collective-permute-start(bf16[16,400,128]{2,1,0:T(8,128)(2,1)S(1)} %get-tuple-element.106), channel_id=1, source_target_pairs={{0,1},{1,0},{2,3},{3,2},{4,5},{5,4},{6,7},{7,6},{8,9},{9,8},{10,11... | collective-permute-start | bytes 4915208 | tf_op jit(solution)/shard_map/ppermute | solution.py:217
  52.0 1.2 %collective-permute-start.2 = (f32[8,128]{1,0:T(8,128)S(1)}, f32[8,128]{1,0:T(8,128)S(1)}, u32[]{:S(2)}, u32[]{:S(2)}) collective-permute-start(f32[8,128]{1,0:T(8,128)S(1)} %get-tuple-element.89), channel_id=1, source_target_pairs={{0,1},{1,0},{2,3},{3,2},{4,5},{5,4},{6,7},{7,6},{8,9},{9,8},{10,11... | collective-permute-start | bytes 12296 | tf_op jit(solution)/shard_map/ppermute | solution.py:217
  75.4 1.5 %collective-permute-start.3 = (f32[40,768]{1,0:T(8,128)S(1)}, f32[40,768]{1,0:T(8,128)S(1)}, u32[]{:S(2)}, u32[]{:S(2)}) collective-permute-start(f32[40,768]{1,0:T(8,128)S(1)} %get-tuple-element.92), channel_id=1, source_target_pairs={{0,1},{1,0},{2,3},{3,2},{4,5},{5,4},{6,7},{7,6},{8,9},{9,8},{10,11... | collective-permute-start | bytes 368648 | tf_op jit(solution)/shard_map/ppermute | solution.py:217
where the time goes:
time: 78.4 us; the launch traced here: 78.1 us
  blocking collectives  55.2 us (70%)
  Pallas kernels  9.19 us (12%)
  waiting for transfers between devices  6.36 us (8%)
  starting transfers between devices  4.19 us (5%)
  local copies, waits for them, and re-layouts  2.41 us (3%)
    all_to_all x3, blocking collectives, exchange(): return lax.all_to_all(x, axes, 0, 0)  55.2 us
    ppermute x4, waiting for transfers between devices, swap(): return lax.ppermute(x, 'c', [(0, 1), (1, 0)])  6.36 us
    ppermute x4, starting transfers between devices, swap(): return lax.ppermute(x, 'c', [(0, 1), (1, 0)])  4.19 us
    pallas_call x1, Pallas kernels, sums(): call(functools.partial(scores_kernel, images, rows), [((tiles, 128, 128),...  4.16 us
    pallas_call x1, Pallas kernels, grads(): call(functools.partial(grads_kernel, images, rows), [((count, packed, 128...  2.64 us
    unnamed x6, local copies, waits for them, and re-layouts  2.25 us
  transfers between devices with their start and end apart: 4, of which 4 were waited for; matrix products, arithmetic and copies ran while one was open for 0% of the time, Pallas kernels for 0%

commit v1 on v0

--- a/solution.py
+++ b/solution.py
@@ -1,4 +1,5 @@
 import functools
+import math
 
 import jax
 import jax.numpy as jnp
@@ -45,7 +46,7 @@
     return tile.astype(bf16)
 
 
-def start_kernel(place_ref, img_hbm, txt_hbm, partner_hbm, keep_ref, send_ref, img, txt, partner, sems):
+def start_kernel(img_hbm, txt_hbm, partner_hbm, keep_ref, send_ref, img, txt, partner, sems):
     copies = [
         pltpu.make_async_copy(src, dst, sems.at[i])
         for i, (src, dst) in enumerate(((img_hbm, img), (txt_hbm, txt), (partner_hbm, partner)))
@@ -54,17 +55,17 @@
         c.start()
     for c in copies:
         c.wait()
-    image_core = place_ref[0] == 0
+    image_core = lax.axis_index("c") == 0
     half, size = img.shape
     a, b = img[...].astype(f32), txt[...].astype(f32)
     keep_ref[:half] = jnp.where(image_core, a, b).astype(bf16)
     send_ref[:half] = jnp.where(image_core, b, a).astype(bf16)
-    p = jnp.concatenate([partner[...]] * (size // half), axis=1)
+    p = jnp.concatenate([partner[...]] * (128 // half), axis=1)
     hi = p // 128
-    row = lax.broadcasted_iota(jnp.int32, (EXTRA, size), 0)
-    tile = jnp.where(row == 0, hi, jnp.where(row == 1, p - hi * 128, 0)).astype(f32).astype(bf16)
-    keep_ref[half:] = tile
-    send_ref[half:] = tile
+    tile = rows_tile([hi.astype(f32), (p - hi * 128).astype(f32)])
+    for dst in (keep_ref, send_ref):
+        dst[half:] = jnp.zeros((EXTRA, size), bf16)
+        dst[half:, :128] = tile
 
 
 def prep_kernel(images, first, second, out):
@@ -82,7 +83,7 @@
         out[b, size:, :] = tile
 
 
-def scores_kernel(images, rows, place_ref, x_ref, y_ref, e_ref, pay_ref):
+def scores_kernel(images, rows, x_ref, y_ref, e_ref, pay_ref, s_ref, xs_ref, ys_ref):
     packed = x_ref.shape[1]
     width = (packed - EXTRA) // rows * 128
     per, half = 128 // rows, rows // 2
@@ -93,6 +94,7 @@
     else:
         nx = texts // per
     lane = lax.broadcasted_iota(jnp.int32, (1, 128), 1)
+    chip = lax.axis_index("y") * lax.axis_size("x") + lax.axis_index("x")
     tail = (x_ref if images else y_ref)[:, packed - EXTRA :, :].astype(f32)
     partner = tail[:, 0, :] * 128.0 + tail[:, 1, :]
 
@@ -104,33 +106,45 @@
 
     def ids(t):
         i = (lane % rows) // half * (texts * half) + (per * t + lane // rows) * half
-        return (place_ref[1] * (texts * rows) + i + lane % half).astype(f32)
+        return (chip * (texts * rows) + i + lane % half).astype(f32)
 
     xs, ys = (partners, ids) if images else (ids, partners)
+    for r in range(nx):
+        xs_ref[r : r + 1] = xs(r)
+    for t in range(ny):
+        ys_ref[t : t + 1] = ys(t)
+    x = unpack(x_ref, 0, nx * per, rows, width)
     y = unpack(y_ref, 0, ny * per, rows, width)
-    targets = [ys(t) for t in range(ny)]
-    sums = []
-    positive = jnp.zeros((128, 128), f32)
+    scores = lax.dot_general(x, y, NT, preferred_element_type=f32)
     for r in range(nx):
-        x = unpack(x_ref, r * per, per, rows, width)
-        s = lax.dot_general(x, y, NT, preferred_element_type=f32) * f32(sharpness)
-        own = jnp.broadcast_to(xs(r), (128, 128)).T
-        lanes = jnp.zeros((128, 128), f32)
         for t in range(ny):
-            piece = s[:, t * 128 : (t + 1) * 128]
-            match = own == targets[t]
-            if not images:
-                positive += jnp.where(match, piece, f32(0.0))
-            e = jnp.exp(piece)
-            lanes += e
-            e_ref[r * ny + t] = jnp.where(match, -e, e)
-        sums.append(jnp.sum(lanes.T, axis=0, keepdims=True))
+            s_ref[r * ny + t] = scores[r * 128 : (r + 1) * 128, t * 128 : (t + 1) * 128]
+    group = nx // 2
+
+    def part(i, positive):
+        for q in range(group):
+            r = i * group + q
+            own = jnp.broadcast_to(xs_ref[pl.ds(r, 1)], (128, 128)).T
+            lanes = jnp.zeros((128, 128), f32)
+            for t in range(ny):
+                piece = s_ref[r * ny + t]
+                match = own == ys_ref[t : t + 1]
+                if not images:
+                    positive += jnp.where(match, piece, f32(0.0))
+                e = jnp.exp2(piece * f32(sharpness * math.log2(math.e)))
+                lanes += e
+                tile = q * ny + t
+                at = pl.ds(tile % 2 * 128, 128)
+                e_ref[i * (group * ny // 2) + tile // 2, at] = jnp.where(match, -e, e).astype(bf16)
+            pay_ref[0, pl.ds(r, 1)] = jnp.sum(lanes.T, axis=0, keepdims=True)
+        return positive
+
+    positive = lax.fori_loop(0, 2, part, jnp.zeros((128, 128), f32)) * f32(sharpness)
     if not images:
         positive = jnp.sum(jnp.sum(positive, axis=0, keepdims=True), axis=1, keepdims=True)
-        sums += [jnp.broadcast_to(positive, (1, 128)), jnp.zeros((7 - nx, 128), f32)]
-    pay = jnp.concatenate(sums, axis=0)
-    for b in range(pay_ref.shape[0]):
-        pay_ref[b] = pay
+        pay_ref[0, nx:] = jnp.broadcast_to(positive, (8 - nx, 128))
+    for b in range(1, pay_ref.shape[0]):
+        pay_ref[b] = pay_ref[0]
 
 
 def grads_kernel(images, rows, y_ref, e_ref, mine_ref, other_ref, out_ref):
@@ -138,8 +152,7 @@
     width = (packed - EXTRA) // rows * 128
     per = 128 // rows
     nx = blocks // per
-    ny = e_ref.shape[0] // nx
-    row_inv = f32(1.0) / mine_ref[:nx]
+    ny = e_ref.shape[0] * 2 // nx
     col_total = other_ref[:ny]
     col_inv = f32(1.0) / col_total
     share = jnp.sum(jnp.log(col_total), axis=0, keepdims=True)
@@ -148,19 +161,23 @@
         share -= 2.0 * other_ref[ny : ny + 1]
     hi = share.astype(bf16).astype(f32)
     mid = (share - hi).astype(bf16).astype(f32)
-    tile = rows_tile([hi, mid, share - hi - mid])
+    share = rows_tile([hi, mid, share - hi - mid])
+    row_inv = f32(1.0) / mine_ref[:nx]
     y = unpack(y_ref, 0, ny * per, rows, width)
+    ds = []
     for r in range(nx):
         ri = jnp.broadcast_to(row_inv[r : r + 1], (128, 128)).T
         d = []
         for t in range(ny):
-            e = e_ref[r * ny + t]
+            tile = r * ny + t
+            e = e_ref[tile // 2, tile % 2 * 128 : tile % 2 * 128 + 128].astype(f32)
             v = jnp.abs(e) * (ri + col_inv[t : t + 1]) - jnp.where(e < 0.0, f32(2.0), f32(0.0))
             d.append(v.astype(bf16))
-        g = jnp.dot(jnp.concatenate(d, axis=1), y, preferred_element_type=f32).astype(bf16)
-        for q in range(per):
-            pack(out_ref, r * per + q, g[q * rows : (q + 1) * rows])
-            out_ref[r * per + q, packed - EXTRA :, :] = tile
+        ds.append(jnp.concatenate(d, axis=1))
+    g = jnp.dot(jnp.concatenate(ds, axis=0), y, preferred_element_type=f32).astype(bf16)
+    for b in range(blocks):
+        pack(out_ref, b, g[b * rows : (b + 1) * rows])
+        out_ref[b, packed - EXTRA :, :] = share
 
 
 def finish_kernel(scale, keep_first, first, second, parts, keep_ref, send_ref, share_ref):
@@ -188,8 +205,8 @@
     send_ref[half:] = jnp.broadcast_to(share[:, :1], (send_ref.shape[0] - half, size))
 
 
-def output_kernel(batch, place_ref, keep_ref, share_ref, recv_ref, img_ref, txt_ref, loss_ref):
-    image_core = place_ref[0] == 0
+def output_kernel(batch, keep_ref, share_ref, recv_ref, img_ref, txt_ref, loss_ref):
+    image_core = lax.axis_index("c") == 0
     half = keep_ref.shape[0]
     keep, recv = keep_ref[...], recv_ref[:half]
     img_ref[...] = jnp.where(image_core, keep, recv)
@@ -197,13 +214,10 @@
     loss_ref[...] = (share_ref[:1, :1] + recv_ref[half : half + 1, :1]) / (2.0 * batch)
 
 
-def call(kernel, outs, scalars=False, **kw):
-    if scalars:
-        kw["in_specs"] = [pl.BlockSpec(memory_space=pltpu.SMEM)]
-        kw["in_specs"] += [pl.BlockSpec(memory_space=pltpu.VMEM)] * (scalars - 1)
+def call(kernel, outs, **kw):
     return pl.pallas_call(
         kernel,
-        out_shape=[jax.ShapeDtypeStruct(s, d) for s, d in outs],
+        out_shape=[jax.ShapeDtypeStruct(*o) for o in outs],
         compiler_params=pltpu.CompilerParams(vmem_limit_bytes=48 * 1024 * 1024),
         **kw,
     )
@@ -223,24 +237,25 @@
     n_plane = lax.axis_size("y") * lax.axis_size("x")
     n_line = lax.axis_size("z")
     batch = rows * n_plane * n_line
-    chip = lax.axis_index("y") * lax.axis_size("x") + lax.axis_index("x")
-    core = lax.axis_index("c")
-    image_core = core == 0
-    place = jnp.stack([core, chip]).astype(jnp.int32)
+    image_core = lax.axis_index("c") == 0
     packed = rows * (size // 128) + EXTRA
     tiles = n_plane * n_line * rows * rows // (128 * 128)
 
+    args = [
+        pltpu.with_memory_space_constraint(a, pltpu.HBM)
+        for a in (image_embed, text_embed, partner.reshape(1, half))
+    ]
     own, send = call(
         start_kernel,
         [((half + EXTRA, size), bf16)] * 2,
-        in_specs=[pl.BlockSpec(memory_space=pltpu.SMEM)] + [pl.BlockSpec(memory_space=pl.ANY)] * 3,
+        in_specs=[pl.BlockSpec(memory_space=pl.ANY)] * 3,
         scratch_shapes=[
             pltpu.VMEM((half, size), bf16),
             pltpu.VMEM((half, size), bf16),
             pltpu.VMEM((1, half), jnp.int32),
             pltpu.SemaphoreType.DMA((3,)),
         ],
-    )(place, image_embed, text_embed, partner.reshape(1, half))
+    )(*args)
     off = swap(send)
 
     def gather_images():
@@ -258,9 +273,10 @@
     def sums(images, count, axes):
         e, pay = call(
             functools.partial(scores_kernel, images, rows),
-            [((tiles, 128, 128), f32), ((count, 8, 128), f32)],
-            scalars=3,
-        )(place, x, y)
+            [((n_plane, packed, 128), bf16), ((count, 8, 128), f32)],
+            input_output_aliases={0: 0},
+            scratch_shapes=[pltpu.VMEM((tiles, 128, 128), f32)] + [pltpu.VMEM((8, 128), f32)] * 2,
+        )(x, y)
         return e, jnp.sum(exchange(pay, axes), axis=0)
 
     e, mine = lax.cond(
@@ -272,7 +288,8 @@
 
     def grads(images, count, axes):
         pay = call(
-            functools.partial(grads_kernel, images, rows), [((count, packed, 128), bf16)]
+            functools.partial(grads_kernel, images, rows),
+            [((count, packed, 128), bf16)],
         )(y, e, mine, other)[0]
         return call(
             functools.partial(finish_kernel, sharpness / (2.0 * batch), images),
@@ -287,8 +304,7 @@
     image_grad, text_grad, loss = call(
         functools.partial(output_kernel, batch),
         [((half, size), f32), ((half, size), f32), ((1, 1), f32)],
-        scalars=4,
-    )(place, keep, share, swap(send))
+    )(keep, share, swap(send))
     return loss.reshape(()), image_grad, text_grad
 
 

time: 78.4 us -> 71.9 us (0.917)
  Pallas kernels: 9.19 us -> 5.01 us
  local copies, waits for them, and re-layouts: 2.41 us -> 0.16 us
    pallas_call x1, Pallas kernels: 4.16 us -> 1.76 us  [sums(): call(functools.partial(scores_kernel, images, rows), [((n_plane, packed,...]
    unnamed x6 -> x0, local copies, waits for them, and re-layouts: 2.25 us -> none
    pallas_call x1, Pallas kernels: 2.64 us -> 1.23 us  [grads(): call(functools.partial(grads_kernel, images, rows), [((count, packed, 128...]
where the time goes in v1:
time: 71.9 us; the launch traced here: 71.6 us
  blocking collectives  55.1 us (77%)
  waiting for transfers between devices  6.51 us (9%)
  Pallas kernels  5.01 us (7%)
  starting transfers between devices  4.12 us (6%)
    all_to_all x3, blocking collectives, exchange(): return lax.all_to_all(x, axes, 0, 0)  55.1 us
    ppermute x4, waiting for transfers between devices, swap(): return lax.ppermute(x, 'c', [(0, 1), (1, 0)])  6.51 us
    ppermute x4, starting transfers between devices, swap(): return lax.ppermute(x, 'c', [(0, 1), (1, 0)])  4.12 us
    pallas_call x1, Pallas kernels, sums(): call(functools.partial(scores_kernel, images, rows), [((n_plane, packed,...  1.76 us
  transfers between devices with their start and end apart: 4, of which 4 were waited for; matrix products, arithmetic and copies ran while one was open for 0% of the time, Pallas kernels for 0%

profile of v1, /device:TPU:1, one launch (start us, length us, event | category | flops | bytes accessed | tf_op | source)
XLA Modules:
  0.0 71.6 jit_solution(6045794382978411102)
XLA Ops:
  0.6 0.9 %shard_map.58 = (bf16[48,768]{1,0:T(8,128)(2,1)S(1)}, bf16[48,768]{1,0:T(8,128)(2,1)S(1)}) custom-call(bf16[32,768]{1,0:T(8,128)(2,1)} %img_hbm.1, bf16[32,768]{1,0:T(8,128)(2,1)} %txt_hbm.1, s32[1,32]{1,0:T(1,128)} %bitcast.2), custom_call_target="tpu_custom_call" | custom-call | tf_op jit(solution)/shard_map/pallas_call | solution.py:248
  1.6 3.3 %collective-permute-start = (bf16[48,768]{1,0:T(8,128)(2,1)S(1)}, bf16[48,768]{1,0:T(8,128)(2,1)S(1)}, u32[]{:S(2)}, u32[]{:S(2)}) collective-permute-start(bf16[48,768]{1,0:T(8,128)(2,1)S(1)} %get-tuple-element.80), channel_id=1, source_target_pairs={{0,1},{1,0},{2,3},{3,2},{4,5},{5,4},{6,7},{7,6},{8,9},{9,8},{10,11... | collective-permute-start | bytes 221192 | tf_op jit(solution)/shard_map/ppermute | solution.py:231
  4.9 0.9 %collective-permute-done = bf16[48,768]{1,0:T(8,128)(2,1)S(1)} collective-permute-done((bf16[48,768]{1,0:T(8,128)(2,1)S(1)}, bf16[48,768]{1,0:T(8,128)(2,1)S(1)}, u32[]{:S(2)}, u32[]{:S(2)}) %collective-permute-start) | collective-permute-done | bytes 73760 | tf_op jit(solution)/shard_map/ppermute | solution.py:231
  5.8 21.9 %conditional.3 = (bf16[16,400,128]{2,1,0:T(8,128)(2,1)S(1)}) conditional(s32[]{:T(128)} %convert_element_type.4, (bf16[48,768]{1,0:T(8,128)(2,1)S(1)}, bf16[48,768]{1,0:T(8,128)(2,1)S(1)}) %tuple.28, (bf16[48,768]{1,0:T(8,128)(2,1)S(1)}, bf16[48,768]{1,0:T(8,128)(2,1)S(1)}) %tuple.29), branch_computations={%region_0.1_spmd, %region_1.2_spmd} | conditional | bytes 4096010 | solution.py:270
  5.8 0.1 branch_0_fun.4
  6.0 21.6 %all_to_all.24 = bf16[8,400,128]{2,1,0:T(8,128)(2,1)S(1)} all-to-all(bf16[8,400,128]{2,1,0:T(8,128)(2,1)S(1)} %branch_0_fun.4), channel_id=1, replica_groups=mesh['z'=8,'y'=4,'x'=4,'c'=2] {'z'}, dimensions={0} | all-to-all | bytes 1638400 | tf_op jit(solution)/shard_map/cond/branch_0_fun/all_to_all | solution.py:227
  27.5 0.2 pad.3
  27.7 0.1 collective-permute-start.1
  27.8 3.5 %collective-permute-done.1 = bf16[16,400,128]{2,1,0:T(8,128)(2,1)S(1)} collective-permute-done((bf16[16,400,128]{2,1,0:T(8,128)(2,1)S(1)}, bf16[16,400,128]{2,1,0:T(8,128)(2,1)S(1)}, u32[]{:S(2)}, u32[]{:S(2)}) %collective-permute-start.1) | collective-permute-done | bytes 1638432 | tf_op jit(solution)/shard_map/ppermute | solution.py:231
  31.3 16.2 %conditional.4 = (bf16[16,400,128]{2,1,0:T(8,128)(2,1)S(1)}, f32[8,128]{1,0:T(8,128)S(1)}) conditional(s32[]{:T(128)} %convert_element_type.4, (bf16[16,400,128]{2,1,0:T(8,128)(2,1)S(1)}, bf16[16,400,128]{2,1,0:T(8,128)(2,1)S(1)}) %tuple.30, (bf16[16,400,128]{2,1,0:T(8,128)(2,1)S(1)}, bf16[16,400,128]{2,1,0:T(8,128)(2,1)S(1)}) %tuple.30), branch_computations={%region_2.4_spmd, %region_4.6_spmd} | conditional | flops 15360 | bytes 200724 | solution.py:282
  31.3 1.8 %branch_0_fun.5 = (bf16[16,400,128]{2,1,0:T(8,128)(2,1)S(1)}, f32[8,8,128]{2,1,0:T(8,128)S(1)}) custom-call(bf16[16,400,128]{2,1,0:T(8,128)(2,1)S(1)} %get-tuple-element.47.x_ref, bf16[16,400,128]{2,1,0:T(8,128)(2,1)S(1)} %get-tuple-element.48.y_ref), custom_call_target="tpu_custom_call", output_to_operand_aliasing={{0}: (0, {})} | custom-call | tf_op jit(solution)/shard_map/cond/branch_0_fun/pallas_call | solution.py:274
  33.0 14.4 %all_to_all.26 = f32[8,8,128]{2,1,0:T(8,128)S(1)} all-to-all(f32[8,8,128]{2,1,0:T(8,128)S(1)} %get-tuple-element.50), channel_id=1, replica_groups=mesh['z'=8,'y'=4,'x'=4,'c'=2] {'z'}, dimensions={0} | all-to-all | bytes 65536 | tf_op jit(solution)/shard_map/cond/branch_0_fun/all_to_all | solution.py:227
  47.5 0.1 collective-permute-start.2
  47.6 1.1 %collective-permute-done.2 = f32[8,128]{1,0:T(8,128)S(1)} collective-permute-done((f32[8,128]{1,0:T(8,128)S(1)}, f32[8,128]{1,0:T(8,128)S(1)}, u32[]{:S(2)}, u32[]{:S(2)}) %collective-permute-start.2) | collective-permute-done | bytes 4128 | tf_op jit(solution)/shard_map/ppermute | solution.py:231
  48.7 20.7 %conditional.5 = ((f32[32,768]{1,0:T(8,128)S(1)}, f32[40,768]{1,0:T(8,128)S(1)}, f32[8,128]{1,0:T(8,128)S(1)})) conditional(s32[]{:T(128)} %convert_element_type.4, (bf16[16,400,128]{2,1,0:T(8,128)(2,1)S(1)}, bf16[16,400,128]{2,1,0:T(8,128)(2,1)S(1)}, f32[8,128]{1,0:T(8,128)S(1)}, f32[8,128]{1,0:T(8,128)S(1)}, bf16[48,768]{1,0:T(8,128)(2,1)S(1)}, ...), branch_computations={%region_6.7_spmd, %region_7.8_spmd} | conditional | bytes 3276808 | solution.py:299
  48.7 1.2 %branch_0_fun.6 = bf16[8,400,128]{2,1,0:T(8,128)(2,1)S(1)} custom-call(bf16[16,400,128]{2,1,0:T(8,128)(2,1)S(1)} %get-tuple-element.57.y_ref, bf16[16,400,128]{2,1,0:T(8,128)(2,1)S(1)} %get-tuple-element.58.e_ref, f32[8,128]{1,0:T(8,128)S(1)} %get-tuple-element.59.mine_ref, f32[8,128]{1,0:T(8,128)S(1)} %get-tuple-element.60.other_ref), custom_call_target="tpu_custom_call" | custom-call | tf_op jit(solution)/shard_map/cond/branch_0_fun/pallas_call | solution.py:290
  49.9 19.2 %all_to_all.28.parts = bf16[8,400,128]{2,1,0:T(8,128)(2,1)S(1)} all-to-all(bf16[8,400,128]{2,1,0:T(8,128)(2,1)S(1)} %branch_0_fun.6), channel_id=1, replica_groups=mesh['z'=8,'y'=4,'x'=4,'c'=2] {'z'}, dimensions={0} | all-to-all | bytes 1638400 | tf_op jit(solution)/shard_map/cond/branch_0_fun/all_to_all | solution.py:227
  69.1 0.2 branch_0_fun.7
  69.4 0.6 collective-permute-start.3
  70.0 1.0 %collective-permute-done.3.recv_ref = f32[40,768]{1,0:T(8,128)S(1)} collective-permute-done((f32[40,768]{1,0:T(8,128)S(1)}, f32[40,768]{1,0:T(8,128)S(1)}, u32[]{:S(2)}, u32[]{:S(2)}) %collective-permute-start.3) | collective-permute-done | bytes 122912 | tf_op jit(solution)/shard_map/ppermute | solution.py:231
  70.9 0.7 shard_map.59
  (1 shorter events, 0.0 us)
Async XLA Ops:
  1.6 4.2 %collective-permute-start = (bf16[48,768]{1,0:T(8,128)(2,1)S(1)}, bf16[48,768]{1,0:T(8,128)(2,1)S(1)}, u32[]{:S(2)}, u32[]{:S(2)}) collective-permute-start(bf16[48,768]{1,0:T(8,128)(2,1)S(1)} %get-tuple-element.80), channel_id=1, source_target_pairs={{0,1},{1,0},{2,3},{3,2},{4,5},{5,4},{6,7},{7,6},{8,9},{9,8},{10,11... | collective-permute-start | bytes 221192 | tf_op jit(solution)/shard_map/ppermute | solution.py:231
  27.7 3.6 %collective-permute-start.1 = (bf16[16,400,128]{2,1,0:T(8,128)(2,1)S(1)}, bf16[16,400,128]{2,1,0:T(8,128)(2,1)S(1)}, u32[]{:S(2)}, u32[]{:S(2)}) collective-permute-start(bf16[16,400,128]{2,1,0:T(8,128)(2,1)S(1)} %get-tuple-element.100), channel_id=1, source_target_pairs={{0,1},{1,0},{2,3},{3,2},{4,5},{5,4},{6,7},{7,6},{8,9},{9,8},{10,11... | collective-permute-start | bytes 4915208 | tf_op jit(solution)/shard_map/ppermute | solution.py:231
  47.5 1.2 %collective-permute-start.2 = (f32[8,128]{1,0:T(8,128)S(1)}, f32[8,128]{1,0:T(8,128)S(1)}, u32[]{:S(2)}, u32[]{:S(2)}) collective-permute-start(f32[8,128]{1,0:T(8,128)S(1)} %get-tuple-element.83), channel_id=1, source_target_pairs={{0,1},{1,0},{2,3},{3,2},{4,5},{5,4},{6,7},{7,6},{8,9},{9,8},{10,11... | collective-permute-start | bytes 12296 | tf_op jit(solution)/shard_map/ppermute | solution.py:231
  69.4 1.6 %collective-permute-start.3 = (f32[40,768]{1,0:T(8,128)S(1)}, f32[40,768]{1,0:T(8,128)S(1)}, u32[]{:S(2)}, u32[]{:S(2)}) collective-permute-start(f32[40,768]{1,0:T(8,128)S(1)} %get-tuple-element.86), channel_id=1, source_target_pairs={{0,1},{1,0},{2,3},{3,2},{4,5},{5,4},{6,7},{7,6},{8,9},{9,8},{10,11... | collective-permute-start | bytes 368648 | tf_op jit(solution)/shard_map/ppermute | solution.py:231

commit v2 on v1

--- a/solution.py
+++ b/solution.py
@@ -83,7 +83,15 @@
         out[b, size:, :] = tile
 
 
-def scores_kernel(images, rows, x_ref, y_ref, e_ref, pay_ref, s_ref, xs_ref, ys_ref):
+def place(images, tiles, r, t, ny):
+    per_half = tiles // 2
+    half, tile = divmod(r * ny + t, per_half)
+    if not images:
+        half = 1 - half
+    return half * (per_half // 2) + tile // 2, slice(tile % 2 * 128, tile % 2 * 128 + 128)
+
+
+def scores_kernel(images, rows, x_ref, y_ref, e_ref, pay_ref, match_ref, *scratch):
     packed = x_ref.shape[1]
     width = (packed - EXTRA) // rows * 128
     per, half = 128 // rows, rows // 2
@@ -109,45 +117,61 @@
         return (chip * (texts * rows) + i + lane % half).astype(f32)
 
     xs, ys = (partners, ids) if images else (ids, partners)
+    xs_ref, ys_ref, *s_refs = scratch
     for r in range(nx):
         xs_ref[r : r + 1] = xs(r)
     for t in range(ny):
         ys_ref[t : t + 1] = ys(t)
-    x = unpack(x_ref, 0, nx * per, rows, width)
-    y = unpack(y_ref, 0, ny * per, rows, width)
-    scores = lax.dot_general(x, y, NT, preferred_element_type=f32)
-    for r in range(nx):
-        for t in range(ny):
-            s_ref[r * ny + t] = scores[r * 128 : (r + 1) * 128, t * 128 : (t + 1) * 128]
-    group = nx // 2
-
-    def part(i, positive):
-        for q in range(group):
-            r = i * group + q
-            own = jnp.broadcast_to(xs_ref[pl.ds(r, 1)], (128, 128)).T
+    part = nx // 2
+
+    def product(h):
+        x = unpack(x_ref, h * part * per, part * per, rows, width)
+        y = unpack(y_ref, 0, ny * per, rows, width)
+        s = lax.dot_general(x, y, NT, preferred_element_type=f32)
+        for r in range(part):
+            for t in range(ny):
+                s_refs[h][r * ny + t] = s[r * 128 : (r + 1) * 128, t * 128 : (t + 1) * 128]
+
+    def weigh(h):
+        for r in range(h * part, (h + 1) * part):
+            own = jnp.broadcast_to(xs_ref[r : r + 1], (128, 128)).T
             lanes = jnp.zeros((128, 128), f32)
+            found = jnp.zeros((128, 128), f32)
             for t in range(ny):
-                piece = s_ref[r * ny + t]
-                match = own == ys_ref[t : t + 1]
-                if not images:
-                    positive += jnp.where(match, piece, f32(0.0))
-                e = jnp.exp2(piece * f32(sharpness * math.log2(math.e)))
+                e = jnp.exp2(s_refs[h][(r - h * part) * ny + t] * f32(sharpness * math.log2(math.e)))
+                matched = jnp.where(own == ys_ref[t : t + 1], e, f32(0.0))
                 lanes += e
-                tile = q * ny + t
-                at = pl.ds(tile % 2 * 128, 128)
-                e_ref[i * (group * ny // 2) + tile // 2, at] = jnp.where(match, -e, e).astype(bf16)
-            pay_ref[0, pl.ds(r, 1)] = jnp.sum(lanes.T, axis=0, keepdims=True)
-        return positive
-
-    positive = lax.fori_loop(0, 2, part, jnp.zeros((128, 128), f32)) * f32(sharpness)
+                found += matched
+                block, at = place(images, nx * ny, r, t, ny)
+                e_ref[block, at] = (e - f32(2.0) * matched).astype(bf16)
+            pay_ref[0, r : r + 1] = jnp.sum(lanes.T, axis=0, keepdims=True)
+            match_ref[r : r + 1] = jnp.sum(found.T, axis=0, keepdims=True)
+
+    once = jnp.minimum(lax.axis_index("c") + 1, 1)
+    product(0)
+
+    def first(i, carry):
+        product(1)
+        weigh(0)
+        return carry
+
+    def second(i, carry):
+        weigh(1)
+        return carry
+
+    lax.fori_loop(0, once, first, 0)
+    lax.fori_loop(0, once, second, 0)
     if not images:
-        positive = jnp.sum(jnp.sum(positive, axis=0, keepdims=True), axis=1, keepdims=True)
-        pay_ref[0, nx:] = jnp.broadcast_to(positive, (8 - nx, 128))
+        m = match_ref[:nx]
+        logs = jnp.where(m > 0.0, jnp.log(jnp.where(m > 0.0, m, f32(1.0))), f32(0.0))
+        logs = jnp.sum(jnp.sum(logs, axis=0, keepdims=True), axis=1, keepdims=True)
+        pay_ref[0, nx:] = jnp.broadcast_to(logs, (8 - nx, 128))
+        match_ref[nx:] = jnp.zeros((8 - nx, 128), f32)
     for b in range(1, pay_ref.shape[0]):
         pay_ref[b] = pay_ref[0]
 
 
-def grads_kernel(images, rows, y_ref, e_ref, mine_ref, other_ref, out_ref):
+def grads_kernel(images, rows, y_ref, e_ref, match_ref, mine_ref, other_ref, out_ref):
     blocks, packed, _ = out_ref.shape
     width = (packed - EXTRA) // rows * 128
     per = 128 // rows
@@ -167,11 +191,13 @@
     ds = []
     for r in range(nx):
         ri = jnp.broadcast_to(row_inv[r : r + 1], (128, 128)).T
+        matched = jnp.broadcast_to(match_ref[r : r + 1], (128, 128)).T
         d = []
         for t in range(ny):
-            tile = r * ny + t
-            e = e_ref[tile // 2, tile % 2 * 128 : tile % 2 * 128 + 128].astype(f32)
-            v = jnp.abs(e) * (ri + col_inv[t : t + 1]) - jnp.where(e < 0.0, f32(2.0), f32(0.0))
+            block, at = place(images, nx * ny, r, t, ny)
+            e = e_ref[block, at].astype(f32)
+            weight = ri + col_inv[t : t + 1]
+            v = jnp.where(e < 0.0, matched * weight - f32(2.0), e * weight)
             d.append(v.astype(bf16))
         ds.append(jnp.concatenate(d, axis=1))
     g = jnp.dot(jnp.concatenate(ds, axis=0), y, preferred_element_type=f32).astype(bf16)
@@ -271,15 +297,16 @@
     y = swap(x)
 
     def sums(images, count, axes):
-        e, pay = call(
+        e, pay, match = call(
             functools.partial(scores_kernel, images, rows),
-            [((n_plane, packed, 128), bf16), ((count, 8, 128), f32)],
+            [((n_plane, packed, 128), bf16), ((count, 8, 128), f32), ((8, 128), f32)],
             input_output_aliases={0: 0},
-            scratch_shapes=[pltpu.VMEM((tiles, 128, 128), f32)] + [pltpu.VMEM((8, 128), f32)] * 2,
+            scratch_shapes=[pltpu.VMEM((8, 128), f32)] * 2
+            + [pltpu.VMEM((tiles // 2, 128, 128), f32)] * 2,
         )(x, y)
-        return e, jnp.sum(exchange(pay, axes), axis=0)
-
-    e, mine = lax.cond(
+        return e, match, jnp.sum(exchange(pay, axes), axis=0)
+
+    e, match, mine = lax.cond(
         image_core,
         functools.partial(sums, True, n_plane, PLANE),
         functools.partial(sums, False, n_line, LINE),
@@ -290,7 +317,7 @@
         pay = call(
             functools.partial(grads_kernel, images, rows),
             [((count, packed, 128), bf16)],
-        )(y, e, mine, other)[0]
+        )(y, e, match, mine, other)[0]
         return call(
             functools.partial(finish_kernel, sharpness / (2.0 * batch), images),
             [((half, size), f32), ((half + 8, size), f32), ((8, 128), f32)],

time: 71.9 us -> 72 us (level)
  no operation moved by 1% of the time
where the time goes in v2:
time: 72 us; the launch traced here: 71.7 us
  blocking collectives  55.2 us (77%)
  waiting for transfers between devices  6.43 us (9%)
  Pallas kernels  5.09 us (7%)
  starting transfers between devices  4.2 us (6%)
    all_to_all x3, blocking collectives, exchange(): return lax.all_to_all(x, axes, 0, 0)  55.2 us
    ppermute x4, waiting for transfers between devices, swap(): return lax.ppermute(x, 'c', [(0, 1), (1, 0)])  6.43 us
    ppermute x4, starting transfers between devices, swap(): return lax.ppermute(x, 'c', [(0, 1), (1, 0)])  4.2 us
    pallas_call x1, Pallas kernels, sums(): call(functools.partial(scores_kernel, images, rows), [((n_plane, packed,...  1.81 us
  transfers between devices with their start and end apart: 4, of which 4 were waited for; matrix products, arithmetic and copies ran while one was open for 0% of the time, Pallas kernels for 0%

profile of v2, /device:TPU:1, one launch (start us, length us, event | category | flops | bytes accessed | tf_op | source)
XLA Modules:
  0.0 71.7 jit_solution(1971658020351432491)
XLA Ops:
  0.6 0.9 %shard_map.58 = (bf16[48,768]{1,0:T(8,128)(2,1)S(1)}, bf16[48,768]{1,0:T(8,128)(2,1)S(1)}) custom-call(bf16[32,768]{1,0:T(8,128)(2,1)} %img_hbm.1, bf16[32,768]{1,0:T(8,128)(2,1)} %txt_hbm.1, s32[1,32]{1,0:T(1,128)} %bitcast.2), custom_call_target="tpu_custom_call" | custom-call | tf_op jit(solution)/shard_map/pallas_call | solution.py:274
  1.6 3.3 %collective-permute-start = (bf16[48,768]{1,0:T(8,128)(2,1)S(1)}, bf16[48,768]{1,0:T(8,128)(2,1)S(1)}, u32[]{:S(2)}, u32[]{:S(2)}) collective-permute-start(bf16[48,768]{1,0:T(8,128)(2,1)S(1)} %get-tuple-element.89), channel_id=1, source_target_pairs={{0,1},{1,0},{2,3},{3,2},{4,5},{5,4},{6,7},{7,6},{8,9},{9,8},{10,11... | collective-permute-start | bytes 221192 | tf_op jit(solution)/shard_map/ppermute | solution.py:257
  4.9 0.9 %collective-permute-done = bf16[48,768]{1,0:T(8,128)(2,1)S(1)} collective-permute-done((bf16[48,768]{1,0:T(8,128)(2,1)S(1)}, bf16[48,768]{1,0:T(8,128)(2,1)S(1)}, u32[]{:S(2)}, u32[]{:S(2)}) %collective-permute-start) | collective-permute-done | bytes 73760 | tf_op jit(solution)/shard_map/ppermute | solution.py:257
  5.8 21.9 %conditional.3 = (bf16[16,400,128]{2,1,0:T(8,128)(2,1)S(1)}) conditional(s32[]{:T(128)} %convert_element_type.4, (bf16[48,768]{1,0:T(8,128)(2,1)S(1)}, bf16[48,768]{1,0:T(8,128)(2,1)S(1)}) %tuple.28, (bf16[48,768]{1,0:T(8,128)(2,1)S(1)}, bf16[48,768]{1,0:T(8,128)(2,1)S(1)}) %tuple.29), branch_computations={%region_0.1_spmd, %region_1.2_spmd} | conditional | bytes 4096010 | solution.py:296
  5.8 0.1 branch_0_fun.4
  6.0 21.6 %all_to_all.24 = bf16[8,400,128]{2,1,0:T(8,128)(2,1)S(1)} all-to-all(bf16[8,400,128]{2,1,0:T(8,128)(2,1)S(1)} %branch_0_fun.4), channel_id=1, replica_groups=mesh['z'=8,'y'=4,'x'=4,'c'=2] {'z'}, dimensions={0} | all-to-all | bytes 1638400 | tf_op jit(solution)/shard_map/cond/branch_0_fun/all_to_all | solution.py:253
  27.5 0.2 pad.3
  27.7 0.1 collective-permute-start.1
  27.8 3.5 %collective-permute-done.1 = bf16[16,400,128]{2,1,0:T(8,128)(2,1)S(1)} collective-permute-done((bf16[16,400,128]{2,1,0:T(8,128)(2,1)S(1)}, bf16[16,400,128]{2,1,0:T(8,128)(2,1)S(1)}, u32[]{:S(2)}, u32[]{:S(2)}) %collective-permute-start.1) | collective-permute-done | bytes 1638432 | tf_op jit(solution)/shard_map/ppermute | solution.py:257
  31.3 16.2 %conditional.4 = (bf16[16,400,128]{2,1,0:T(8,128)(2,1)S(1)}, f32[8,128]{1,0:T(8,128)S(1)}, f32[8,128]{1,0:T(8,128)S(1)}) conditional(s32[]{:T(128)} %convert_element_type.4, (bf16[16,400,128]{2,1,0:T(8,128)(2,1)S(1)}, bf16[16,400,128]{2,1,0:T(8,128)(2,1)S(1)}) %tuple.30, (bf16[16,400,128]{2,1,0:T(8,128)(2,1)S(1)}, ...), branch_computations={%region_2.4_spmd, %region_4.6_spmd} | conditional | flops 15360 | bytes 200732 | solution.py:309
  31.3 1.8 %branch_0_fun.5 = (bf16[16,400,128]{2,1,0:T(8,128)(2,1)S(1)}, f32[8,8,128]{2,1,0:T(8,128)S(1)}, f32[8,128]{1,0:T(8,128)S(1)}) custom-call(bf16[16,400,128]{2,1,0:T(8,128)(2,1)S(1)} %get-tuple-element.51.x_ref, bf16[16,400,128]{2,1,0:T(8,128)(2,1)S(1)} %get-tuple-element.52.y_ref), custom_call_target="tpu_custom_call", output_to_operand_aliasing={{0}: (0, {})} | custom-call | tf_op jit(solution)/shard_map/cond/branch_0_fun/pallas_call | solution.py:300
  33.1 14.4 %all_to_all.26 = f32[8,8,128]{2,1,0:T(8,128)S(1)} all-to-all(f32[8,8,128]{2,1,0:T(8,128)S(1)} %get-tuple-element.55), channel_id=1, replica_groups=mesh['z'=8,'y'=4,'x'=4,'c'=2] {'z'}, dimensions={0} | all-to-all | bytes 65536 | tf_op jit(solution)/shard_map/cond/branch_0_fun/all_to_all | solution.py:253
  47.5 0.2 collective-permute-start.2
  47.7 1.1 %collective-permute-done.2 = f32[8,128]{1,0:T(8,128)S(1)} collective-permute-done((f32[8,128]{1,0:T(8,128)S(1)}, f32[8,128]{1,0:T(8,128)S(1)}, u32[]{:S(2)}, u32[]{:S(2)}) %collective-permute-start.2) | collective-permute-done | bytes 4128 | tf_op jit(solution)/shard_map/ppermute | solution.py:257
  48.8 20.7 %conditional.5 = ((f32[32,768]{1,0:T(8,128)S(1)}, f32[40,768]{1,0:T(8,128)S(1)}, f32[8,128]{1,0:T(8,128)S(1)})) conditional(s32[]{:T(128)} %convert_element_type.4, (bf16[16,400,128]{2,1,0:T(8,128)(2,1)S(1)}, bf16[16,400,128]{2,1,0:T(8,128)(2,1)S(1)}, f32[8,128]{1,0:T(8,128)S(1)}, f32[8,128]{1,0:T(8,128)S(1)}, f32[8,128]{1,0:T(8,128)S(1)}, ...), branch_computations={%region_6.7_spmd, %region_7.8_spmd} | conditional | bytes 3276808 | solution.py:326
  48.8 1.3 %branch_0_fun.6 = bf16[8,400,128]{2,1,0:T(8,128)(2,1)S(1)} custom-call(bf16[16,400,128]{2,1,0:T(8,128)(2,1)S(1)} %get-tuple-element.63.y_ref, bf16[16,400,128]{2,1,0:T(8,128)(2,1)S(1)} %get-tuple-element.64.e_ref, f32[8,128]{1,0:T(8,128)S(1)} %get-tuple-element.65.match_ref, f32[8,128]{1,0:T(8,128)S(1)} %get-tuple-element.66.mine_ref, ...), custom_call_target="tpu_custom_call" | custom-call | tf_op jit(solution)/shard_map/cond/branch_0_fun/pallas_call | solution.py:317
  50.0 19.2 %all_to_all.28.parts = bf16[8,400,128]{2,1,0:T(8,128)(2,1)S(1)} all-to-all(bf16[8,400,128]{2,1,0:T(8,128)(2,1)S(1)} %branch_0_fun.6), channel_id=1, replica_groups=mesh['z'=8,'y'=4,'x'=4,'c'=2] {'z'}, dimensions={0} | all-to-all | bytes 1638400 | tf_op jit(solution)/shard_map/cond/branch_0_fun/all_to_all | solution.py:253
  69.2 0.2 branch_0_fun.7
  69.5 0.6 collective-permute-start.3
  70.1 1.0 %collective-permute-done.3.recv_ref = f32[40,768]{1,0:T(8,128)S(1)} collective-permute-done((f32[40,768]{1,0:T(8,128)S(1)}, f32[40,768]{1,0:T(8,128)S(1)}, u32[]{:S(2)}, u32[]{:S(2)}) %collective-permute-start.3) | collective-permute-done | bytes 122912 | tf_op jit(solution)/shard_map/ppermute | solution.py:257
  71.0 0.7 shard_map.59
  (1 shorter events, 0.0 us)
Async XLA Ops:
  1.6 4.2 %collective-permute-start = (bf16[48,768]{1,0:T(8,128)(2,1)S(1)}, bf16[48,768]{1,0:T(8,128)(2,1)S(1)}, u32[]{:S(2)}, u32[]{:S(2)}) collective-permute-start(bf16[48,768]{1,0:T(8,128)(2,1)S(1)} %get-tuple-element.89), channel_id=1, source_target_pairs={{0,1},{1,0},{2,3},{3,2},{4,5},{5,4},{6,7},{7,6},{8,9},{9,8},{10,11... | collective-permute-start | bytes 221192 | tf_op jit(solution)/shard_map/ppermute | solution.py:257
  27.7 3.6 %collective-permute-start.1 = (bf16[16,400,128]{2,1,0:T(8,128)(2,1)S(1)}, bf16[16,400,128]{2,1,0:T(8,128)(2,1)S(1)}, u32[]{:S(2)}, u32[]{:S(2)}) collective-permute-start(bf16[16,400,128]{2,1,0:T(8,128)(2,1)S(1)} %get-tuple-element.112), channel_id=1, source_target_pairs={{0,1},{1,0},{2,3},{3,2},{4,5},{5,4},{6,7},{7,6},{8,9},{9,8},{10,11... | collective-permute-start | bytes 4915208 | tf_op jit(solution)/shard_map/ppermute | solution.py:257
  47.5 1.2 %collective-permute-start.2 = (f32[8,128]{1,0:T(8,128)S(1)}, f32[8,128]{1,0:T(8,128)S(1)}, u32[]{:S(2)}, u32[]{:S(2)}) collective-permute-start(f32[8,128]{1,0:T(8,128)S(1)} %get-tuple-element.93), channel_id=1, source_target_pairs={{0,1},{1,0},{2,3},{3,2},{4,5},{5,4},{6,7},{7,6},{8,9},{9,8},{10,11... | collective-permute-start | bytes 12296 | tf_op jit(solution)/shard_map/ppermute | solution.py:257
  69.5 1.6 %collective-permute-start.3 = (f32[40,768]{1,0:T(8,128)S(1)}, f32[40,768]{1,0:T(8,128)S(1)}, u32[]{:S(2)}, u32[]{:S(2)}) collective-permute-start(f32[40,768]{1,0:T(8,128)S(1)} %get-tuple-element.96), channel_id=1, source_target_pairs={{0,1},{1,0},{2,3},{3,2},{4,5},{5,4},{6,7},{7,6},{8,9},{9,8},{10,11... | collective-permute-start | bytes 368648 | tf_op jit(solution)/shard_map/ppermute | solution.py:257

commit v3 on v1

v3 whole, which is shorter than its diff:
```python
import functools
import math

import jax
import jax.numpy as jnp
from jax import lax
from jax.experimental import pallas as pl
from jax.experimental.pallas import tpu as pltpu
from jax.sharding import Mesh, PartitionSpec as P

sharpness = 1.0 / 0.07
f32 = jnp.float32
bf16 = jnp.bfloat16
NT = (((1,), (1,)), ((), ()))
PLANE, LINE = ("y", "x"), "z"
EXTRA = 16


def normalize(embed):
    flat = embed.astype(f32)
    factor = lax.rsqrt(jnp.sum(flat * flat, axis=1, keepdims=True) + 1e-06)
    return flat * factor, factor


def unpack(ref, rows, width):
    count = ref.shape[0]
    return jnp.concatenate(
        [
            ref[:, k * rows : (k + 1) * rows, :].reshape(count * rows, 128)
            for k in range(width // 128)
        ],
        axis=1,
    )


def rows_tile(values):
    row = lax.broadcasted_iota(jnp.int32, (EXTRA, 128), 0)
    tile = jnp.zeros((EXTRA, 128), f32)
    for i, v in enumerate(values):
        tile = jnp.where(row == i, v, tile)
    return tile.astype(bf16)


def start_kernel(img_hbm, txt_hbm, partner_hbm, pay_ref, txt_ref, img, txt, partner, sems):
    copies = [
        pltpu.make_async_copy(src, dst, sems.at[i])
        for i, (src, dst) in enumerate(((img_hbm, img), (txt_hbm, txt), (partner_hbm, partner)))
    ]
    for c in copies:
        c.start()
    for c in copies:
        c.wait()
    rows, size = img.shape
    p = jnp.concatenate([partner[...]] * (128 // rows), axis=1)
    hi = p // 128
    tile = rows_tile([hi.astype(f32), (p - hi * 128).astype(f32)])
    unit = normalize(img[...])[0].astype(bf16)
    texts = normalize(txt[...])[0].astype(bf16)
    chunks = size // 128
    for k in range(chunks):
        at = slice(k * 128, (k + 1) * 128)
        txt_ref[k * rows : (k + 1) * rows, :] = texts[:, at]
        for b in range(pay_ref.shape[0]):
            pay_ref[b, k * rows : (k + 1) * rows, :] = unit[:, at]
    for b in range(pay_ref.shape[0]):
        pay_ref[b, chunks * rows :, :] = tile


def chip_texts_kernel(rows, own_ref, off_ref, out_ref):
    low = lax.axis_index("c") == 0
    own, off = own_ref[...].astype(f32), off_ref[...].astype(f32)
    first, second = jnp.where(low, own, off).astype(bf16), jnp.where(low, off, own).astype(bf16)
    for k in range(own.shape[0] // rows):
        at = slice(k * rows, (k + 1) * rows)
        out_ref[2 * k * rows : (2 * k + 1) * rows, :] = first[at]
        out_ref[(2 * k + 1) * rows : (2 * k + 2) * rows, :] = second[at]


def order_texts(images, pieces, texts_ref):
    count = texts_ref.shape[0]
    steps = (count - 1) // 2
    sign = -1 if images else 1
    away = [0, count // 2]
    away += [sign * (k + 1) for k in range(steps)] + [-sign * (k + 1) for k in range(steps)]
    z = lax.axis_index("z")
    for piece, d in zip(pieces, away):
        texts_ref[lax.rem(z + (d + count), count)] = piece[...]


def scores_kernel(images, width, low_ref, high_ref, *refs):
    *pieces, e_ref, pay_ref, match_ref, texts_ref = refs
    plane, packed, _ = low_ref.shape
    line, body, _ = texts_ref.shape
    rows = body * 128 // width // 2
    order_texts(images, pieces, texts_ref)
    lane = lax.broadcasted_iota(jnp.int32, (1, 128), 1)
    chip = lax.axis_index("y") * lax.axis_size("x") + lax.axis_index("x")
    partner = []
    for ref in (low_ref, high_ref):
        tail = ref[:, packed - EXTRA :, :].astype(f32)
        partner.append(tail[:, 0, :] * 128.0 + tail[:, 1, :])
    per = 128 // rows
    image_chunks, text_chunks = 2 * plane // per, 2 * line // per

    def partners(t):
        source, first = partner[t * per // plane], t * per % plane
        p = source[first : first + 1]
        for q in range(1, per):
            p = jnp.where(lane >= q * rows, source[first + q : first + q + 1], p)
        return p

    def ids(t):
        block = t * per // 2 + lane // (2 * rows)
        i = (chip * 2 + lane % (2 * rows) // rows) * (line * rows) + block * rows
        return (i + lane % rows).astype(f32)

    all_images = jnp.concatenate([unpack(r, rows, width) for r in (low_ref, high_ref)], axis=0)
    all_texts = unpack(texts_ref, 2 * rows, width)
    if images:
        x, y, nx, ny, xs, ys = all_images, all_texts, image_chunks, text_chunks, partners, ids
    else:
        x, y, nx, ny, xs, ys = all_texts, all_images, text_chunks, image_chunks, ids, partners
    targets = [ys(t) for t in range(ny)]
    scores = lax.dot_general(x, y, NT, preferred_element_type=f32)
    for r in range(nx):
        own = jnp.broadcast_to(xs(r), (128, 128)).T
        lanes = jnp.zeros((128, 128), f32)
        found = jnp.zeros((128, 128), f32)
        for t in range(ny):
            s = scores[r * 128 : (r + 1) * 128, t * 128 : (t + 1) * 128]
            e = jnp.exp2(s * f32(sharpness * math.log2(math.e)))
            matched = jnp.where(own == targets[t], e, f32(0.0))
            lanes += e
            found += matched
            e_ref[r * ny + t] = (e - f32(2.0) * matched).astype(bf16)
        pay_ref[0, r : r + 1] = jnp.sum(lanes.T, axis=0, keepdims=True)
        match_ref[r : r + 1] = jnp.sum(found.T, axis=0, keepdims=True)
    if not images:
        m = match_ref[:nx]
        logs = jnp.where(m > 0.0, jnp.log(jnp.where(m > 0.0, m, f32(1.0))), f32(0.0))
        logs = jnp.sum(jnp.sum(logs, axis=0, keepdims=True), axis=1, keepdims=True)
        pay_ref[0, nx:] = jnp.broadcast_to(logs, (8 - nx, 128))
        match_ref[nx:] = jnp.zeros((8 - nx, 128), f32)
    for b in range(1, pay_ref.shape[0]):
        pay_ref[b] = pay_ref[0]


def grads_kernel(images, width, e_ref, match_ref, mine_ref, other_ref, *refs):
    if images:
        *pieces, out_ref, texts_ref = refs
        order_texts(images, pieces, texts_ref)
    else:
        low_ref, high_ref, out_ref = refs
    blocks, packed, _ = out_ref.shape
    rows = (packed - EXTRA) * 128 // width // 2
    nx = blocks * 2 * rows // 128
    ny = e_ref.shape[0] // nx
    if images:
        y = unpack(texts_ref, 2 * rows, width)
    else:
        y = jnp.concatenate([unpack(r, rows, width) for r in (low_ref, high_ref)], axis=0)
    col_total = other_ref[:ny]
    col_inv = f32(1.0) / col_total
    share = jnp.sum(jnp.log(col_total), axis=0, keepdims=True)
    share = jnp.broadcast_to(jnp.sum(share, axis=1, keepdims=True), (1, 128))
    if images:
        share -= 2.0 * other_ref[ny : ny + 1]
    hi = share.astype(bf16).astype(f32)
    mid = (share - hi).astype(bf16).astype(f32)
    share = rows_tile([hi, mid, share - hi - mid])
    row_inv = f32(1.0) / mine_ref[:nx]
    ds = []
    for r in range(nx):
        ri = jnp.broadcast_to(row_inv[r : r + 1], (128, 128)).T
        matched = jnp.broadcast_to(match_ref[r : r + 1], (128, 128)).T
        d = []
        for t in range(ny):
            e = e_ref[r * ny + t].astype(f32)
            weight = ri + col_inv[t : t + 1]
            v = jnp.where(e < 0.0, matched * weight - f32(2.0), e * weight)
            d.append(v.astype(bf16))
        ds.append(jnp.concatenate(d, axis=1))
    g = jnp.dot(jnp.concatenate(ds, axis=0), y, preferred_element_type=f32).astype(bf16)
    for b in range(blocks):
        for h in range(2):
            first = (h * blocks + b) * rows if images else (b * 2 + h) * rows
            for k in range(width // 128):
                at = (2 * k + h) * rows
                out_ref[b, at : at + rows, :] = g[first : first + rows, k * 128 : (k + 1) * 128]
        out_ref[b, packed - EXTRA :, :] = share


def sum_kernel(images, parts, keep_ref, send_ref, share_ref):
    rows, size = keep_ref.shape
    body = 2 * rows * (size // 128)
    total = parts[0, :body, :].astype(f32)
    for b in range(1, parts.shape[0]):
        total += parts[b, :body, :].astype(f32)
    low, high = (
        jnp.concatenate(
            [total[(2 * k + h) * rows : (2 * k + h + 1) * rows] for k in range(size // 128)],
            axis=1,
        )
        for h in range(2)
    )
    keep, send = (low, high) if images else (high, low)
    keep_ref[...] = keep
    send_ref[:rows] = send
    share = parts[:, body:, :].astype(f32)
    share = jnp.sum(jnp.sum(share, axis=0), axis=0, keepdims=True)
    share_ref[...] = jnp.broadcast_to(share, share_ref.shape)
    send_ref[rows:] = jnp.broadcast_to(share[:, :1], (send_ref.shape[0] - rows, size))


def output_kernel(batch, img_ref, txt_ref, keep_ref, share_ref, recv_ref, img_out, txt_out, loss_ref):
    low = lax.axis_index("c") == 0
    rows = keep_ref.shape[0]
    keep, recv = keep_ref[...], recv_ref[:rows]
    for src, first, second, dst in ((img_ref, keep, recv, img_out), (txt_ref, recv, keep, txt_out)):
        g = jnp.where(low, first, second) * f32(sharpness / (2.0 * batch))
        unit, factor = normalize(src[...])
        dst[...] = factor * (g - unit * jnp.sum(unit * g, axis=1, keepdims=True))
    loss_ref[...] = (share_ref[:1, :1] + recv_ref[rows : rows + 1, :1]) / (2.0 * batch)


def call(kernel, outs, **kw):
    return pl.pallas_call(
        kernel,
        out_shape=[o if isinstance(o, pl.MemoryRef) else jax.ShapeDtypeStruct(*o) for o in outs],
        compiler_params=pltpu.CompilerParams(vmem_limit_bytes=48 * 1024 * 1024),
        **kw,
    )


def exchange(x, axes):
    return lax.all_to_all(x, axes, 0, 0)


def swap(x):
    return lax.ppermute(x, "c", [(0, 1), (1, 0)])


def local(image_embed, text_embed, partner):
    rows, size = image_embed.shape
    n_plane = lax.axis_size("y") * lax.axis_size("x")
    n_line = lax.axis_size("z")
    batch = 2 * rows * n_plane * n_line
    image_core = lax.axis_index("c") == 0
    half = rows * (size // 128)
    packed = 2 * half + EXTRA
    tiles = n_plane * n_line * 4 * rows * rows // (128 * 128)

    args = [
        pltpu.with_memory_space_constraint(a, pltpu.HBM)
        for a in (image_embed, text_embed, partner.reshape(1, rows))
    ]
    pay, own_texts = call(
        start_kernel,
        [((n_plane, half + EXTRA, 128), bf16), ((half, 128), bf16)],
        in_specs=[pl.BlockSpec(memory_space=pl.ANY)] * 3,
        scratch_shapes=[
            pltpu.VMEM((rows, size), bf16),
            pltpu.VMEM((rows, size), bf16),
            pltpu.VMEM((1, rows), jnp.int32),
            pltpu.SemaphoreType.DMA((3,)),
        ],
    )(*args)
    own_images = exchange(pay, PLANE)
    here = call(functools.partial(chip_texts_kernel, rows), [((2 * half, 128), bf16)])(
        own_texts, swap(own_texts)
    )[0]

    def along(k):
        up = [(2 * z, 2 * ((z + k) % n_line)) for z in range(n_line)]
        down = [(2 * z + 1, 2 * ((z - k) % n_line) + 1) for z in range(n_line)]
        return lax.ppermute(here, ("z", "c"), up + down)

    far = along(n_line // 2)
    near = [along(k + 1) for k in range((n_line - 1) // 2)]
    pieces = [here, far, *near, *[swap(p) for p in near]]
    off_images = swap(own_images)

    def sums(images, count, axes):
        low, high = (own_images, off_images) if images else (off_images, own_images)
        e, pay, match = call(
            functools.partial(scores_kernel, images, size),
            [
                pltpu.VMEM((tiles, 128, 128), bf16),
                ((count, 8, 128), f32),
                ((8, 128), f32),
            ],
            scratch_shapes=[pltpu.VMEM((n_line, 2 * half, 128), bf16)],
        )(low, high, *pieces)
        return e, match, jnp.sum(exchange(pay, axes), axis=0)

    e, match, mine = lax.cond(
        image_core,
        functools.partial(sums, True, n_plane, PLANE),
        functools.partial(sums, False, n_line, LINE),
    )
    other = swap(mine)

    def grads(images, count, axes):
        y = pieces if images else [off_images, own_images]
        kw = {}
        if images:
            kw["scratch_shapes"] = [pltpu.VMEM((n_line, 2 * half, 128), bf16)]
        pay = call(
            functools.partial(grads_kernel, images, size), [((count, packed, 128), bf16)], **kw
        )(e, match, mine, other, *y)[0]
        return call(
            functools.partial(sum_kernel, images),
            [((rows, size), f32), ((rows + 8, size), f32), ((8, 128), f32)],
        )(exchange(pay, axes))

    keep, send, share = lax.cond(
        image_core,
        functools.partial(grads, True, n_plane, PLANE),
        functools.partial(grads, False, n_line, LINE),
    )
    image_grad, text_grad, loss = call(
        functools.partial(output_kernel, batch),
        [((rows, size), f32), ((rows, size), f32), ((1, 1), f32)],
    )(image_embed, text_embed, keep, share, swap(send))
    return loss.reshape(()), image_grad, text_grad


def solution(mesh):
    shape = (mesh.shape["row"], 4, mesh.shape["col"] // 8, 2)
    fine = Mesh(mesh.devices.reshape(shape), ("z", "y", "x", "c"))
    by_image, by_text = P(("z", "y", "x", "c")), P(("y", "x", "c", "z"))
    return jax.shard_map(
        local,
        mesh=fine,
        in_specs=(by_image, by_text, by_image),
        out_specs=(P(), by_image, by_text),
        check_vma=False,
    )
```

time: 71.9 us -> 86.4 us (1.20)
  starting transfers between devices: 4.12 us -> 16.6 us
  waiting for transfers between devices: 6.51 us -> 10.1 us
  blocking collectives: 55.1 us -> 53.2 us
    ppermute x0 -> x4, starting transfers between devices: none -> 11.8 us  [along(): return lax.ppermute(here, ('z', 'c'), up + down)]
    ppermute x0 -> x4, waiting for transfers between devices: none -> 5.25 us  [along(): return lax.ppermute(here, ('z', 'c'), up + down)]
    all_to_all x3, blocking collectives: 55.1 us -> 53.2 us  [exchange(): return lax.all_to_all(x, axes, 0, 0)]
    ppermute x4 -> x7, waiting for transfers between devices: 6.51 us -> 4.88 us  [swap(): return lax.ppermute(x, 'c', [(0, 1), (1, 0)])]
    ppermute x4 -> x7, starting transfers between devices: 4.12 us -> 4.81 us  [swap(): return lax.ppermute(x, 'c', [(0, 1), (1, 0)])]
  transfers between devices with their start and end apart: 4 -> 11, of which waited for: 4 -> 7; matrix products, arithmetic and copies ran while one was open for 0% -> 0% of each run, Pallas kernels for 0% -> 0%
where the time goes in v3:
time: 86.4 us; the launch traced here: 86.1 us
  blocking collectives  53.2 us (62%)
  starting transfers between devices  16.6 us (19%)
  waiting for transfers between devices  10.1 us (12%)
  Pallas kernels  5.54 us (6%)
    all_to_all x3, blocking collectives, exchange(): return lax.all_to_all(x, axes, 0, 0)  53.2 us
    ppermute x4, starting transfers between devices, along(): return lax.ppermute(here, ('z', 'c'), up + down)  11.8 us
    ppermute x4, waiting for transfers between devices, along(): return lax.ppermute(here, ('z', 'c'), up + down)  5.25 us
    ppermute x7, waiting for transfers between devices, swap(): return lax.ppermute(x, 'c', [(0, 1), (1, 0)])  4.88 us
    ppermute x7, starting transfers between devices, swap(): return lax.ppermute(x, 'c', [(0, 1), (1, 0)])  4.81 us
    pallas_call x1, Pallas kernels, sums(): call(functools.partial(scores_kernel, images, size), [pltpu.VMEM((tiles,...  2.24 us
  transfers between devices with their start and end apart: 11, of which 7 were waited for; matrix products, arithmetic and copies ran while one was open for 0% of the time, Pallas kernels for 0%

profile of v3, /device:TPU:1, one launch (start us, length us, event | category | flops | bytes accessed | tf_op | source)
XLA Modules:
  0.0 86.1 jit_solution(995575172410682652)
XLA Ops:
  0.6 1.0 %shard_map.58 = (bf16[16,208,128]{2,1,0:T(8,128)(2,1)S(1)}, bf16[192,128]{1,0:T(8,128)(2,1)S(1)}) custom-call(bf16[32,768]{1,0:T(8,128)(2,1)} %img_ref.1, bf16[32,768]{1,0:T(8,128)(2,1)} %txt_ref.1, s32[1,32]{1,0:T(1,128)} %bitcast.2), custom_call_target="tpu_custom_call" | custom-call | tf_op jit(solution)/shard_map/pallas_call | solution.py:257
  1.6 21.6 %all_to_all.25 = bf16[16,208,128]{2,1,0:T(8,128)(2,1)S(1)} all-to-all(bf16[16,208,128]{2,1,0:T(8,128)(2,1)S(1)} %get-tuple-element.134), channel_id=1, replica_groups=mesh['z'=8,'y'=4,'x'=4,'c'=2] {'y','x'}, dimensions={0} | all-to-all | bytes 1703936 | tf_op jit(solution)/shard_map/all_to_all | solution.py:236
  23.2 1.8 %collective-permute-start = (bf16[16,208,128]{2,1,0:T(8,128)(2,1)S(1)}, bf16[16,208,128]{2,1,0:T(8,128)(2,1)S(1)}, u32[]{:S(2)}, u32[]{:S(2)}) collective-permute-start(bf16[16,208,128]{2,1,0:T(8,128)(2,1)S(1)} %all_to_all.25), channel_id=1, source_target_pairs={{0,1},{1,0},{2,3},{3,2},{4,5},{5,4},{6,7},{7,6},{8,9},{9,8},{10,11... | collective-permute-start | bytes 2555912 | tf_op jit(solution)/shard_map/ppermute | solution.py:240
  25.0 0.0 collective-permute-start.1
  25.0 2.1 %collective-permute-done.1.off_ref = bf16[192,128]{1,0:T(8,128)(2,1)S(1)} collective-permute-done((bf16[192,128]{1,0:T(8,128)(2,1)S(1)}, bf16[192,128]{1,0:T(8,128)(2,1)S(1)}, u32[]{:S(2)}, u32[]{:S(2)}) %collective-permute-start.1) | collective-permute-done | bytes 49184 | tf_op jit(solution)/shard_map/ppermute | solution.py:240
  27.1 6.5 %collective-permute-start.5 = (bf16[384,128]{1,0:T(8,128)(2,1)S(1)}, bf16[384,128]{1,0:T(8,128)(2,1)S(1)}, u32[]{:S(2)}, u32[]{:S(2)}) collective-permute-start(bf16[384,128]{1,0:T(8,128)(2,1)S(1)} %shard_map.59), channel_id=1, source_target_pairs={{0,96},{32,128},{64,160},{96,192},{128,224},{160,0},{192,32},{224,... | collective-permute-start | bytes 294920 | tf_op jit(solution)/shard_map/ppermute | solution.py:276
  33.7 0.3 collective-permute-start.4
  33.9 0.5 collective-permute-start.3
  34.4 4.5 %collective-permute-start.2 = (bf16[384,128]{1,0:T(8,128)(2,1)S(1)}, bf16[384,128]{1,0:T(8,128)(2,1)S(1)}, u32[]{:S(2)}, u32[]{:S(2)}) collective-permute-start(bf16[384,128]{1,0:T(8,128)(2,1)S(1)} %shard_map.59), channel_id=1, source_target_pairs={{0,128},{32,160},{64,192},{96,224},{128,0},{160,32},{192,64},{224,... | collective-permute-start | bytes 294920 | tf_op jit(solution)/shard_map/ppermute | solution.py:276
  38.9 0.0 collective-permute-done.5
  38.9 0.0 collective-permute-start.8
  38.9 1.0 %collective-permute-done.4 = bf16[384,128]{1,0:T(8,128)(2,1)S(1)} collective-permute-done((bf16[384,128]{1,0:T(8,128)(2,1)S(1)}, bf16[384,128]{1,0:T(8,128)(2,1)S(1)}, u32[]{:S(2)}, u32[]{:S(2)}) %collective-permute-start.4) | collective-permute-done | bytes 98336 | tf_op jit(solution)/shard_map/ppermute | solution.py:276
  39.9 0.8 collective-permute-start.7
  40.7 3.9 %collective-permute-done.3 = bf16[384,128]{1,0:T(8,128)(2,1)S(1)} collective-permute-done((bf16[384,128]{1,0:T(8,128)(2,1)S(1)}, bf16[384,128]{1,0:T(8,128)(2,1)S(1)}, u32[]{:S(2)}, u32[]{:S(2)}) %collective-permute-start.3) | collective-permute-done | bytes 98336 | tf_op jit(solution)/shard_map/ppermute | solution.py:276
  44.6 1.0 %collective-permute-start.6 = (bf16[384,128]{1,0:T(8,128)(2,1)S(1)}, bf16[384,128]{1,0:T(8,128)(2,1)}, u32[]{:S(2)}, u32[]{:S(2)}) collective-permute-start(bf16[384,128]{1,0:T(8,128)(2,1)S(1)} %collective-permute-done.3), channel_id=1, source_target_pairs={{0,1},{1,0},{2,3},{3,2},{4,5},{5,4},{6,7},{7,6},{8,9},{9,8},{10,11... | collective-permute-start | bytes 294920 | tf_op jit(solution)/shard_map/ppermute | solution.py:240
  45.5 0.4 collective-permute-done.2
  45.9 0.0 collective-permute-done.8
  45.9 0.0 collective-permute-done.7
  45.9 0.7 collective-permute-done.6
  46.6 0.0 collective-permute-done
  46.6 14.5 %conditional.2 = (bf16[32,128,128]{2,1,0:T(8,128)(2,1)S(1)}, f32[8,128]{1,0:T(8,128)S(1)}, f32[8,128]{1,0:T(8,128)S(1)}) conditional(s32[]{:T(128)} %convert_element_type.4, (bf16[16,208,128]{2,1,0:T(8,128)(2,1)S(1)}, bf16[16,208,128]{2,1,0:T(8,128)(2,1)S(1)}, bf16[384,128]{1,0:T(8,128)(2,1)S(1)}, bf16[384,128]{1,0:T(8,128)(2,1)S(1)}, ...), branch_computations={%region_0.0_spmd, %region_2.0_spmd} | conditional | flops 15360 | bytes 200732 | solution.py:296
  46.6 2.2 %branch_0_fun.3 = (bf16[32,128,128]{2,1,0:T(8,128)(2,1)S(1)}, f32[8,8,128]{2,1,0:T(8,128)S(1)}, f32[8,128]{1,0:T(8,128)S(1)}) custom-call(bf16[16,208,128]{2,1,0:T(8,128)(2,1)S(1)} %get-tuple-element.76.low_ref, bf16[16,208,128]{2,1,0:T(8,128)(2,1)S(1)} %get-tuple-element.77.high_ref, bf16[384,128]{1,0:T(8,128)(2,1)S(1)} %get-tuple-element.78.refs_0_, ...), custom_call_target="tpu_custom_call" | custom-call | tf_op jit(solution)/shard_map/cond/branch_0_fun/pallas_call | solution.py:285
  48.8 12.3 %all_to_all.21 = f32[8,8,128]{2,1,0:T(8,128)S(1)} all-to-all(f32[8,8,128]{2,1,0:T(8,128)S(1)} %get-tuple-element.88), channel_id=1, replica_groups=mesh['z'=8,'y'=4,'x'=4,'c'=2] {'z'}, dimensions={0} | all-to-all | bytes 65536 | tf_op jit(solution)/shard_map/cond/branch_0_fun/all_to_all | solution.py:236
  61.1 0.1 collective-permute-start.9
  61.2 1.2 %collective-permute-done.9 = f32[8,128]{1,0:T(8,128)S(1)} collective-permute-done((f32[8,128]{1,0:T(8,128)S(1)}, f32[8,128]{1,0:T(8,128)S(1)}, u32[]{:S(2)}, u32[]{:S(2)}) %collective-permute-start.9) | collective-permute-done | bytes 4128 | tf_op jit(solution)/shard_map/ppermute | solution.py:240
  62.4 20.8 %conditional.3 = ((f32[32,768]{1,0:T(8,128)S(1)}, f32[40,768]{1,0:T(8,128)S(1)}, f32[8,128]{1,0:T(8,128)S(1)})) conditional(s32[]{:T(128)} %convert_element_type.4, (bf16[32,128,128]{2,1,0:T(8,128)(2,1)S(1)}, f32[8,128]{1,0:T(8,128)S(1)}, f32[8,128]{1,0:T(8,128)S(1)}, f32[8,128]{1,0:T(8,128)S(1)}, bf16[16,208,128]{2,1,0:T(8,128)(2,1)S(1)}, ...), branch_computations={%region_4.0_spmd, %region_5.0_spmd} | conditional | bytes 3276808 | solution.py:316
  62.4 1.3 %branch_0_fun.4 = bf16[8,400,128]{2,1,0:T(8,128)(2,1)S(1)} custom-call(bf16[32,128,128]{2,1,0:T(8,128)(2,1)S(1)} %get-tuple-element.102.e_ref, f32[8,128]{1,0:T(8,128)S(1)} %get-tuple-element.103.match_ref, f32[8,128]{1,0:T(8,128)S(1)} %get-tuple-element.104.mine_ref, f32[8,128]{1,0:T(8,128)S(1)} %get-tuple-element.105.other_ref, ...), custom_call_target="tpu_custom_call" | custom-call | tf_op jit(solution)/shard_map/cond/branch_0_fun/pallas_call | solution.py:308
  63.6 19.3 %all_to_all.23.parts = bf16[8,400,128]{2,1,0:T(8,128)(2,1)S(1)} all-to-all(bf16[8,400,128]{2,1,0:T(8,128)(2,1)S(1)} %branch_0_fun.4), channel_id=1, replica_groups=mesh['z'=8,'y'=4,'x'=4,'c'=2] {'z'}, dimensions={0} | all-to-all | bytes 1638400 | tf_op jit(solution)/shard_map/cond/branch_0_fun/all_to_all | solution.py:236
  83.0 0.1 branch_0_fun.5
  83.1 1.1 %collective-permute-start.10 = (f32[40,768]{1,0:T(8,128)S(1)}, f32[40,768]{1,0:T(8,128)S(1)}, u32[]{:S(2)}, u32[]{:S(2)}) collective-permute-start(f32[40,768]{1,0:T(8,128)S(1)} %get-tuple-element.141), channel_id=1, source_target_pairs={{0,1},{1,0},{2,3},{3,2},{4,5},{5,4},{6,7},{7,6},{8,9},{9,8},{10,11... | collective-permute-start | bytes 368648 | tf_op jit(solution)/shard_map/ppermute | solution.py:240
  84.2 1.0 %collective-permute-done.10.recv_ref = f32[40,768]{1,0:T(8,128)S(1)} collective-permute-done((f32[40,768]{1,0:T(8,128)S(1)}, f32[40,768]{1,0:T(8,128)S(1)}, u32[]{:S(2)}, u32[]{:S(2)}) %collective-permute-start.10) | collective-permute-done | bytes 122912 | tf_op jit(solution)/shard_map/ppermute | solution.py:240
  85.2 0.9 %shard_map.60 = (f32[32,768]{1,0:T(8,128)}, f32[32,768]{1,0:T(8,128)}, f32[1,1]{1,0:T(1,128)}) custom-call(bf16[32,768]{1,0:T(8,128)(2,1)S(1)} %copy-done, bf16[32,768]{1,0:T(8,128)(2,1)S(1)} %copy-done.1, f32[32,768]{1,0:T(8,128)S(1)} %get-tuple-element.139.keep_ref, f32[8,128]{1,0:T(8,128)S(1)} %get-tuple-element.140.share_ref, ...), custom_call_target="tpu_custom_call" | custom-call | tf_op jit(solution)/shard_map/pallas_call | solution.py:321
  (6 shorter events, 0.0 us)
Async XLA Ops:
  23.2 23.4 %collective-permute-start = (bf16[16,208,128]{2,1,0:T(8,128)(2,1)S(1)}, bf16[16,208,128]{2,1,0:T(8,128)(2,1)S(1)}, u32[]{:S(2)}, u32[]{:S(2)}) collective-permute-start(bf16[16,208,128]{2,1,0:T(8,128)(2,1)S(1)} %all_to_all.25), channel_id=1, source_target_pairs={{0,1},{1,0},{2,3},{3,2},{4,5},{5,4},{6,7},{7,6},{8,9},{9,8},{10,11... | collective-permute-start | bytes 2555912 | tf_op jit(solution)/shard_map/ppermute | solution.py:240
  25.0 2.1 %collective-permute-start.1 = (bf16[192,128]{1,0:T(8,128)(2,1)S(1)}, bf16[192,128]{1,0:T(8,128)(2,1)S(1)}, u32[]{:S(2)}, u32[]{:S(2)}) collective-permute-start(bf16[192,128]{1,0:T(8,128)(2,1)S(1)} %get-tuple-element.135.own_ref), channel_id=1, source_target_pairs={{0,1},{1,0},{2,3},{3,2},{4,5},{5,4},{6,7},{7,6},{8,9},{9,8},{10,11... | collective-permute-start | bytes 147464 | tf_op jit(solution)/shard_map/ppermute | solution.py:240
  27.1 11.8 %collective-permute-start.5 = (bf16[384,128]{1,0:T(8,128)(2,1)S(1)}, bf16[384,128]{1,0:T(8,128)(2,1)S(1)}, u32[]{:S(2)}, u32[]{:S(2)}) collective-permute-start(bf16[384,128]{1,0:T(8,128)(2,1)S(1)} %shard_map.59), channel_id=1, source_target_pairs={{0,96},{32,128},{64,160},{96,192},{128,224},{160,0},{192,32},{224,... | collective-permute-start | bytes 294920 | tf_op jit(solution)/shard_map/ppermute | solution.py:276
  33.7 6.2 %collective-permute-start.4 = (bf16[384,128]{1,0:T(8,128)(2,1)S(1)}, bf16[384,128]{1,0:T(8,128)(2,1)S(1)}, u32[]{:S(2)}, u32[]{:S(2)}) collective-permute-start(bf16[384,128]{1,0:T(8,128)(2,1)S(1)} %shard_map.59), channel_id=1, source_target_pairs={{0,64},{32,96},{64,128},{96,160},{128,192},{160,224},{192,0},{224,... | collective-permute-start | bytes 294920 | tf_op jit(solution)/shard_map/ppermute | solution.py:276
  33.9 10.6 %collective-permute-start.3 = (bf16[384,128]{1,0:T(8,128)(2,1)S(1)}, bf16[384,128]{1,0:T(8,128)(2,1)S(1)}, u32[]{:S(2)}, u32[]{:S(2)}) collective-permute-start(bf16[384,128]{1,0:T(8,128)(2,1)S(1)} %shard_map.59), channel_id=1, source_target_pairs={{0,32},{32,64},{64,96},{96,128},{128,160},{160,192},{192,224},{224... | collective-permute-start | bytes 294920 | tf_op jit(solution)/shard_map/ppermute | solution.py:276
  34.4 11.5 %collective-permute-start.2 = (bf16[384,128]{1,0:T(8,128)(2,1)S(1)}, bf16[384,128]{1,0:T(8,128)(2,1)S(1)}, u32[]{:S(2)}, u32[]{:S(2)}) collective-permute-start(bf16[384,128]{1,0:T(8,128)(2,1)S(1)} %shard_map.59), channel_id=1, source_target_pairs={{0,128},{32,160},{64,192},{96,224},{128,0},{160,32},{192,64},{224,... | collective-permute-start | bytes 294920 | tf_op jit(solution)/shard_map/ppermute | solution.py:276
  38.9 7.0 %collective-permute-start.8 = (bf16[384,128]{1,0:T(8,128)(2,1)S(1)}, bf16[384,128]{1,0:T(8,128)(2,1)S(1)}, u32[]{:S(2)}, u32[]{:S(2)}) collective-permute-start(bf16[384,128]{1,0:T(8,128)(2,1)S(1)} %collective-permute-done.5), channel_id=1, source_target_pairs={{0,1},{1,0},{2,3},{3,2},{4,5},{5,4},{6,7},{7,6},{8,9},{9,8},{10,11... | collective-permute-start | bytes 294920 | tf_op jit(solution)/shard_map/ppermute | solution.py:240
  39.9 6.0 %collective-permute-start.7 = (bf16[384,128]{1,0:T(8,128)(2,1)S(1)}, bf16[384,128]{1,0:T(8,128)(2,1)S(1)}, u32[]{:S(2)}, u32[]{:S(2)}) collective-permute-start(bf16[384,128]{1,0:T(8,128)(2,1)S(1)} %collective-permute-done.4), channel_id=1, source_target_pairs={{0,1},{1,0},{2,3},{3,2},{4,5},{5,4},{6,7},{7,6},{8,9},{9,8},{10,11... | collective-permute-start | bytes 294920 | tf_op jit(solution)/shard_map/ppermute | solution.py:240
  44.6 2.0 %collective-permute-start.6 = (bf16[384,128]{1,0:T(8,128)(2,1)S(1)}, bf16[384,128]{1,0:T(8,128)(2,1)}, u32[]{:S(2)}, u32[]{:S(2)}) collective-permute-start(bf16[384,128]{1,0:T(8,128)(2,1)S(1)} %collective-permute-done.3), channel_id=1, source_target_pairs={{0,1},{1,0},{2,3},{3,2},{4,5},{5,4},{6,7},{7,6},{8,9},{9,8},{10,11... | collective-permute-start | bytes 294920 | tf_op jit(solution)/shard_map/ppermute | solution.py:240
  61.1 1.2 %collective-permute-start.9 = (f32[8,128]{1,0:T(8,128)S(1)}, f32[8,128]{1,0:T(8,128)S(1)}, u32[]{:S(2)}, u32[]{:S(2)}) collective-permute-start(f32[8,128]{1,0:T(8,128)S(1)} %get-tuple-element.138), channel_id=1, source_target_pairs={{0,1},{1,0},{2,3},{3,2},{4,5},{5,4},{6,7},{7,6},{8,9},{9,8},{10,11... | collective-permute-start | bytes 12296 | tf_op jit(solution)/shard_map/ppermute | solution.py:240
  62.4 22.9 %copy-start = (bf16[32,768]{1,0:T(8,128)(2,1)S(1)}, bf16[32,768]{1,0:T(8,128)(2,1)}, u32[]{:S(2)}) copy-start(bf16[32,768]{1,0:T(8,128)(2,1)} %img_ref.1) | copy-start | bytes 147460
  62.4 22.9 %copy-start.1 = (bf16[32,768]{1,0:T(8,128)(2,1)S(1)}, bf16[32,768]{1,0:T(8,128)(2,1)}, u32[]{:S(2)}) copy-start(bf16[32,768]{1,0:T(8,128)(2,1)} %txt_ref.1) | copy-start | bytes 147460
  83.1 2.1 %collective-permute-start.10 = (f32[40,768]{1,0:T(8,128)S(1)}, f32[40,768]{1,0:T(8,128)S(1)}, u32[]{:S(2)}, u32[]{:S(2)}) collective-permute-start(f32[40,768]{1,0:T(8,128)S(1)} %get-tuple-element.141), channel_id=1, source_target_pairs={{0,1},{1,0},{2,3},{3,2},{4,5},{5,4},{6,7},{7,6},{8,9},{9,8},{10,11... | collective-permute-start | bytes 368648 | tf_op jit(solution)/shard_map/ppermute | solution.py:240

commit v4 on v2

--- a/solution.py
+++ b/solution.py
@@ -44,6 +44,16 @@
     for i, v in enumerate(values):
         tile = jnp.where(row == i, v, tile)
     return tile.astype(bf16)
+
+
+LEVELS = 32760.0
+
+
+def encode(value):
+    most = jnp.max(jnp.abs(value), axis=0, keepdims=True)
+    t = jnp.ceil(f32(8.0) * jnp.log2(jnp.maximum(most, f32(1e-30))) + f32(0.01))
+    scaled = value * (f32(LEVELS) * jnp.exp2(t * f32(-0.125)))
+    return jnp.floor(scaled + f32(0.5)).astype(jnp.int32), t.astype(jnp.int32)
 
 
 def start_kernel(img_hbm, txt_hbm, partner_hbm, keep_ref, send_ref, img, txt, partner, sems):
@@ -183,9 +193,9 @@
     share = jnp.broadcast_to(jnp.sum(share, axis=1, keepdims=True), (1, 128))
     if images:
         share -= 2.0 * other_ref[ny : ny + 1]
-    hi = share.astype(bf16).astype(f32)
-    mid = (share - hi).astype(bf16).astype(f32)
-    share = rows_tile([hi, mid, share - hi - mid])
+    whole = jnp.floor(share + f32(0.5))
+    share = [whole.astype(jnp.int32), ((share - whole) * f32(32768.0)).astype(jnp.int32)]
+    rest = [jnp.zeros((EXTRA - 2 - width // 128, 128), jnp.int32)]
     row_inv = f32(1.0) / mine_ref[:nx]
     y = unpack(y_ref, 0, ny * per, rows, width)
     ds = []
@@ -200,23 +210,33 @@
             v = jnp.where(e < 0.0, matched * weight - f32(2.0), e * weight)
             d.append(v.astype(bf16))
         ds.append(jnp.concatenate(d, axis=1))
-    g = jnp.dot(jnp.concatenate(ds, axis=0), y, preferred_element_type=f32).astype(bf16)
+    g = jnp.dot(jnp.concatenate(ds, axis=0), y, preferred_element_type=f32)
     for b in range(blocks):
-        pack(out_ref, b, g[b * rows : (b + 1) * rows])
-        out_ref[b, packed - EXTRA :, :] = share
+        steps = []
+        for k in range(width // 128):
+            q, t = encode(g[b * rows : (b + 1) * rows, k * 128 : (k + 1) * 128])
+            out_ref[b, k * rows : (k + 1) * rows, :] = q.astype(jnp.int16)
+            steps.append(t)
+        tile = jnp.concatenate(steps + share + rest, axis=0)
+        out_ref[b, packed - EXTRA :, :] = tile.astype(jnp.int16)
 
 
 def finish_kernel(scale, keep_first, first, second, parts, keep_ref, send_ref, share_ref):
     half, size = keep_ref.shape
     rows = 2 * half
     body = rows * (size // 128)
-    total = parts[0, :body, :].astype(f32)
-    for b in range(1, parts.shape[0]):
-        total += parts[b, :body, :].astype(f32)
-    total = total * f32(scale)
-    total = jnp.concatenate(
-        [total[k * rows : (k + 1) * rows] for k in range(size // 128)], axis=1
-    )
+    chunks = size // 128
+    tail = parts[:, body:, :].astype(jnp.int32).astype(f32)
+    step = jnp.exp2(tail[:, :chunks] * f32(0.125)) * f32(scale / LEVELS)
+    total = []
+    for k in range(chunks):
+        piece = None
+        for b in range(parts.shape[0]):
+            q = parts[b, k * rows : (k + 1) * rows, :].astype(jnp.int32).astype(f32)
+            q = q * step[b, k : k + 1]
+            piece = q if piece is None else piece + q
+        total.append(piece)
+    total = jnp.concatenate(total, axis=1)
     grads = []
     for i, src in enumerate((first, second)):
         unit, factor = normalize(src[:half, :])
@@ -225,8 +245,8 @@
     keep, send = grads if keep_first else grads[::-1]
     keep_ref[...] = keep
     send_ref[:half] = send
-    share = parts[:, body:, :].astype(f32)
-    share = jnp.sum(jnp.sum(share, axis=0), axis=0, keepdims=True)
+    share = jnp.sum(tail[:, chunks : chunks + 1], axis=0)
+    share += jnp.sum(tail[:, chunks + 1 : chunks + 2], axis=0) * f32(1.0 / 32768.0)
     share_ref[...] = jnp.broadcast_to(share, share_ref.shape)
     send_ref[half:] = jnp.broadcast_to(share[:, :1], (send_ref.shape[0] - half, size))
 
@@ -316,7 +336,7 @@
     def grads(images, count, axes):
         pay = call(
             functools.partial(grads_kernel, images, rows),
-            [((count, packed, 128), bf16)],
+            [((count, packed, 128), jnp.int16)],
         )(y, e, match, mine, other)[0]
         return call(
             functools.partial(finish_kernel, sharpness / (2.0 * batch), images),

time: 72 us -> 72.9 us (1.013)
  no operation moved by 1% of the time
where the time goes in v4:
time: 72.9 us; the launch traced here: 72.7 us
  blocking collectives  55.4 us (76%)
  waiting for transfers between devices  6.43 us (9%)
  Pallas kernels  5.56 us (8%)
  starting transfers between devices  4.46 us (6%)
    all_to_all x3, blocking collectives, exchange(): return lax.all_to_all(x, axes, 0, 0)  55.4 us
    ppermute x4, waiting for transfers between devices, swap(): return lax.ppermute(x, 'c', [(0, 1), (1, 0)])  6.43 us
    ppermute x4, starting transfers between devices, swap(): return lax.ppermute(x, 'c', [(0, 1), (1, 0)])  4.46 us
    pallas_call x1, Pallas kernels, sums(): call(functools.partial(scores_kernel, images, rows), [((n_plane, packed,...  1.81 us
    pallas_call x1, Pallas kernels, grads(): call(functools.partial(grads_kernel, images, rows), [((count, packed, 128...  1.63 us
  transfers between devices with their start and end apart: 4, of which 4 were waited for; matrix products, arithmetic and copies ran while one was open for 0% of the time, Pallas kernels for 0%

profile of v4, /device:TPU:1, one launch (start us, length us, event | category | flops | bytes accessed | tf_op | source)
XLA Modules:
  0.0 72.7 jit_solution(3118604160468542409)
XLA Ops:
  0.6 0.9 %shard_map.58 = (bf16[48,768]{1,0:T(8,128)(2,1)S(1)}, bf16[48,768]{1,0:T(8,128)(2,1)S(1)}) custom-call(bf16[32,768]{1,0:T(8,128)(2,1)} %img_hbm.1, bf16[32,768]{1,0:T(8,128)(2,1)} %txt_hbm.1, s32[1,32]{1,0:T(1,128)} %bitcast.2), custom_call_target="tpu_custom_call" | custom-call | tf_op jit(solution)/shard_map/pallas_call | solution.py:294
  1.6 3.3 %collective-permute-start = (bf16[48,768]{1,0:T(8,128)(2,1)S(1)}, bf16[48,768]{1,0:T(8,128)(2,1)S(1)}, u32[]{:S(2)}, u32[]{:S(2)}) collective-permute-start(bf16[48,768]{1,0:T(8,128)(2,1)S(1)} %get-tuple-element.89), channel_id=1, source_target_pairs={{0,1},{1,0},{2,3},{3,2},{4,5},{5,4},{6,7},{7,6},{8,9},{9,8},{10,11... | collective-permute-start | bytes 221192 | tf_op jit(solution)/shard_map/ppermute | solution.py:277
  4.9 0.9 %collective-permute-done = bf16[48,768]{1,0:T(8,128)(2,1)S(1)} collective-permute-done((bf16[48,768]{1,0:T(8,128)(2,1)S(1)}, bf16[48,768]{1,0:T(8,128)(2,1)S(1)}, u32[]{:S(2)}, u32[]{:S(2)}) %collective-permute-start) | collective-permute-done | bytes 73760 | tf_op jit(solution)/shard_map/ppermute | solution.py:277
  5.8 21.9 %conditional.3 = (bf16[16,400,128]{2,1,0:T(8,128)(2,1)S(1)}) conditional(s32[]{:T(128)} %convert_element_type.4, (bf16[48,768]{1,0:T(8,128)(2,1)S(1)}, bf16[48,768]{1,0:T(8,128)(2,1)S(1)}) %tuple.28, (bf16[48,768]{1,0:T(8,128)(2,1)S(1)}, bf16[48,768]{1,0:T(8,128)(2,1)S(1)}) %tuple.29), branch_computations={%region_0.1_spmd, %region_1.2_spmd} | conditional | bytes 4096010 | solution.py:316
  5.8 0.1 branch_0_fun.4
  6.0 21.6 %all_to_all.24 = bf16[8,400,128]{2,1,0:T(8,128)(2,1)S(1)} all-to-all(bf16[8,400,128]{2,1,0:T(8,128)(2,1)S(1)} %branch_0_fun.4), channel_id=1, replica_groups=mesh['z'=8,'y'=4,'x'=4,'c'=2] {'z'}, dimensions={0} | all-to-all | bytes 1638400 | tf_op jit(solution)/shard_map/cond/branch_0_fun/all_to_all | solution.py:273
  27.5 0.2 pad.3
  27.7 0.1 collective-permute-start.1
  27.8 3.5 %collective-permute-done.1 = bf16[16,400,128]{2,1,0:T(8,128)(2,1)S(1)} collective-permute-done((bf16[16,400,128]{2,1,0:T(8,128)(2,1)S(1)}, bf16[16,400,128]{2,1,0:T(8,128)(2,1)S(1)}, u32[]{:S(2)}, u32[]{:S(2)}) %collective-permute-start.1) | collective-permute-done | bytes 1638432 | tf_op jit(solution)/shard_map/ppermute | solution.py:277
  31.3 16.2 %conditional.4 = (bf16[16,400,128]{2,1,0:T(8,128)(2,1)S(1)}, f32[8,128]{1,0:T(8,128)S(1)}, f32[8,128]{1,0:T(8,128)S(1)}) conditional(s32[]{:T(128)} %convert_element_type.4, (bf16[16,400,128]{2,1,0:T(8,128)(2,1)S(1)}, bf16[16,400,128]{2,1,0:T(8,128)(2,1)S(1)}) %tuple.30, (bf16[16,400,128]{2,1,0:T(8,128)(2,1)S(1)}, ...), branch_computations={%region_2.4_spmd, %region_4.6_spmd} | conditional | flops 15360 | bytes 200732 | solution.py:329
  31.3 1.8 %branch_0_fun.5 = (bf16[16,400,128]{2,1,0:T(8,128)(2,1)S(1)}, f32[8,8,128]{2,1,0:T(8,128)S(1)}, f32[8,128]{1,0:T(8,128)S(1)}) custom-call(bf16[16,400,128]{2,1,0:T(8,128)(2,1)S(1)} %get-tuple-element.51.x_ref, bf16[16,400,128]{2,1,0:T(8,128)(2,1)S(1)} %get-tuple-element.52.y_ref), custom_call_target="tpu_custom_call", output_to_operand_aliasing={{0}: (0, {})} | custom-call | tf_op jit(solution)/shard_map/cond/branch_0_fun/pallas_call | solution.py:320
  33.1 14.4 %all_to_all.26 = f32[8,8,128]{2,1,0:T(8,128)S(1)} all-to-all(f32[8,8,128]{2,1,0:T(8,128)S(1)} %get-tuple-element.55), channel_id=1, replica_groups=mesh['z'=8,'y'=4,'x'=4,'c'=2] {'z'}, dimensions={0} | all-to-all | bytes 65536 | tf_op jit(solution)/shard_map/cond/branch_0_fun/all_to_all | solution.py:273
  47.5 0.2 collective-permute-start.2
  47.7 1.1 %collective-permute-done.2 = f32[8,128]{1,0:T(8,128)S(1)} collective-permute-done((f32[8,128]{1,0:T(8,128)S(1)}, f32[8,128]{1,0:T(8,128)S(1)}, u32[]{:S(2)}, u32[]{:S(2)}) %collective-permute-start.2) | collective-permute-done | bytes 4128 | tf_op jit(solution)/shard_map/ppermute | solution.py:277
  48.8 21.4 %conditional.5 = ((f32[32,768]{1,0:T(8,128)S(1)}, f32[40,768]{1,0:T(8,128)S(1)}, f32[8,128]{1,0:T(8,128)S(1)})) conditional(s32[]{:T(128)} %convert_element_type.4, (bf16[16,400,128]{2,1,0:T(8,128)(2,1)S(1)}, bf16[16,400,128]{2,1,0:T(8,128)(2,1)S(1)}, f32[8,128]{1,0:T(8,128)S(1)}, f32[8,128]{1,0:T(8,128)S(1)}, f32[8,128]{1,0:T(8,128)S(1)}, ...), branch_computations={%region_6.7_spmd, %region_7.8_spmd} | conditional | bytes 3276808 | solution.py:346
  48.8 1.6 %branch_0_fun.6 = s16[8,400,128]{2,1,0:T(8,128)(2,1)S(1)} custom-call(bf16[16,400,128]{2,1,0:T(8,128)(2,1)S(1)} %get-tuple-element.63.y_ref, bf16[16,400,128]{2,1,0:T(8,128)(2,1)S(1)} %get-tuple-element.64.e_ref, f32[8,128]{1,0:T(8,128)S(1)} %get-tuple-element.65.match_ref, f32[8,128]{1,0:T(8,128)S(1)} %get-tuple-element.66.mine_ref, ...), custom_call_target="tpu_custom_call" | custom-call | tf_op jit(solution)/shard_map/cond/branch_0_fun/pallas_call | solution.py:337
  50.4 19.4 %all_to_all.28.parts = s16[8,400,128]{2,1,0:T(8,128)(2,1)S(1)} all-to-all(s16[8,400,128]{2,1,0:T(8,128)(2,1)S(1)} %branch_0_fun.6), channel_id=1, replica_groups=mesh['z'=8,'y'=4,'x'=4,'c'=2] {'z'}, dimensions={0} | all-to-all | bytes 1638400 | tf_op jit(solution)/shard_map/cond/branch_0_fun/all_to_all | solution.py:273
  69.8 0.3 branch_0_fun.7
  70.2 0.8 %collective-permute-start.3 = (f32[40,768]{1,0:T(8,128)S(1)}, f32[40,768]{1,0:T(8,128)S(1)}, u32[]{:S(2)}, u32[]{:S(2)}) collective-permute-start(f32[40,768]{1,0:T(8,128)S(1)} %get-tuple-element.96), channel_id=1, source_target_pairs={{0,1},{1,0},{2,3},{3,2},{4,5},{5,4},{6,7},{7,6},{8,9},{9,8},{10,11... | collective-permute-start | bytes 368648 | tf_op jit(solution)/shard_map/ppermute | solution.py:277
  71.0 1.0 %collective-permute-done.3.recv_ref = f32[40,768]{1,0:T(8,128)S(1)} collective-permute-done((f32[40,768]{1,0:T(8,128)S(1)}, f32[40,768]{1,0:T(8,128)S(1)}, u32[]{:S(2)}, u32[]{:S(2)}) %collective-permute-start.3) | collective-permute-done | bytes 122912 | tf_op jit(solution)/shard_map/ppermute | solution.py:277
  72.0 0.7 shard_map.59
  (1 shorter events, 0.0 us)
Async XLA Ops:
  1.6 4.2 %collective-permute-start = (bf16[48,768]{1,0:T(8,128)(2,1)S(1)}, bf16[48,768]{1,0:T(8,128)(2,1)S(1)}, u32[]{:S(2)}, u32[]{:S(2)}) collective-permute-start(bf16[48,768]{1,0:T(8,128)(2,1)S(1)} %get-tuple-element.89), channel_id=1, source_target_pairs={{0,1},{1,0},{2,3},{3,2},{4,5},{5,4},{6,7},{7,6},{8,9},{9,8},{10,11... | collective-permute-start | bytes 221192 | tf_op jit(solution)/shard_map/ppermute | solution.py:277
  27.7 3.6 %collective-permute-start.1 = (bf16[16,400,128]{2,1,0:T(8,128)(2,1)S(1)}, bf16[16,400,128]{2,1,0:T(8,128)(2,1)S(1)}, u32[]{:S(2)}, u32[]{:S(2)}) collective-permute-start(bf16[16,400,128]{2,1,0:T(8,128)(2,1)S(1)} %get-tuple-element.112), channel_id=1, source_target_pairs={{0,1},{1,0},{2,3},{3,2},{4,5},{5,4},{6,7},{7,6},{8,9},{9,8},{10,11... | collective-permute-start | bytes 4915208 | tf_op jit(solution)/shard_map/ppermute | solution.py:277
  47.5 1.2 %collective-permute-start.2 = (f32[8,128]{1,0:T(8,128)S(1)}, f32[8,128]{1,0:T(8,128)S(1)}, u32[]{:S(2)}, u32[]{:S(2)}) collective-permute-start(f32[8,128]{1,0:T(8,128)S(1)} %get-tuple-element.93), channel_id=1, source_target_pairs={{0,1},{1,0},{2,3},{3,2},{4,5},{5,4},{6,7},{7,6},{8,9},{9,8},{10,11... | collective-permute-start | bytes 12296 | tf_op jit(solution)/shard_map/ppermute | solution.py:277
  70.2 1.8 %collective-permute-start.3 = (f32[40,768]{1,0:T(8,128)S(1)}, f32[40,768]{1,0:T(8,128)S(1)}, u32[]{:S(2)}, u32[]{:S(2)}) collective-permute-start(f32[40,768]{1,0:T(8,128)S(1)} %get-tuple-element.96), channel_id=1, source_target_pairs={{0,1},{1,0},{2,3},{3,2},{4,5},{5,4},{6,7},{7,6},{8,9},{9,8},{10,11... | collective-permute-start | bytes 368648 | tf_op jit(solution)/shard_map/ppermute | solution.py:277

commit v5 on v4

--- a/solution.py
+++ b/solution.py
@@ -53,7 +53,7 @@
     most = jnp.max(jnp.abs(value), axis=0, keepdims=True)
     t = jnp.ceil(f32(8.0) * jnp.log2(jnp.maximum(most, f32(1e-30))) + f32(0.01))
     scaled = value * (f32(LEVELS) * jnp.exp2(t * f32(-0.125)))
-    return jnp.floor(scaled + f32(0.5)).astype(jnp.int32), t.astype(jnp.int32)
+    return jnp.round(scaled).astype(jnp.int32), t.astype(jnp.int32)
 
 
 def start_kernel(img_hbm, txt_hbm, partner_hbm, keep_ref, send_ref, img, txt, partner, sems):

time: 72.9 us -> 72.6 us (level)
  no operation moved by 1% of the time
where the time goes in v5:
time: 72.6 us; the launch traced here: 72.4 us
  blocking collectives  55.4 us (76%)
  waiting for transfers between devices  6.43 us (9%)
  Pallas kernels  5.4 us (7%)
  starting transfers between devices  4.32 us (6%)
    all_to_all x3, blocking collectives, exchange(): return lax.all_to_all(x, axes, 0, 0)  55.4 us
    ppermute x4, waiting for transfers between devices, swap(): return lax.ppermute(x, 'c', [(0, 1), (1, 0)])  6.43 us
    ppermute x4, starting transfers between devices, swap(): return lax.ppermute(x, 'c', [(0, 1), (1, 0)])  4.32 us
    pallas_call x1, Pallas kernels, sums(): call(functools.partial(scores_kernel, images, rows), [((n_plane, packed,...  1.81 us
    pallas_call x1, Pallas kernels, grads(): call(functools.partial(grads_kernel, images, rows), [((count, packed, 128...  1.47 us
  transfers between devices with their start and end apart: 4, of which 4 were waited for; matrix products, arithmetic and copies ran while one was open for 0% of the time, Pallas kernels for 0%

profile of v5, /device:TPU:1, one launch (start us, length us, event | category | flops | bytes accessed | tf_op | source)
XLA Modules:
  0.0 72.4 jit_solution(6875431624953243619)
XLA Ops:
  0.6 0.9 %shard_map.58 = (bf16[48,768]{1,0:T(8,128)(2,1)S(1)}, bf16[48,768]{1,0:T(8,128)(2,1)S(1)}) custom-call(bf16[32,768]{1,0:T(8,128)(2,1)} %img_hbm.1, bf16[32,768]{1,0:T(8,128)(2,1)} %txt_hbm.1, s32[1,32]{1,0:T(1,128)} %bitcast.2), custom_call_target="tpu_custom_call" | custom-call | tf_op jit(solution)/shard_map/pallas_call | solution.py:294
  1.6 3.3 %collective-permute-start = (bf16[48,768]{1,0:T(8,128)(2,1)S(1)}, bf16[48,768]{1,0:T(8,128)(2,1)S(1)}, u32[]{:S(2)}, u32[]{:S(2)}) collective-permute-start(bf16[48,768]{1,0:T(8,128)(2,1)S(1)} %get-tuple-element.89), channel_id=1, source_target_pairs={{0,1},{1,0},{2,3},{3,2},{4,5},{5,4},{6,7},{7,6},{8,9},{9,8},{10,11... | collective-permute-start | bytes 221192 | tf_op jit(solution)/shard_map/ppermute | solution.py:277
  4.9 0.9 %collective-permute-done = bf16[48,768]{1,0:T(8,128)(2,1)S(1)} collective-permute-done((bf16[48,768]{1,0:T(8,128)(2,1)S(1)}, bf16[48,768]{1,0:T(8,128)(2,1)S(1)}, u32[]{:S(2)}, u32[]{:S(2)}) %collective-permute-start) | collective-permute-done | bytes 73760 | tf_op jit(solution)/shard_map/ppermute | solution.py:277
  5.8 21.9 %conditional.3 = (bf16[16,400,128]{2,1,0:T(8,128)(2,1)S(1)}) conditional(s32[]{:T(128)} %convert_element_type.4, (bf16[48,768]{1,0:T(8,128)(2,1)S(1)}, bf16[48,768]{1,0:T(8,128)(2,1)S(1)}) %tuple.28, (bf16[48,768]{1,0:T(8,128)(2,1)S(1)}, bf16[48,768]{1,0:T(8,128)(2,1)S(1)}) %tuple.29), branch_computations={%region_0.1_spmd, %region_1.2_spmd} | conditional | bytes 4096010 | solution.py:316
  5.8 0.1 branch_0_fun.4
  6.0 21.6 %all_to_all.24 = bf16[8,400,128]{2,1,0:T(8,128)(2,1)S(1)} all-to-all(bf16[8,400,128]{2,1,0:T(8,128)(2,1)S(1)} %branch_0_fun.4), channel_id=1, replica_groups=mesh['z'=8,'y'=4,'x'=4,'c'=2] {'z'}, dimensions={0} | all-to-all | bytes 1638400 | tf_op jit(solution)/shard_map/cond/branch_0_fun/all_to_all | solution.py:273
  27.5 0.2 pad.3
  27.7 0.1 collective-permute-start.1
  27.8 3.5 %collective-permute-done.1 = bf16[16,400,128]{2,1,0:T(8,128)(2,1)S(1)} collective-permute-done((bf16[16,400,128]{2,1,0:T(8,128)(2,1)S(1)}, bf16[16,400,128]{2,1,0:T(8,128)(2,1)S(1)}, u32[]{:S(2)}, u32[]{:S(2)}) %collective-permute-start.1) | collective-permute-done | bytes 1638432 | tf_op jit(solution)/shard_map/ppermute | solution.py:277
  31.3 16.2 %conditional.4 = (bf16[16,400,128]{2,1,0:T(8,128)(2,1)S(1)}, f32[8,128]{1,0:T(8,128)S(1)}, f32[8,128]{1,0:T(8,128)S(1)}) conditional(s32[]{:T(128)} %convert_element_type.4, (bf16[16,400,128]{2,1,0:T(8,128)(2,1)S(1)}, bf16[16,400,128]{2,1,0:T(8,128)(2,1)S(1)}) %tuple.30, (bf16[16,400,128]{2,1,0:T(8,128)(2,1)S(1)}, ...), branch_computations={%region_2.4_spmd, %region_4.6_spmd} | conditional | flops 15360 | bytes 200732 | solution.py:329
  31.3 1.8 %branch_0_fun.5 = (bf16[16,400,128]{2,1,0:T(8,128)(2,1)S(1)}, f32[8,8,128]{2,1,0:T(8,128)S(1)}, f32[8,128]{1,0:T(8,128)S(1)}) custom-call(bf16[16,400,128]{2,1,0:T(8,128)(2,1)S(1)} %get-tuple-element.51.x_ref, bf16[16,400,128]{2,1,0:T(8,128)(2,1)S(1)} %get-tuple-element.52.y_ref), custom_call_target="tpu_custom_call", output_to_operand_aliasing={{0}: (0, {})} | custom-call | tf_op jit(solution)/shard_map/cond/branch_0_fun/pallas_call | solution.py:320
  33.1 14.4 %all_to_all.26 = f32[8,8,128]{2,1,0:T(8,128)S(1)} all-to-all(f32[8,8,128]{2,1,0:T(8,128)S(1)} %get-tuple-element.55), channel_id=1, replica_groups=mesh['z'=8,'y'=4,'x'=4,'c'=2] {'z'}, dimensions={0} | all-to-all | bytes 65536 | tf_op jit(solution)/shard_map/cond/branch_0_fun/all_to_all | solution.py:273
  47.5 0.2 collective-permute-start.2
  47.7 1.1 %collective-permute-done.2 = f32[8,128]{1,0:T(8,128)S(1)} collective-permute-done((f32[8,128]{1,0:T(8,128)S(1)}, f32[8,128]{1,0:T(8,128)S(1)}, u32[]{:S(2)}, u32[]{:S(2)}) %collective-permute-start.2) | collective-permute-done | bytes 4128 | tf_op jit(solution)/shard_map/ppermute | solution.py:277
  48.8 21.2 %conditional.5 = ((f32[32,768]{1,0:T(8,128)S(1)}, f32[40,768]{1,0:T(8,128)S(1)}, f32[8,128]{1,0:T(8,128)S(1)})) conditional(s32[]{:T(128)} %convert_element_type.4, (bf16[16,400,128]{2,1,0:T(8,128)(2,1)S(1)}, bf16[16,400,128]{2,1,0:T(8,128)(2,1)S(1)}, f32[8,128]{1,0:T(8,128)S(1)}, f32[8,128]{1,0:T(8,128)S(1)}, f32[8,128]{1,0:T(8,128)S(1)}, ...), branch_computations={%region_6.7_spmd, %region_7.8_spmd} | conditional | bytes 3276808 | solution.py:346
  48.8 1.5 %branch_0_fun.6 = s16[8,400,128]{2,1,0:T(8,128)(2,1)S(1)} custom-call(bf16[16,400,128]{2,1,0:T(8,128)(2,1)S(1)} %get-tuple-element.63.y_ref, bf16[16,400,128]{2,1,0:T(8,128)(2,1)S(1)} %get-tuple-element.64.e_ref, f32[8,128]{1,0:T(8,128)S(1)} %get-tuple-element.65.match_ref, f32[8,128]{1,0:T(8,128)S(1)} %get-tuple-element.66.mine_ref, ...), custom_call_target="tpu_custom_call" | custom-call | tf_op jit(solution)/shard_map/cond/branch_0_fun/pallas_call | solution.py:337
  50.2 19.4 %all_to_all.28.parts = s16[8,400,128]{2,1,0:T(8,128)(2,1)S(1)} all-to-all(s16[8,400,128]{2,1,0:T(8,128)(2,1)S(1)} %branch_0_fun.6), channel_id=1, replica_groups=mesh['z'=8,'y'=4,'x'=4,'c'=2] {'z'}, dimensions={0} | all-to-all | bytes 1638400 | tf_op jit(solution)/shard_map/cond/branch_0_fun/all_to_all | solution.py:273
  69.6 0.3 branch_0_fun.7
  70.0 0.7 collective-permute-start.3
  70.7 1.0 %collective-permute-done.3.recv_ref = f32[40,768]{1,0:T(8,128)S(1)} collective-permute-done((f32[40,768]{1,0:T(8,128)S(1)}, f32[40,768]{1,0:T(8,128)S(1)}, u32[]{:S(2)}, u32[]{:S(2)}) %collective-permute-start.3) | collective-permute-done | bytes 122912 | tf_op jit(solution)/shard_map/ppermute | solution.py:277
  71.7 0.7 shard_map.59
  (1 shorter events, 0.0 us)
Async XLA Ops:
  1.6 4.2 %collective-permute-start = (bf16[48,768]{1,0:T(8,128)(2,1)S(1)}, bf16[48,768]{1,0:T(8,128)(2,1)S(1)}, u32[]{:S(2)}, u32[]{:S(2)}) collective-permute-start(bf16[48,768]{1,0:T(8,128)(2,1)S(1)} %get-tuple-element.89), channel_id=1, source_target_pairs={{0,1},{1,0},{2,3},{3,2},{4,5},{5,4},{6,7},{7,6},{8,9},{9,8},{10,11... | collective-permute-start | bytes 221192 | tf_op jit(solution)/shard_map/ppermute | solution.py:277
  27.7 3.6 %collective-permute-start.1 = (bf16[16,400,128]{2,1,0:T(8,128)(2,1)S(1)}, bf16[16,400,128]{2,1,0:T(8,128)(2,1)S(1)}, u32[]{:S(2)}, u32[]{:S(2)}) collective-permute-start(bf16[16,400,128]{2,1,0:T(8,128)(2,1)S(1)} %get-tuple-element.112), channel_id=1, source_target_pairs={{0,1},{1,0},{2,3},{3,2},{4,5},{5,4},{6,7},{7,6},{8,9},{9,8},{10,11... | collective-permute-start | bytes 4915208 | tf_op jit(solution)/shard_map/ppermute | solution.py:277
  47.5 1.2 %collective-permute-start.2 = (f32[8,128]{1,0:T(8,128)S(1)}, f32[8,128]{1,0:T(8,128)S(1)}, u32[]{:S(2)}, u32[]{:S(2)}) collective-permute-start(f32[8,128]{1,0:T(8,128)S(1)} %get-tuple-element.93), channel_id=1, source_target_pairs={{0,1},{1,0},{2,3},{3,2},{4,5},{5,4},{6,7},{7,6},{8,9},{9,8},{10,11... | collective-permute-start | bytes 12296 | tf_op jit(solution)/shard_map/ppermute | solution.py:277
  70.0 1.7 %collective-permute-start.3 = (f32[40,768]{1,0:T(8,128)S(1)}, f32[40,768]{1,0:T(8,128)S(1)}, u32[]{:S(2)}, u32[]{:S(2)}) collective-permute-start(f32[40,768]{1,0:T(8,128)S(1)} %get-tuple-element.96), channel_id=1, source_target_pairs={{0,1},{1,0},{2,3},{3,2},{4,5},{5,4},{6,7},{7,6},{8,9},{9,8},{10,11... | collective-permute-start | bytes 368648 | tf_op jit(solution)/shard_map/ppermute | solution.py:277

commit v6 on v5

--- a/solution.py
+++ b/solution.py
@@ -198,6 +198,7 @@
     rest = [jnp.zeros((EXTRA - 2 - width // 128, 128), jnp.int32)]
     row_inv = f32(1.0) / mine_ref[:nx]
     y = unpack(y_ref, 0, ny * per, rows, width)
+    gs = []
     ds = []
     for r in range(nx):
         ri = jnp.broadcast_to(row_inv[r : r + 1], (128, 128)).T
@@ -210,11 +211,18 @@
             v = jnp.where(e < 0.0, matched * weight - f32(2.0), e * weight)
             d.append(v.astype(bf16))
         ds.append(jnp.concatenate(d, axis=1))
-    g = jnp.dot(jnp.concatenate(ds, axis=0), y, preferred_element_type=f32)
+        if (r + 1) % (nx // 2) == 0:
+            gs.append(jnp.dot(jnp.concatenate(ds, axis=0), y, preferred_element_type=f32))
+            ds = []
     for b in range(blocks):
         steps = []
         for k in range(width // 128):
-            q, t = encode(g[b * rows : (b + 1) * rows, k * 128 : (k + 1) * 128])
+            q, t = encode(
+                gs[b * 2 // blocks][
+                    b % (blocks // 2) * rows : (b % (blocks // 2) + 1) * rows,
+                    k * 128 : (k + 1) * 128,
+                ]
+            )
             out_ref[b, k * rows : (k + 1) * rows, :] = q.astype(jnp.int16)
             steps.append(t)
         tile = jnp.concatenate(steps + share + rest, axis=0)

time: 72.6 us -> 72.3 us (level)
  no operation moved by 1% of the time
where the time goes in v6:
time: 72.3 us; the launch traced here: 72 us
  blocking collectives  55.3 us (76%)
  waiting for transfers between devices  6.43 us (9%)
  Pallas kernels  5.12 us (7%)
  starting transfers between devices  4.32 us (6%)
    all_to_all x3, blocking collectives, exchange(): return lax.all_to_all(x, axes, 0, 0)  55.3 us
    ppermute x4, waiting for transfers between devices, swap(): return lax.ppermute(x, 'c', [(0, 1), (1, 0)])  6.43 us
    ppermute x4, starting transfers between devices, swap(): return lax.ppermute(x, 'c', [(0, 1), (1, 0)])  4.32 us
    pallas_call x1, Pallas kernels, sums(): call(functools.partial(scores_kernel, images, rows), [((n_plane, packed,...  1.81 us
  transfers between devices with their start and end apart: 4, of which 4 were waited for; matrix products, arithmetic and copies ran while one was open for 0% of the time, Pallas kernels for 0%

profile of v6, /device:TPU:1, one launch (start us, length us, event | category | flops | bytes accessed | tf_op | source)
XLA Modules:
  0.0 72.0 jit_solution(11843940657243541011)
XLA Ops:
  0.6 0.9 %shard_map.58 = (bf16[48,768]{1,0:T(8,128)(2,1)S(1)}, bf16[48,768]{1,0:T(8,128)(2,1)S(1)}) custom-call(bf16[32,768]{1,0:T(8,128)(2,1)} %img_hbm.1, bf16[32,768]{1,0:T(8,128)(2,1)} %txt_hbm.1, s32[1,32]{1,0:T(1,128)} %bitcast.2), custom_call_target="tpu_custom_call" | custom-call | tf_op jit(solution)/shard_map/pallas_call | solution.py:302
  1.6 3.3 %collective-permute-start = (bf16[48,768]{1,0:T(8,128)(2,1)S(1)}, bf16[48,768]{1,0:T(8,128)(2,1)S(1)}, u32[]{:S(2)}, u32[]{:S(2)}) collective-permute-start(bf16[48,768]{1,0:T(8,128)(2,1)S(1)} %get-tuple-element.89), channel_id=1, source_target_pairs={{0,1},{1,0},{2,3},{3,2},{4,5},{5,4},{6,7},{7,6},{8,9},{9,8},{10,11... | collective-permute-start | bytes 221192 | tf_op jit(solution)/shard_map/ppermute | solution.py:285
  4.9 0.9 %collective-permute-done = bf16[48,768]{1,0:T(8,128)(2,1)S(1)} collective-permute-done((bf16[48,768]{1,0:T(8,128)(2,1)S(1)}, bf16[48,768]{1,0:T(8,128)(2,1)S(1)}, u32[]{:S(2)}, u32[]{:S(2)}) %collective-permute-start) | collective-permute-done | bytes 73760 | tf_op jit(solution)/shard_map/ppermute | solution.py:285
  5.8 21.9 %conditional.3 = (bf16[16,400,128]{2,1,0:T(8,128)(2,1)S(1)}) conditional(s32[]{:T(128)} %convert_element_type.4, (bf16[48,768]{1,0:T(8,128)(2,1)S(1)}, bf16[48,768]{1,0:T(8,128)(2,1)S(1)}) %tuple.28, (bf16[48,768]{1,0:T(8,128)(2,1)S(1)}, bf16[48,768]{1,0:T(8,128)(2,1)S(1)}) %tuple.29), branch_computations={%region_0.1_spmd, %region_1.2_spmd} | conditional | bytes 4096010 | solution.py:324
  5.8 0.1 branch_0_fun.4
  6.0 21.6 %all_to_all.24 = bf16[8,400,128]{2,1,0:T(8,128)(2,1)S(1)} all-to-all(bf16[8,400,128]{2,1,0:T(8,128)(2,1)S(1)} %branch_0_fun.4), channel_id=1, replica_groups=mesh['z'=8,'y'=4,'x'=4,'c'=2] {'z'}, dimensions={0} | all-to-all | bytes 1638400 | tf_op jit(solution)/shard_map/cond/branch_0_fun/all_to_all | solution.py:281
  27.5 0.2 pad.3
  27.7 0.1 collective-permute-start.1
  27.8 3.5 %collective-permute-done.1 = bf16[16,400,128]{2,1,0:T(8,128)(2,1)S(1)} collective-permute-done((bf16[16,400,128]{2,1,0:T(8,128)(2,1)S(1)}, bf16[16,400,128]{2,1,0:T(8,128)(2,1)S(1)}, u32[]{:S(2)}, u32[]{:S(2)}) %collective-permute-start.1) | collective-permute-done | bytes 1638432 | tf_op jit(solution)/shard_map/ppermute | solution.py:285
  31.3 16.2 %conditional.4 = (bf16[16,400,128]{2,1,0:T(8,128)(2,1)S(1)}, f32[8,128]{1,0:T(8,128)S(1)}, f32[8,128]{1,0:T(8,128)S(1)}) conditional(s32[]{:T(128)} %convert_element_type.4, (bf16[16,400,128]{2,1,0:T(8,128)(2,1)S(1)}, bf16[16,400,128]{2,1,0:T(8,128)(2,1)S(1)}) %tuple.30, (bf16[16,400,128]{2,1,0:T(8,128)(2,1)S(1)}, ...), branch_computations={%region_2.4_spmd, %region_4.6_spmd} | conditional | flops 15360 | bytes 200732 | solution.py:337
  31.3 1.8 %branch_0_fun.5 = (bf16[16,400,128]{2,1,0:T(8,128)(2,1)S(1)}, f32[8,8,128]{2,1,0:T(8,128)S(1)}, f32[8,128]{1,0:T(8,128)S(1)}) custom-call(bf16[16,400,128]{2,1,0:T(8,128)(2,1)S(1)} %get-tuple-element.51.x_ref, bf16[16,400,128]{2,1,0:T(8,128)(2,1)S(1)} %get-tuple-element.52.y_ref), custom_call_target="tpu_custom_call", output_to_operand_aliasing={{0}: (0, {})} | custom-call | tf_op jit(solution)/shard_map/cond/branch_0_fun/pallas_call | solution.py:328
  33.1 14.4 %all_to_all.26 = f32[8,8,128]{2,1,0:T(8,128)S(1)} all-to-all(f32[8,8,128]{2,1,0:T(8,128)S(1)} %get-tuple-element.55), channel_id=1, replica_groups=mesh['z'=8,'y'=4,'x'=4,'c'=2] {'z'}, dimensions={0} | all-to-all | bytes 65536 | tf_op jit(solution)/shard_map/cond/branch_0_fun/all_to_all | solution.py:281
  47.5 0.2 collective-permute-start.2
  47.7 1.1 %collective-permute-done.2 = f32[8,128]{1,0:T(8,128)S(1)} collective-permute-done((f32[8,128]{1,0:T(8,128)S(1)}, f32[8,128]{1,0:T(8,128)S(1)}, u32[]{:S(2)}, u32[]{:S(2)}) %collective-permute-start.2) | collective-permute-done | bytes 4128 | tf_op jit(solution)/shard_map/ppermute | solution.py:285
  48.8 20.9 %conditional.5 = ((f32[32,768]{1,0:T(8,128)S(1)}, f32[40,768]{1,0:T(8,128)S(1)}, f32[8,128]{1,0:T(8,128)S(1)})) conditional(s32[]{:T(128)} %convert_element_type.4, (bf16[16,400,128]{2,1,0:T(8,128)(2,1)S(1)}, bf16[16,400,128]{2,1,0:T(8,128)(2,1)S(1)}, f32[8,128]{1,0:T(8,128)S(1)}, f32[8,128]{1,0:T(8,128)S(1)}, f32[8,128]{1,0:T(8,128)S(1)}, ...), branch_computations={%region_6.7_spmd, %region_7.8_spmd} | conditional | bytes 3276808 | solution.py:354
  48.8 1.2 %branch_0_fun.6 = s16[8,400,128]{2,1,0:T(8,128)(2,1)S(1)} custom-call(bf16[16,400,128]{2,1,0:T(8,128)(2,1)S(1)} %get-tuple-element.63.y_ref, bf16[16,400,128]{2,1,0:T(8,128)(2,1)S(1)} %get-tuple-element.64.e_ref, f32[8,128]{1,0:T(8,128)S(1)} %get-tuple-element.65.match_ref, f32[8,128]{1,0:T(8,128)S(1)} %get-tuple-element.66.mine_ref, ...), custom_call_target="tpu_custom_call" | custom-call | tf_op jit(solution)/shard_map/cond/branch_0_fun/pallas_call | solution.py:345
  49.9 19.4 %all_to_all.28.parts = s16[8,400,128]{2,1,0:T(8,128)(2,1)S(1)} all-to-all(s16[8,400,128]{2,1,0:T(8,128)(2,1)S(1)} %branch_0_fun.6), channel_id=1, replica_groups=mesh['z'=8,'y'=4,'x'=4,'c'=2] {'z'}, dimensions={0} | all-to-all | bytes 1638400 | tf_op jit(solution)/shard_map/cond/branch_0_fun/all_to_all | solution.py:281
  69.3 0.3 branch_0_fun.7
  69.7 0.7 collective-permute-start.3
  70.4 1.0 %collective-permute-done.3.recv_ref = f32[40,768]{1,0:T(8,128)S(1)} collective-permute-done((f32[40,768]{1,0:T(8,128)S(1)}, f32[40,768]{1,0:T(8,128)S(1)}, u32[]{:S(2)}, u32[]{:S(2)}) %collective-permute-start.3) | collective-permute-done | bytes 122912 | tf_op jit(solution)/shard_map/ppermute | solution.py:285
  71.3 0.7 shard_map.59
  (1 shorter events, 0.0 us)
Async XLA Ops:
  1.6 4.2 %collective-permute-start = (bf16[48,768]{1,0:T(8,128)(2,1)S(1)}, bf16[48,768]{1,0:T(8,128)(2,1)S(1)}, u32[]{:S(2)}, u32[]{:S(2)}) collective-permute-start(bf16[48,768]{1,0:T(8,128)(2,1)S(1)} %get-tuple-element.89), channel_id=1, source_target_pairs={{0,1},{1,0},{2,3},{3,2},{4,5},{5,4},{6,7},{7,6},{8,9},{9,8},{10,11... | collective-permute-start | bytes 221192 | tf_op jit(solution)/shard_map/ppermute | solution.py:285
  27.7 3.6 %collective-permute-start.1 = (bf16[16,400,128]{2,1,0:T(8,128)(2,1)S(1)}, bf16[16,400,128]{2,1,0:T(8,128)(2,1)S(1)}, u32[]{:S(2)}, u32[]{:S(2)}) collective-permute-start(bf16[16,400,128]{2,1,0:T(8,128)(2,1)S(1)} %get-tuple-element.112), channel_id=1, source_target_pairs={{0,1},{1,0},{2,3},{3,2},{4,5},{5,4},{6,7},{7,6},{8,9},{9,8},{10,11... | collective-permute-start | bytes 4915208 | tf_op jit(solution)/shard_map/ppermute | solution.py:285
  47.5 1.2 %collective-permute-start.2 = (f32[8,128]{1,0:T(8,128)S(1)}, f32[8,128]{1,0:T(8,128)S(1)}, u32[]{:S(2)}, u32[]{:S(2)}) collective-permute-start(f32[8,128]{1,0:T(8,128)S(1)} %get-tuple-element.93), channel_id=1, source_target_pairs={{0,1},{1,0},{2,3},{3,2},{4,5},{5,4},{6,7},{7,6},{8,9},{9,8},{10,11... | collective-permute-start | bytes 12296 | tf_op jit(solution)/shard_map/ppermute | solution.py:285
  69.7 1.7 %collective-permute-start.3 = (f32[40,768]{1,0:T(8,128)S(1)}, f32[40,768]{1,0:T(8,128)S(1)}, u32[]{:S(2)}, u32[]{:S(2)}) collective-permute-start(f32[40,768]{1,0:T(8,128)S(1)} %get-tuple-element.96), channel_id=1, source_target_pairs={{0,1},{1,0},{2,3},{3,2},{4,5},{5,4},{6,7},{7,6},{8,9},{9,8},{10,11... | collective-permute-start | bytes 368648 | tf_op jit(solution)/shard_map/ppermute | solution.py:285

commit v7 on v6

--- a/solution.py
+++ b/solution.py
@@ -101,7 +101,28 @@
     return half * (per_half // 2) + tile // 2, slice(tile % 2 * 128, tile % 2 * 128 + 128)
 
 
-def scores_kernel(images, rows, x_ref, y_ref, e_ref, pay_ref, match_ref, *scratch):
+def image_sums_kernel(rows, x_ref, y_ref, pay_ref, sums_ref):
+    packed = x_ref.shape[1]
+    width = (packed - EXTRA) // rows * 128
+    texts = x_ref.shape[0] // 2
+    x = unpack(x_ref, 0, x_ref.shape[0], rows, width)
+    y = unpack(y_ref, 0, texts, rows, width)
+    scores = lax.dot_general(x, y, NT, preferred_element_type=f32)
+    for r in range(x.shape[0] // 128):
+        lanes = jnp.zeros((128, 128), f32)
+        for t in range(y.shape[0] // 128):
+            s = scores[r * 128 : (r + 1) * 128, t * 128 : (t + 1) * 128]
+            lanes += jnp.exp2(s * f32(sharpness * math.log2(math.e)))
+        sums_ref[r : r + 1] = jnp.sum(lanes.T, axis=0, keepdims=True)
+    for b in range(pay_ref.shape[0]):
+        pay_ref[b] = sums_ref[...]
+
+
+def scores_kernel(images, rows, x_ref, y_ref, *refs):
+    if images:
+        unused, e_ref, match_ref, *scratch = refs
+    else:
+        e_ref, pay_ref, match_ref, *scratch = refs
     packed = x_ref.shape[1]
     width = (packed - EXTRA) // rows * 128
     per, half = 128 // rows, rows // 2
@@ -150,11 +171,13 @@
             for t in range(ny):
                 e = jnp.exp2(s_refs[h][(r - h * part) * ny + t] * f32(sharpness * math.log2(math.e)))
                 matched = jnp.where(own == ys_ref[t : t + 1], e, f32(0.0))
-                lanes += e
+                if not images:
+                    lanes += e
                 found += matched
                 block, at = place(images, nx * ny, r, t, ny)
                 e_ref[block, at] = (e - f32(2.0) * matched).astype(bf16)
-            pay_ref[0, r : r + 1] = jnp.sum(lanes.T, axis=0, keepdims=True)
+            if not images:
+                pay_ref[0, r : r + 1] = jnp.sum(lanes.T, axis=0, keepdims=True)
             match_ref[r : r + 1] = jnp.sum(found.T, axis=0, keepdims=True)
 
     once = jnp.minimum(lax.axis_index("c") + 1, 1)
@@ -177,8 +200,8 @@
         logs = jnp.sum(jnp.sum(logs, axis=0, keepdims=True), axis=1, keepdims=True)
         pay_ref[0, nx:] = jnp.broadcast_to(logs, (8 - nx, 128))
         match_ref[nx:] = jnp.zeros((8 - nx, 128), f32)
-    for b in range(1, pay_ref.shape[0]):
-        pay_ref[b] = pay_ref[0]
+        for b in range(1, pay_ref.shape[0]):
+            pay_ref[b] = pay_ref[0]
 
 
 def grads_kernel(images, rows, y_ref, e_ref, match_ref, mine_ref, other_ref, out_ref):
@@ -324,21 +347,35 @@
     x = lax.cond(image_core, gather_images, gather_texts)
     y = swap(x)
 
-    def sums(images, count, axes):
+    tile_kw = dict(
+        input_output_aliases={0: 0},
+        scratch_shapes=[pltpu.VMEM((8, 128), f32)] * 2
+        + [pltpu.VMEM((tiles // 2, 128, 128), f32)] * 2,
+    )
+    e_out = ((n_plane, packed, 128), bf16)
+
+    def image_sums():
+        pay, own_sums = call(
+            functools.partial(image_sums_kernel, rows),
+            [((n_plane, 8, 128), f32), ((8, 128), f32)],
+        )(x, y)
+        every = exchange(pay, PLANE)
+        e, match = call(
+            functools.partial(scores_kernel, True, rows),
+            [e_out, ((8, 128), f32)],
+            **tile_kw,
+        )(x, y, own_sums)
+        return e, match, jnp.sum(every, axis=0)
+
+    def text_sums():
         e, pay, match = call(
-            functools.partial(scores_kernel, images, rows),
-            [((n_plane, packed, 128), bf16), ((count, 8, 128), f32), ((8, 128), f32)],
-            input_output_aliases={0: 0},
-            scratch_shapes=[pltpu.VMEM((8, 128), f32)] * 2
-            + [pltpu.VMEM((tiles // 2, 128, 128), f32)] * 2,
+            functools.partial(scores_kernel, False, rows),
+            [e_out, ((n_line, 8, 128), f32), ((8, 128), f32)],
+            **tile_kw,
         )(x, y)
-        return e, match, jnp.sum(exchange(pay, axes), axis=0)
-
-    e, match, mine = lax.cond(
-        image_core,
-        functools.partial(sums, True, n_plane, PLANE),
-        functools.partial(sums, False, n_line, LINE),
-    )
+        return e, match, jnp.sum(exchange(pay, LINE), axis=0)
+
+    e, match, mine = lax.cond(image_core, image_sums, text_sums)
     other = swap(mine)
 
     def grads(images, count, axes):

time: 72.3 us -> 72.6 us (level)
  no operation moved by 1% of the time
where the time goes in v7:
time: 72.6 us; the launch traced here: 72.3 us
  blocking collectives  55.5 us (76%)
  waiting for transfers between devices  6.2 us (9%)
  Pallas kernels  5.17 us (7%)
  starting transfers between devices  4.6 us (6%)
    all_to_all x3, blocking collectives, exchange(): return lax.all_to_all(x, axes, 0, 0)  55.5 us
    ppermute x4, waiting for transfers between devices, swap(): return lax.ppermute(x, 'c', [(0, 1), (1, 0)])  6.2 us
    ppermute x4, starting transfers between devices, swap(): return lax.ppermute(x, 'c', [(0, 1), (1, 0)])  4.6 us
    pallas_call x1, Pallas kernels, text_sums(): call(functools.partial(scores_kernel, False, rows), [e_out, ((n_line, 8,...  1.82 us
  transfers between devices with their start and end apart: 4, of which 4 were waited for; matrix products, arithmetic and copies ran while one was open for 0% of the time, Pallas kernels for 0%

profile of v7, /device:TPU:1, one launch (start us, length us, event | category | flops | bytes accessed | tf_op | source)
XLA Modules:
  0.0 72.3 jit_solution(14710391261616679687)
XLA Ops:
  0.6 0.9 %shard_map.58 = (bf16[48,768]{1,0:T(8,128)(2,1)S(1)}, bf16[48,768]{1,0:T(8,128)(2,1)S(1)}) custom-call(bf16[32,768]{1,0:T(8,128)(2,1)} %img_hbm.1, bf16[32,768]{1,0:T(8,128)(2,1)} %txt_hbm.1, s32[1,32]{1,0:T(1,128)} %bitcast.2), custom_call_target="tpu_custom_call" | custom-call | tf_op jit(solution)/shard_map/pallas_call | solution.py:325
  1.6 3.3 %collective-permute-start = (bf16[48,768]{1,0:T(8,128)(2,1)S(1)}, bf16[48,768]{1,0:T(8,128)(2,1)S(1)}, u32[]{:S(2)}, u32[]{:S(2)}) collective-permute-start(bf16[48,768]{1,0:T(8,128)(2,1)S(1)} %get-tuple-element.90), channel_id=1, source_target_pairs={{0,1},{1,0},{2,3},{3,2},{4,5},{5,4},{6,7},{7,6},{8,9},{9,8},{10,11... | collective-permute-start | bytes 221192 | tf_op jit(solution)/shard_map/ppermute | solution.py:308
  4.9 0.9 %collective-permute-done = bf16[48,768]{1,0:T(8,128)(2,1)S(1)} collective-permute-done((bf16[48,768]{1,0:T(8,128)(2,1)S(1)}, bf16[48,768]{1,0:T(8,128)(2,1)S(1)}, u32[]{:S(2)}, u32[]{:S(2)}) %collective-permute-start) | collective-permute-done | bytes 73760 | tf_op jit(solution)/shard_map/ppermute | solution.py:308
  5.8 21.9 %conditional.3 = (bf16[16,400,128]{2,1,0:T(8,128)(2,1)S(1)}) conditional(s32[]{:T(128)} %convert_element_type.4, (bf16[48,768]{1,0:T(8,128)(2,1)S(1)}, bf16[48,768]{1,0:T(8,128)(2,1)S(1)}) %tuple.28, (bf16[48,768]{1,0:T(8,128)(2,1)S(1)}, bf16[48,768]{1,0:T(8,128)(2,1)S(1)}) %tuple.29), branch_computations={%region_0.1_spmd, %region_1.2_spmd} | conditional | bytes 4096010 | solution.py:347
  5.8 0.1 branch_0_fun.4
  6.0 21.6 %all_to_all.24 = bf16[8,400,128]{2,1,0:T(8,128)(2,1)S(1)} all-to-all(bf16[8,400,128]{2,1,0:T(8,128)(2,1)S(1)} %branch_0_fun.4), channel_id=1, replica_groups=mesh['z'=8,'y'=4,'x'=4,'c'=2] {'z'}, dimensions={0} | all-to-all | bytes 1638400 | tf_op jit(solution)/shard_map/cond/branch_0_fun/all_to_all | solution.py:304
  27.5 0.2 pad.3
  27.7 0.1 collective-permute-start.1
  27.8 3.5 %collective-permute-done.1 = bf16[16,400,128]{2,1,0:T(8,128)(2,1)S(1)} collective-permute-done((bf16[16,400,128]{2,1,0:T(8,128)(2,1)S(1)}, bf16[16,400,128]{2,1,0:T(8,128)(2,1)S(1)}, u32[]{:S(2)}, u32[]{:S(2)}) %collective-permute-start.1) | collective-permute-done | bytes 1638432 | tf_op jit(solution)/shard_map/ppermute | solution.py:308
  31.3 16.2 %conditional.4 = (bf16[16,400,128]{2,1,0:T(8,128)(2,1)S(1)}, f32[8,128]{1,0:T(8,128)S(1)}, f32[8,128]{1,0:T(8,128)S(1)}) conditional(s32[]{:T(128)} %convert_element_type.4, (bf16[16,400,128]{2,1,0:T(8,128)(2,1)S(1)}, bf16[16,400,128]{2,1,0:T(8,128)(2,1)S(1)}) %tuple.30, (bf16[16,400,128]{2,1,0:T(8,128)(2,1)S(1)}, ...), branch_computations={%region_2.4_spmd, %region_4.6_spmd} | conditional | flops 15360 | bytes 266300 | solution.py:378
  31.3 1.8 %branch_0_fun.5 = (bf16[16,400,128]{2,1,0:T(8,128)(2,1)S(1)}, f32[8,8,128]{2,1,0:T(8,128)S(1)}, f32[8,128]{1,0:T(8,128)S(1)}) custom-call(bf16[16,400,128]{2,1,0:T(8,128)(2,1)S(1)} %get-tuple-element.51.x_ref, bf16[16,400,128]{2,1,0:T(8,128)(2,1)S(1)} %get-tuple-element.52.y_ref), custom_call_target="tpu_custom_call", output_to_operand_aliasing={{0}: (0, {})} | custom-call | tf_op jit(solution)/shard_map/cond/branch_0_fun/pallas_call | solution.py:371
  33.1 14.4 %all_to_all.26 = f32[8,8,128]{2,1,0:T(8,128)S(1)} all-to-all(f32[8,8,128]{2,1,0:T(8,128)S(1)} %get-tuple-element.55), channel_id=1, replica_groups=mesh['z'=8,'y'=4,'x'=4,'c'=2] {'z'}, dimensions={0} | all-to-all | bytes 65536 | tf_op jit(solution)/shard_map/cond/branch_0_fun/all_to_all | solution.py:304
  47.5 0.5 collective-permute-start.2
  48.0 0.8 %collective-permute-done.2 = f32[8,128]{1,0:T(8,128)S(1)} collective-permute-done((f32[8,128]{1,0:T(8,128)S(1)}, f32[8,128]{1,0:T(8,128)S(1)}, u32[]{:S(2)}, u32[]{:S(2)}) %collective-permute-start.2) | collective-permute-done | bytes 4128 | tf_op jit(solution)/shard_map/ppermute | solution.py:308
  48.8 21.1 %conditional.5 = ((f32[32,768]{1,0:T(8,128)S(1)}, f32[40,768]{1,0:T(8,128)S(1)}, f32[8,128]{1,0:T(8,128)S(1)})) conditional(s32[]{:T(128)} %convert_element_type.4, (bf16[16,400,128]{2,1,0:T(8,128)(2,1)S(1)}, bf16[16,400,128]{2,1,0:T(8,128)(2,1)S(1)}, f32[8,128]{1,0:T(8,128)S(1)}, f32[8,128]{1,0:T(8,128)S(1)}, f32[8,128]{1,0:T(8,128)S(1)}, ...), branch_computations={%region_6.7_spmd, %region_7.8_spmd} | conditional | bytes 3276808 | solution.py:391
  48.8 1.2 %branch_0_fun.6 = s16[8,400,128]{2,1,0:T(8,128)(2,1)S(1)} custom-call(bf16[16,400,128]{2,1,0:T(8,128)(2,1)S(1)} %get-tuple-element.64.y_ref, bf16[16,400,128]{2,1,0:T(8,128)(2,1)S(1)} %get-tuple-element.65.e_ref, f32[8,128]{1,0:T(8,128)S(1)} %get-tuple-element.66.match_ref, f32[8,128]{1,0:T(8,128)S(1)} %get-tuple-element.67.mine_ref, ...), custom_call_target="tpu_custom_call" | custom-call | tf_op jit(solution)/shard_map/cond/branch_0_fun/pallas_call | solution.py:382
  50.0 19.5 %all_to_all.27.parts = s16[8,400,128]{2,1,0:T(8,128)(2,1)S(1)} all-to-all(s16[8,400,128]{2,1,0:T(8,128)(2,1)S(1)} %branch_0_fun.6), channel_id=1, replica_groups=mesh['z'=8,'y'=4,'x'=4,'c'=2] {'z'}, dimensions={0} | all-to-all | bytes 1638400 | tf_op jit(solution)/shard_map/cond/branch_0_fun/all_to_all | solution.py:304
  69.6 0.3 branch_0_fun.7
  69.9 0.7 collective-permute-start.3
  70.6 1.0 %collective-permute-done.3.recv_ref = f32[40,768]{1,0:T(8,128)S(1)} collective-permute-done((f32[40,768]{1,0:T(8,128)S(1)}, f32[40,768]{1,0:T(8,128)S(1)}, u32[]{:S(2)}, u32[]{:S(2)}) %collective-permute-start.3) | collective-permute-done | bytes 122912 | tf_op jit(solution)/shard_map/ppermute | solution.py:308
  71.6 0.7 shard_map.59
  (1 shorter events, 0.0 us)
Async XLA Ops:
  1.6 4.2 %collective-permute-start = (bf16[48,768]{1,0:T(8,128)(2,1)S(1)}, bf16[48,768]{1,0:T(8,128)(2,1)S(1)}, u32[]{:S(2)}, u32[]{:S(2)}) collective-permute-start(bf16[48,768]{1,0:T(8,128)(2,1)S(1)} %get-tuple-element.90), channel_id=1, source_target_pairs={{0,1},{1,0},{2,3},{3,2},{4,5},{5,4},{6,7},{7,6},{8,9},{9,8},{10,11... | collective-permute-start | bytes 221192 | tf_op jit(solution)/shard_map/ppermute | solution.py:308
  27.7 3.6 %collective-permute-start.1 = (bf16[16,400,128]{2,1,0:T(8,128)(2,1)S(1)}, bf16[16,400,128]{2,1,0:T(8,128)(2,1)S(1)}, u32[]{:S(2)}, u32[]{:S(2)}) collective-permute-start(bf16[16,400,128]{2,1,0:T(8,128)(2,1)S(1)} %get-tuple-element.113), channel_id=1, source_target_pairs={{0,1},{1,0},{2,3},{3,2},{4,5},{5,4},{6,7},{7,6},{8,9},{9,8},{10,11... | collective-permute-start | bytes 4915208 | tf_op jit(solution)/shard_map/ppermute | solution.py:308
  47.5 1.3 %collective-permute-start.2 = (f32[8,128]{1,0:T(8,128)S(1)}, f32[8,128]{1,0:T(8,128)S(1)}, u32[]{:S(2)}, u32[]{:S(2)}) collective-permute-start(f32[8,128]{1,0:T(8,128)S(1)} %get-tuple-element.94), channel_id=1, source_target_pairs={{0,1},{1,0},{2,3},{3,2},{4,5},{5,4},{6,7},{7,6},{8,9},{9,8},{10,11... | collective-permute-start | bytes 12296 | tf_op jit(solution)/shard_map/ppermute | solution.py:308
  69.9 1.7 %collective-permute-start.3 = (f32[40,768]{1,0:T(8,128)S(1)}, f32[40,768]{1,0:T(8,128)S(1)}, u32[]{:S(2)}, u32[]{:S(2)}) collective-permute-start(f32[40,768]{1,0:T(8,128)S(1)} %get-tuple-element.97), channel_id=1, source_target_pairs={{0,1},{1,0},{2,3},{3,2},{4,5},{5,4},{6,7},{7,6},{8,9},{9,8},{10,11... | collective-permute-start | bytes 368648 | tf_op jit(solution)/shard_map/ppermute | solution.py:308

commit v8 on v6

--- a/solution.py
+++ b/solution.py
@@ -93,27 +93,12 @@
         out[b, size:, :] = tile
 
 
-def place(images, tiles, r, t, ny):
-    per_half = tiles // 2
-    half, tile = divmod(r * ny + t, per_half)
-    if not images:
-        half = 1 - half
-    return half * (per_half // 2) + tile // 2, slice(tile % 2 * 128, tile % 2 * 128 + 128)
-
-
-def scores_kernel(images, rows, x_ref, y_ref, e_ref, pay_ref, match_ref, *scratch):
-    packed = x_ref.shape[1]
-    width = (packed - EXTRA) // rows * 128
+def vectors(rows, image_ref, texts):
     per, half = 128 // rows, rows // 2
-    texts = x_ref.shape[0] // 2
-    nx, ny = x_ref.shape[0] // per, y_ref.shape[0] // per
-    if images:
-        ny = texts // per
-    else:
-        nx = texts // per
+    packed = image_ref.shape[1]
     lane = lax.broadcasted_iota(jnp.int32, (1, 128), 1)
     chip = lax.axis_index("y") * lax.axis_size("x") + lax.axis_index("x")
-    tail = (x_ref if images else y_ref)[:, packed - EXTRA :, :].astype(f32)
+    tail = image_ref[:, packed - EXTRA :, :].astype(f32)
     partner = tail[:, 0, :] * 128.0 + tail[:, 1, :]
 
     def partners(t):
@@ -126,67 +111,104 @@
         i = (lane % rows) // half * (texts * half) + (per * t + lane // rows) * half
         return (chip * (texts * rows) + i + lane % half).astype(f32)
 
-    xs, ys = (partners, ids) if images else (ids, partners)
-    xs_ref, ys_ref, *s_refs = scratch
-    for r in range(nx):
+    return partners, ids
+
+
+def weigh(tiles, own, targets):
+    own = jnp.broadcast_to(own, (128, 128)).T
+    lanes = jnp.zeros((128, 128), f32)
+    found = jnp.zeros((128, 128), f32)
+    out = []
+    for s, target in zip(tiles, targets):
+        e = jnp.exp2(s * f32(sharpness * math.log2(math.e)))
+        matched = jnp.where(own == target, e, f32(0.0))
+        lanes += e
+        found += matched
+        out.append((e - f32(2.0) * matched).astype(bf16))
+    sums = jnp.sum(lanes.T, axis=0, keepdims=True)
+    return out, sums, jnp.sum(found.T, axis=0, keepdims=True)
+
+
+def first_kernel(rows, x_ref, y_ref, e_ref, sums_ref, match_ref):
+    blocks, packed, _ = x_ref.shape
+    width = (packed - EXTRA) // rows * 128
+    n = blocks * rows // 128
+    low = lax.axis_index("c") == 0
+    x_partners, ids = vectors(rows, x_ref, blocks)
+    y_partners, _ = vectors(rows, y_ref, blocks)
+    xs = [jnp.where(low, x_partners(r), ids(r)) for r in range(n)]
+    ys = [jnp.where(low, ids(t), y_partners(t)) for t in range(n)]
+    x = unpack(x_ref, 0, blocks, rows, width)
+    y = unpack(y_ref, 0, blocks, rows, width)
+    scores = lax.dot_general(x, y, NT, preferred_element_type=f32)
+    sums_ref[...] = jnp.zeros(sums_ref.shape, f32)
+    match_ref[...] = jnp.zeros(match_ref.shape, f32)
+    for r in range(n):
+        tiles = [scores[r * 128 : (r + 1) * 128, t * 128 : (t + 1) * 128] for t in range(n)]
+        out, total, matched = weigh(tiles, xs[r], ys)
+        for t in range(n):
+            e_ref[r * n + t] = out[t]
+        sums_ref[r : r + 1] = total
+        match_ref[r : r + 1] = matched
+
+
+def second_kernel(images, rows, free_ref, other_ref, sums_ref, matches_ref, *refs):
+    *own, e_ref, pay_ref, match_ref, xs_ref, ys_ref, s_ref = refs
+    blocks, packed, _ = free_ref.shape
+    width = (packed - EXTRA) // rows * 128
+    n = blocks * rows // 128
+    if images:
+        x_ref, y_ref = free_ref, other_ref
+        xs, ys = vectors(rows, x_ref, blocks)
+    else:
+        (x_ref,), y_ref = own, other_ref
+        ys, xs = vectors(rows, y_ref, blocks)
+    for r in range(n):
         xs_ref[r : r + 1] = xs(r)
-    for t in range(ny):
-        ys_ref[t : t + 1] = ys(t)
-    part = nx // 2
-
-    def product(h):
-        x = unpack(x_ref, h * part * per, part * per, rows, width)
-        y = unpack(y_ref, 0, ny * per, rows, width)
-        s = lax.dot_general(x, y, NT, preferred_element_type=f32)
-        for r in range(part):
-            for t in range(ny):
-                s_refs[h][r * ny + t] = s[r * 128 : (r + 1) * 128, t * 128 : (t + 1) * 128]
-
-    def weigh(h):
-        for r in range(h * part, (h + 1) * part):
-            own = jnp.broadcast_to(xs_ref[r : r + 1], (128, 128)).T
-            lanes = jnp.zeros((128, 128), f32)
-            found = jnp.zeros((128, 128), f32)
-            for t in range(ny):
-                e = jnp.exp2(s_refs[h][(r - h * part) * ny + t] * f32(sharpness * math.log2(math.e)))
-                matched = jnp.where(own == ys_ref[t : t + 1], e, f32(0.0))
-                lanes += e
-                found += matched
-                block, at = place(images, nx * ny, r, t, ny)
-                e_ref[block, at] = (e - f32(2.0) * matched).astype(bf16)
-            pay_ref[0, r : r + 1] = jnp.sum(lanes.T, axis=0, keepdims=True)
-            match_ref[r : r + 1] = jnp.sum(found.T, axis=0, keepdims=True)
-
-    once = jnp.minimum(lax.axis_index("c") + 1, 1)
-    product(0)
-
-    def first(i, carry):
-        product(1)
-        weigh(0)
+        ys_ref[r : r + 1] = ys(r)
+    x = unpack(x_ref, 0, blocks, rows, width)
+    y = unpack(y_ref, 0, blocks, rows, width)
+    scores = lax.dot_general(x, y, NT, preferred_element_type=f32)
+    for r in range(n):
+        for t in range(n):
+            s_ref[r * n + t] = scores[r * 128 : (r + 1) * 128, t * 128 : (t + 1) * 128]
+    pay_ref[0] = sums_ref[...]
+    match_ref[...] = matches_ref[...]
+
+    def turn(i, carry):
+        for r in range(n):
+            tiles = [s_ref[r * n + t] for t in range(n)]
+            targets = [ys_ref[t : t + 1] for t in range(n)]
+            out, total, matched = weigh(tiles, xs_ref[r : r + 1], targets)
+            for t in range(n):
+                tile = r * n + t
+                e_ref[tile // 2, tile % 2 * 128 : tile % 2 * 128 + 128] = out[t]
+            if images:
+                pay_ref[0, n + r : n + r + 1] = total
+                match_ref[n + r : n + r + 1] = matched
+            else:
+                pay_ref[0, r : r + 1] = sums_ref[r : r + 1] + total
+                match_ref[r : r + 1] = matches_ref[r : r + 1] + matched
         return carry
 
-    def second(i, carry):
-        weigh(1)
-        return carry
-
-    lax.fori_loop(0, once, first, 0)
-    lax.fori_loop(0, once, second, 0)
+    lax.fori_loop(0, jnp.minimum(lax.axis_index("c") + 1, 1), turn, 0)
     if not images:
-        m = match_ref[:nx]
+        m = match_ref[:n]
         logs = jnp.where(m > 0.0, jnp.log(jnp.where(m > 0.0, m, f32(1.0))), f32(0.0))
         logs = jnp.sum(jnp.sum(logs, axis=0, keepdims=True), axis=1, keepdims=True)
-        pay_ref[0, nx:] = jnp.broadcast_to(logs, (8 - nx, 128))
-        match_ref[nx:] = jnp.zeros((8 - nx, 128), f32)
+        pay_ref[0, n:] = jnp.broadcast_to(logs, (8 - n, 128))
     for b in range(1, pay_ref.shape[0]):
         pay_ref[b] = pay_ref[0]
 
 
-def grads_kernel(images, rows, y_ref, e_ref, match_ref, mine_ref, other_ref, out_ref):
+def grads_kernel(images, rows, first_ref, second_ref, match_ref, mine_ref, other_ref, *refs):
+    *y_refs, out_ref = refs
     blocks, packed, _ = out_ref.shape
     width = (packed - EXTRA) // rows * 128
     per = 128 // rows
     nx = blocks // per
-    ny = e_ref.shape[0] * 2 // nx
+    n = y_refs[0].shape[0] * rows // 128
+    ny = n * len(y_refs)
     col_total = other_ref[:ny]
     col_inv = f32(1.0) / col_total
     share = jnp.sum(jnp.log(col_total), axis=0, keepdims=True)
@@ -197,7 +219,8 @@
     share = [whole.astype(jnp.int32), ((share - whole) * f32(32768.0)).astype(jnp.int32)]
     rest = [jnp.zeros((EXTRA - 2 - width // 128, 128), jnp.int32)]
     row_inv = f32(1.0) / mine_ref[:nx]
-    y = unpack(y_ref, 0, ny * per, rows, width)
+    y = [unpack(ref, 0, ref.shape[0], rows, width) for ref in y_refs]
+    y = y[0] if images else jnp.concatenate(y, axis=0)
     gs = []
     ds = []
     for r in range(nx):
@@ -205,8 +228,11 @@
         matched = jnp.broadcast_to(match_ref[r : r + 1], (128, 128)).T
         d = []
         for t in range(ny):
-            block, at = place(images, nx * ny, r, t, ny)
-            e = e_ref[block, at].astype(f32)
+            tile = r % n * n + t % n
+            if r < n and t < n:
+                e = first_ref[tile].astype(f32)
+            else:
+                e = second_ref[tile // 2, tile % 2 * 128 : tile % 2 * 128 + 128].astype(f32)
             weight = ri + col_inv[t : t + 1]
             v = jnp.where(e < 0.0, matched * weight - f32(2.0), e * weight)
             d.append(v.astype(bf16))
@@ -271,7 +297,7 @@
 def call(kernel, outs, **kw):
     return pl.pallas_call(
         kernel,
-        out_shape=[jax.ShapeDtypeStruct(*o) for o in outs],
+        out_shape=[o if isinstance(o, pl.MemoryRef) else jax.ShapeDtypeStruct(*o) for o in outs],
         compiler_params=pltpu.CompilerParams(vmem_limit_bytes=48 * 1024 * 1024),
         **kw,
     )
@@ -314,27 +340,36 @@
 
     def gather_images():
         kernel = functools.partial(prep_kernel, True)
-        return exchange(call(kernel, [((n_plane, packed, 128), bf16)])(own, off)[0], PLANE)
+        every = exchange(call(kernel, [((n_plane, packed, 128), bf16)])(own, off)[0], PLANE)
+        return every[:n_line], every[n_line:]
 
     def gather_texts():
         kernel = functools.partial(prep_kernel, False)
         every = exchange(call(kernel, [((n_line, packed, 128), bf16)])(off, own)[0], LINE)
-        return jnp.pad(every, ((0, n_plane - n_line), (0, 0), (0, 0)))
-
-    x = lax.cond(image_core, gather_images, gather_texts)
-    y = swap(x)
+        return every, every
+
+    x1, x2 = lax.cond(image_core, gather_images, gather_texts)
+    y1, y2 = swap(x1), swap(x2)
+    e1, sums1, match1 = call(
+        functools.partial(first_kernel, rows),
+        [pltpu.VMEM((tiles // 2, 128, 128), bf16), ((8, 128), f32), ((8, 128), f32)],
+        cost_estimate=pl.CostEstimate(
+            flops=tiles * 128 * 128 * size, bytes_accessed=2 * x1.size, transcendentals=x1.size
+        ),
+    )(x1, y1)
 
     def sums(images, count, axes):
-        e, pay, match = call(
-            functools.partial(scores_kernel, images, rows),
-            [((n_plane, packed, 128), bf16), ((count, 8, 128), f32), ((8, 128), f32)],
+        arrays = (x2, y1, sums1, match1) if images else (x2, y2, sums1, match1, x1)
+        e2, pay, match = call(
+            functools.partial(second_kernel, images, rows),
+            [((n_line, packed, 128), bf16), ((count, 8, 128), f32), ((8, 128), f32)],
             input_output_aliases={0: 0},
             scratch_shapes=[pltpu.VMEM((8, 128), f32)] * 2
-            + [pltpu.VMEM((tiles // 2, 128, 128), f32)] * 2,
-        )(x, y)
-        return e, match, jnp.sum(exchange(pay, axes), axis=0)
-
-    e, match, mine = lax.cond(
+            + [pltpu.VMEM((tiles // 2, 128, 128), f32)],
+        )(*arrays)
+        return e2, match, jnp.sum(exchange(pay, axes), axis=0)
+
+    e2, match, mine = lax.cond(
         image_core,
         functools.partial(sums, True, n_plane, PLANE),
         functools.partial(sums, False, n_line, LINE),
@@ -345,7 +380,7 @@
         pay = call(
             functools.partial(grads_kernel, images, rows),
             [((count, packed, 128), jnp.int16)],
-        )(y, e, match, mine, other)[0]
+        )(e1, e2, match, mine, other, *([y1] if images else [y1, y2]))[0]
         return call(
             functools.partial(finish_kernel, sharpness / (2.0 * batch), images),
             [((half, size), f32), ((half + 8, size), f32), ((8, 128), f32)],

time: 72.3 us -> 73.1 us (1.011)
  Pallas kernels: 5.12 us -> 7.51 us
  waiting for transfers between devices: 6.43 us -> 5.34 us
  blocking collectives: 55.3 us -> 54.5 us
    pallas_call x1 -> x2, Pallas kernels: 1.81 us -> 3.06 us  [the longest x1 2.24 us: sums(): call(functools.partial(second_kernel, images, rows), [((n_line, packed, 1...]
    pallas_call x1, Pallas kernels: 1.19 us -> 2.33 us  [grads(): call(functools.partial(grads_kernel, images, rows), [((count, packed, 128...]
    ppermute x4 -> x5, waiting for transfers between devices: 6.43 us -> 5.34 us  [swap(): return lax.ppermute(x, 'c', [(0, 1), (1, 0)])]
    all_to_all x3, blocking collectives: 55.3 us -> 54.5 us  [exchange(): return lax.all_to_all(x, axes, 0, 0)]
    ppermute x4 -> x5, starting transfers between devices: 4.32 us -> 4.72 us  [swap(): return lax.ppermute(x, 'c', [(0, 1), (1, 0)])]
  transfers between devices with their start and end apart: 4 -> 5, of which waited for: 4 -> 5; matrix products, arithmetic and copies ran while one was open for 0% -> 0% of each run, Pallas kernels for 0% -> 1%
where the time goes in v8:
time: 73.1 us; the launch traced here: 72.8 us
  blocking collectives  54.5 us (75%)
  Pallas kernels  7.51 us (10%)
  waiting for transfers between devices  5.34 us (7%)
  starting transfers between devices  4.72 us (6%)
    all_to_all x3, blocking collectives, exchange(): return lax.all_to_all(x, axes, 0, 0)  54.5 us
    ppermute x5, waiting for transfers between devices, swap(): return lax.ppermute(x, 'c', [(0, 1), (1, 0)])  5.34 us
    ppermute x5, starting transfers between devices, swap(): return lax.ppermute(x, 'c', [(0, 1), (1, 0)])  4.72 us
    pallas_call x1, Pallas kernels, grads(): call(functools.partial(grads_kernel, images, rows), [((count, packed, 128...  2.33 us
    pallas_call x1, Pallas kernels, sums(): call(functools.partial(second_kernel, images, rows), [((n_line, packed, 1...  2.24 us
  transfers between devices with their start and end apart: 5, of which 5 were waited for; matrix products, arithmetic and copies ran while one was open for 0% of the time, Pallas kernels for 1%

profile of v8, /device:TPU:1, one launch (start us, length us, event | category | flops | bytes accessed | tf_op | source)
XLA Modules:
  0.0 72.8 jit_solution(16783736750299811741)
XLA Ops:
  0.6 0.9 %shard_map.58 = (bf16[48,768]{1,0:T(8,128)(2,1)S(1)}, bf16[48,768]{1,0:T(8,128)(2,1)S(1)}) custom-call(bf16[32,768]{1,0:T(8,128)(2,1)} %img_hbm.1, bf16[32,768]{1,0:T(8,128)(2,1)} %txt_hbm.1, s32[1,32]{1,0:T(1,128)} %bitcast.2), custom_call_target="tpu_custom_call" | custom-call | tf_op jit(solution)/shard_map/pallas_call | solution.py:328
  1.6 3.3 %collective-permute-start = (bf16[48,768]{1,0:T(8,128)(2,1)S(1)}, bf16[48,768]{1,0:T(8,128)(2,1)S(1)}, u32[]{:S(2)}, u32[]{:S(2)}) collective-permute-start(bf16[48,768]{1,0:T(8,128)(2,1)S(1)} %get-tuple-element.115), channel_id=1, source_target_pairs={{0,1},{1,0},{2,3},{3,2},{4,5},{5,4},{6,7},{7,6},{8,9},{9,8},{10,11... | collective-permute-start | bytes 221192 | tf_op jit(solution)/shard_map/ppermute | solution.py:311
  4.9 0.9 %collective-permute-done = bf16[48,768]{1,0:T(8,128)(2,1)S(1)} collective-permute-done((bf16[48,768]{1,0:T(8,128)(2,1)S(1)}, bf16[48,768]{1,0:T(8,128)(2,1)S(1)}, u32[]{:S(2)}, u32[]{:S(2)}) %collective-permute-start) | collective-permute-done | bytes 73760 | tf_op jit(solution)/shard_map/ppermute | solution.py:311
  5.8 21.8 %conditional.3 = (bf16[8,400,128]{2,1,0:T(8,128)(2,1)S(1)}, bf16[8,400,128]{2,1,0:T(8,128)(2,1)S(1)}) conditional(s32[]{:T(128)} %convert_element_type.2, (bf16[48,768]{1,0:T(8,128)(2,1)S(1)}, bf16[48,768]{1,0:T(8,128)(2,1)S(1)}) %tuple.30, (bf16[48,768]{1,0:T(8,128)(2,1)S(1)}, bf16[48,768]{1,0:T(8,128)(2,1)S(1)}) %tuple.31), branch_computations={%region_0.0_spmd, %region_1.0_spmd} | conditional | bytes 6553616 | solution.py:351
  5.8 0.1 branch_0_fun.4
  6.0 21.6 %all_to_all.24 = bf16[8,400,128]{2,1,0:T(8,128)(2,1)S(1)} all-to-all(bf16[8,400,128]{2,1,0:T(8,128)(2,1)S(1)} %branch_0_fun.4), channel_id=1, replica_groups=mesh['z'=8,'y'=4,'x'=4,'c'=2] {'z'}, dimensions={0} | all-to-all | bytes 1638400 | tf_op jit(solution)/shard_map/cond/branch_0_fun/all_to_all | solution.py:307
  27.5 0.1 copy.11
  27.6 0.3 collective-permute-start.1
  27.9 0.3 collective-permute-start.2
  28.2 1.8 %collective-permute-done.1.y_ref = bf16[8,400,128]{2,1,0:T(8,128)(2,1)S(1)} collective-permute-done((bf16[8,400,128]{2,1,0:T(8,128)(2,1)S(1)}, bf16[8,400,128]{2,1,0:T(8,128)(2,1)S(1)}, u32[]{:S(2)}, u32[]{:S(2)}) %collective-permute-start.1) | collective-permute-done | bytes 819232 | tf_op jit(solution)/shard_map/ppermute | solution.py:311
  30.0 0.8 %shard_map.59 = (bf16[16,128,128]{2,1,0:T(8,128)(2,1)S(1)}, f32[8,128]{1,0:T(8,128)S(1)}, f32[8,128]{1,0:T(8,128)S(1)}) custom-call(bf16[8,400,128]{2,1,0:T(8,128)(2,1)S(1)} %get-tuple-element.117.x_ref, bf16[8,400,128]{2,1,0:T(8,128)(2,1)S(1)} %collective-permute-done.1.y_ref), custom_call_target="tpu_custom_call" | custom-call | flops 402653184 | bytes 819200 | tf_op jit(solution)/shard_map/pallas_call | solution.py:353
  30.8 0.5 collective-permute-done.2
  31.3 17.0 %conditional.4 = (bf16[8,400,128]{2,1,0:T(8,128)(2,1)S(1)}, f32[8,128]{1,0:T(8,128)S(1)}, f32[8,128]{1,0:T(8,128)S(1)}) conditional(s32[]{:T(128)} %convert_element_type.2, (bf16[8,400,128]{2,1,0:T(8,128)(2,1)S(1)}, bf16[8,400,128]{2,1,0:T(8,128)(2,1)}, f32[8,128]{1,0:T(8,128)S(1)}, f32[8,128]{1,0:T(8,128)S(1)}, ...), branch_computations={%region_2.0_spmd, %region_4.0_spmd} | conditional | flops 15360 | bytes 200732 | solution.py:372
  31.3 2.2 %branch_0_fun.5 = (bf16[8,400,128]{2,1,0:T(8,128)(2,1)S(1)}, f32[8,8,128]{2,1,0:T(8,128)S(1)}, f32[8,128]{1,0:T(8,128)S(1)}) custom-call(bf16[8,400,128]{2,1,0:T(8,128)(2,1)S(1)} %get-tuple-element.64.free_ref, bf16[8,400,128]{2,1,0:T(8,128)(2,1)} %get-tuple-element.65.other_ref, ...), custom_call_target="tpu_custom_call", output_to_operand_aliasing={{0}: (0, {})} | custom-call | tf_op jit(solution)/shard_map/cond/branch_0_fun/pallas_call | solution.py:363
  33.5 14.7 %all_to_all.26 = f32[8,8,128]{2,1,0:T(8,128)S(1)} all-to-all(f32[8,8,128]{2,1,0:T(8,128)S(1)} %get-tuple-element.71), channel_id=1, replica_groups=mesh['z'=8,'y'=4,'x'=4,'c'=2] {'z'}, dimensions={0} | all-to-all | bytes 65536 | tf_op jit(solution)/shard_map/cond/branch_0_fun/all_to_all | solution.py:307
  48.3 0.1 collective-permute-start.3
  48.4 1.2 %collective-permute-done.3 = f32[8,128]{1,0:T(8,128)S(1)} collective-permute-done((f32[8,128]{1,0:T(8,128)S(1)}, f32[8,128]{1,0:T(8,128)S(1)}, u32[]{:S(2)}, u32[]{:S(2)}) %collective-permute-start.3) | collective-permute-done | bytes 4128 | tf_op jit(solution)/shard_map/ppermute | solution.py:311
  49.5 20.9 %conditional.5 = ((f32[32,768]{1,0:T(8,128)S(1)}, f32[40,768]{1,0:T(8,128)S(1)}, f32[8,128]{1,0:T(8,128)S(1)})) conditional(s32[]{:T(128)} %convert_element_type.2, (bf16[16,128,128]{2,1,0:T(8,128)(2,1)S(1)}, bf16[8,400,128]{2,1,0:T(8,128)(2,1)S(1)}, f32[8,128]{1,0:T(8,128)S(1)}, f32[8,128]{1,0:T(8,128)S(1)}, f32[8,128]{1,0:T(8,128)S(1)}, ...), branch_computations={%region_6.0_spmd, %region_7.0_spmd} | conditional | bytes 3276808 | solution.py:389
  49.5 2.3 %branch_0_fun.6 = s16[8,400,128]{2,1,0:T(8,128)(2,1)S(1)} custom-call(bf16[16,128,128]{2,1,0:T(8,128)(2,1)S(1)} %get-tuple-element.81.first_ref, bf16[8,400,128]{2,1,0:T(8,128)(2,1)S(1)} %get-tuple-element.82.second_ref, f32[8,128]{1,0:T(8,128)S(1)} %get-tuple-element.83.match_ref, f32[8,128]{1,0:T(8,128)S(1)} %get-tuple-element.84.mine_ref, ...), custom_call_target="tpu_custom_call" | custom-call | tf_op jit(solution)/shard_map/cond/branch_0_fun/pallas_call | solution.py:380
  51.9 18.2 %all_to_all.28.parts = s16[8,400,128]{2,1,0:T(8,128)(2,1)S(1)} all-to-all(s16[8,400,128]{2,1,0:T(8,128)(2,1)S(1)} %branch_0_fun.6), channel_id=1, replica_groups=mesh['z'=8,'y'=4,'x'=4,'c'=2] {'z'}, dimensions={0} | all-to-all | bytes 1638400 | tf_op jit(solution)/shard_map/cond/branch_0_fun/all_to_all | solution.py:307
  70.1 0.3 branch_0_fun.7
  70.4 0.7 collective-permute-start.4
  71.1 1.0 %collective-permute-done.4.recv_ref = f32[40,768]{1,0:T(8,128)S(1)} collective-permute-done((f32[40,768]{1,0:T(8,128)S(1)}, f32[40,768]{1,0:T(8,128)S(1)}, u32[]{:S(2)}, u32[]{:S(2)}) %collective-permute-start.4) | collective-permute-done | bytes 122912 | tf_op jit(solution)/shard_map/ppermute | solution.py:311
  72.1 0.7 shard_map.60
  (1 shorter events, 0.0 us)
Async XLA Ops:
  1.6 4.2 %collective-permute-start = (bf16[48,768]{1,0:T(8,128)(2,1)S(1)}, bf16[48,768]{1,0:T(8,128)(2,1)S(1)}, u32[]{:S(2)}, u32[]{:S(2)}) collective-permute-start(bf16[48,768]{1,0:T(8,128)(2,1)S(1)} %get-tuple-element.115), channel_id=1, source_target_pairs={{0,1},{1,0},{2,3},{3,2},{4,5},{5,4},{6,7},{7,6},{8,9},{9,8},{10,11... | collective-permute-start | bytes 221192 | tf_op jit(solution)/shard_map/ppermute | solution.py:311
  27.6 2.4 %collective-permute-start.1 = (bf16[8,400,128]{2,1,0:T(8,128)(2,1)S(1)}, bf16[8,400,128]{2,1,0:T(8,128)(2,1)S(1)}, u32[]{:S(2)}, u32[]{:S(2)}) collective-permute-start(bf16[8,400,128]{2,1,0:T(8,128)(2,1)S(1)} %get-tuple-element.117.x_ref), channel_id=1, source_target_pairs={{0,1},{1,0},{2,3},{3,2},{4,5},{5,4},{6,7},{7,6},{8,9},{9,8},{10,11... | collective-permute-start | bytes 2457608 | tf_op jit(solution)/shard_map/ppermute | solution.py:311
  27.9 3.4 %collective-permute-start.2 = (bf16[8,400,128]{2,1,0:T(8,128)(2,1)S(1)}, bf16[8,400,128]{2,1,0:T(8,128)(2,1)}, u32[]{:S(2)}, u32[]{:S(2)}) collective-permute-start(bf16[8,400,128]{2,1,0:T(8,128)(2,1)S(1)} %get-tuple-element.119), channel_id=1, source_target_pairs={{0,1},{1,0},{2,3},{3,2},{4,5},{5,4},{6,7},{7,6},{8,9},{9,8},{10,11... | collective-permute-start | bytes 2457608 | tf_op jit(solution)/shard_map/ppermute | solution.py:311
  48.3 1.2 %collective-permute-start.3 = (f32[8,128]{1,0:T(8,128)S(1)}, f32[8,128]{1,0:T(8,128)S(1)}, u32[]{:S(2)}, u32[]{:S(2)}) collective-permute-start(f32[8,128]{1,0:T(8,128)S(1)} %get-tuple-element.124), channel_id=1, source_target_pairs={{0,1},{1,0},{2,3},{3,2},{4,5},{5,4},{6,7},{7,6},{8,9},{9,8},{10,11... | collective-permute-start | bytes 12296 | tf_op jit(solution)/shard_map/ppermute | solution.py:311
  70.4 1.7 %collective-permute-start.4 = (f32[40,768]{1,0:T(8,128)S(1)}, f32[40,768]{1,0:T(8,128)S(1)}, u32[]{:S(2)}, u32[]{:S(2)}) collective-permute-start(f32[40,768]{1,0:T(8,128)S(1)} %get-tuple-element.127), channel_id=1, source_target_pairs={{0,1},{1,0},{2,3},{3,2},{4,5},{5,4},{6,7},{7,6},{8,9},{9,8},{10,11... | collective-permute-start | bytes 368648 | tf_op jit(solution)/shard_map/ppermute | solution.py:311

commit v9 on v8

--- a/solution.py
+++ b/solution.py
@@ -14,6 +14,7 @@
 NT = (((1,), (1,)), ((), ()))
 PLANE, LINE = ("y", "x"), "z"
 EXTRA = 16
+FIRST = 2
 
 
 def normalize(embed):
@@ -137,35 +138,43 @@
     x_partners, ids = vectors(rows, x_ref, blocks)
     y_partners, _ = vectors(rows, y_ref, blocks)
     xs = [jnp.where(low, x_partners(r), ids(r)) for r in range(n)]
-    ys = [jnp.where(low, ids(t), y_partners(t)) for t in range(n)]
+    ys = [jnp.where(low, ids(t), y_partners(t)) for t in range(FIRST)]
     x = unpack(x_ref, 0, blocks, rows, width)
-    y = unpack(y_ref, 0, blocks, rows, width)
+    y = unpack(y_ref, 0, FIRST * 128 // rows, rows, width)
     scores = lax.dot_general(x, y, NT, preferred_element_type=f32)
     sums_ref[...] = jnp.zeros(sums_ref.shape, f32)
     match_ref[...] = jnp.zeros(match_ref.shape, f32)
     for r in range(n):
-        tiles = [scores[r * 128 : (r + 1) * 128, t * 128 : (t + 1) * 128] for t in range(n)]
+        tiles = [scores[r * 128 : (r + 1) * 128, t * 128 : (t + 1) * 128] for t in range(FIRST)]
         out, total, matched = weigh(tiles, xs[r], ys)
-        for t in range(n):
-            e_ref[r * n + t] = out[t]
+        for t in range(FIRST):
+            e_ref[r * FIRST + t] = out[t]
         sums_ref[r : r + 1] = total
         match_ref[r : r + 1] = matched
 
 
-def second_kernel(images, rows, free_ref, other_ref, sums_ref, matches_ref, *refs):
-    *own, e_ref, pay_ref, match_ref, xs_ref, ys_ref, s_ref = refs
+def second_kernel(images, rows, free_ref, x1_ref, y1_ref, sums_ref, matches_ref, *refs):
+    *far, e_ref, pay_ref, match_ref, xs_ref, ys_ref, s_ref = refs
     blocks, packed, _ = free_ref.shape
     width = (packed - EXTRA) // rows * 128
     n = blocks * rows // 128
-    if images:
-        x_ref, y_ref = free_ref, other_ref
-        xs, ys = vectors(rows, x_ref, blocks)
-    else:
-        (x_ref,), y_ref = own, other_ref
-        ys, xs = vectors(rows, y_ref, blocks)
+    rest = n - FIRST
+    x_ref, y_ref = (free_ref, y1_ref) if images else (x1_ref, far[0])
+    partners, ids = vectors(rows, x1_ref if images else y1_ref, blocks)
+    far_partners, _ = vectors(rows, x_ref if images else y_ref, blocks)
+    near = (partners, ids) if images else (ids, partners)
+    xs, ys = (far_partners, ids) if images else (ids, far_partners)
     for r in range(n):
-        xs_ref[r : r + 1] = xs(r)
-        ys_ref[r : r + 1] = ys(r)
+        xs_ref[r : r + 1] = near[0](r)
+        xs_ref[n + r : n + r + 1] = xs(r)
+        ys_ref[r : r + 1] = near[1](r)
+        ys_ref[n + r : n + r + 1] = ys(r)
+    x = unpack(x1_ref, 0, blocks, rows, width)
+    y = unpack(y1_ref, FIRST * 128 // rows, rest * 128 // rows, rows, width)
+    scores = lax.dot_general(x, y, NT, preferred_element_type=f32)
+    for r in range(n):
+        for t in range(rest):
+            s_ref[n * n + r * rest + t] = scores[r * 128 : (r + 1) * 128, t * 128 : (t + 1) * 128]
     x = unpack(x_ref, 0, blocks, rows, width)
     y = unpack(y_ref, 0, blocks, rows, width)
     scores = lax.dot_general(x, y, NT, preferred_element_type=f32)
@@ -177,9 +186,17 @@
 
     def turn(i, carry):
         for r in range(n):
+            tiles = [s_ref[n * n + r * rest + t] for t in range(rest)]
+            targets = [ys_ref[FIRST + t : FIRST + t + 1] for t in range(rest)]
+            out, total, matched = weigh(tiles, xs_ref[r : r + 1], targets)
+            for t in range(rest):
+                e_ref[r * rest + t, 256:384] = out[t]
+            pay_ref[0, r : r + 1] = sums_ref[r : r + 1] + total
+            match_ref[r : r + 1] = matches_ref[r : r + 1] + matched
+        for r in range(n):
             tiles = [s_ref[r * n + t] for t in range(n)]
-            targets = [ys_ref[t : t + 1] for t in range(n)]
-            out, total, matched = weigh(tiles, xs_ref[r : r + 1], targets)
+            targets = [ys_ref[n + t : n + t + 1] for t in range(n)]
+            out, total, matched = weigh(tiles, xs_ref[n + r : n + r + 1], targets)
             for t in range(n):
                 tile = r * n + t
                 e_ref[tile // 2, tile % 2 * 128 : tile % 2 * 128 + 128] = out[t]
@@ -187,8 +204,8 @@
                 pay_ref[0, n + r : n + r + 1] = total
                 match_ref[n + r : n + r + 1] = matched
             else:
-                pay_ref[0, r : r + 1] = sums_ref[r : r + 1] + total
-                match_ref[r : r + 1] = matches_ref[r : r + 1] + matched
+                pay_ref[0, r : r + 1] = pay_ref[0, r : r + 1] + total
+                match_ref[r : r + 1] = match_ref[r : r + 1] + matched
         return carry
 
     lax.fori_loop(0, jnp.minimum(lax.axis_index("c") + 1, 1), turn, 0)
@@ -229,8 +246,10 @@
         d = []
         for t in range(ny):
             tile = r % n * n + t % n
-            if r < n and t < n:
-                e = first_ref[tile].astype(f32)
+            if r < n and t < FIRST:
+                e = first_ref[r * FIRST + t].astype(f32)
+            elif r < n and t < n:
+                e = second_ref[r * (n - FIRST) + t - FIRST, 256:384].astype(f32)
             else:
                 e = second_ref[tile // 2, tile % 2 * 128 : tile % 2 * 128 + 128].astype(f32)
             weight = ri + col_inv[t : t + 1]
@@ -352,20 +371,19 @@
     y1, y2 = swap(x1), swap(x2)
     e1, sums1, match1 = call(
         functools.partial(first_kernel, rows),
-        [pltpu.VMEM((tiles // 2, 128, 128), bf16), ((8, 128), f32), ((8, 128), f32)],
+        [pltpu.VMEM((tiles // 8 * FIRST, 128, 128), bf16), ((8, 128), f32), ((8, 128), f32)],
         cost_estimate=pl.CostEstimate(
             flops=tiles * 128 * 128 * size, bytes_accessed=2 * x1.size, transcendentals=x1.size
         ),
     )(x1, y1)
 
     def sums(images, count, axes):
-        arrays = (x2, y1, sums1, match1) if images else (x2, y2, sums1, match1, x1)
+        arrays = (x2, x1, y1, sums1, match1) if images else (x2, x1, y1, sums1, match1, y2)
         e2, pay, match = call(
             functools.partial(second_kernel, images, rows),
             [((n_line, packed, 128), bf16), ((count, 8, 128), f32), ((8, 128), f32)],
             input_output_aliases={0: 0},
-            scratch_shapes=[pltpu.VMEM((8, 128), f32)] * 2
-            + [pltpu.VMEM((tiles // 2, 128, 128), f32)],
+            scratch_shapes=[pltpu.VMEM((8, 128), f32)] * 2 + [pltpu.VMEM((tiles, 128, 128), f32)],
         )(*arrays)
         return e2, match, jnp.sum(exchange(pay, axes), axis=0)
 

time: 73.1 us -> 74.9 us (1.025)
  blocking collectives: 54.5 us -> 55.6 us
    all_to_all x3, blocking collectives: 54.5 us -> 55.6 us  [exchange(): return lax.all_to_all(x, axes, 0, 0)]
    pallas_call x1, Pallas kernels: 2.33 us -> 1.19 us  [grads(): call(functools.partial(grads_kernel, images, rows), [((count, packed, 128...]
    pallas_call x1, Pallas kernels: 0.15 us -> 1.07 us  [gather_texts(): call(kernel, [((n_line, packed, 128), bf16)])(off, own)[0]]
    pallas_call x1, Pallas kernels: 0.34 us -> 1.26 us  [grads(): call(functools.partial(finish_kernel, sharpness / (2.0 * batch), images),...]
where the time goes in v9:
time: 74.9 us; the launch traced here: 74.6 us
  blocking collectives  55.6 us (74%)
  Pallas kernels  7.86 us (10%)
  waiting for transfers between devices  5.64 us (8%)
  starting transfers between devices  4.72 us (6%)
    all_to_all x3, blocking collectives, exchange(): return lax.all_to_all(x, axes, 0, 0)  55.6 us
    ppermute x5, waiting for transfers between devices, swap(): return lax.ppermute(x, 'c', [(0, 1), (1, 0)])  5.64 us
    ppermute x5, starting transfers between devices, swap(): return lax.ppermute(x, 'c', [(0, 1), (1, 0)])  4.72 us
    pallas_call x1, Pallas kernels, local(): call(start_kernel, [((half + EXTRA, size), bf16)] * 2, in_specs=[pl.Block...  1.57 us
    pallas_call x1, Pallas kernels, sums(): call(functools.partial(second_kernel, images, rows), [((n_line, packed, 1...  1.56 us
  transfers between devices with their start and end apart: 5, of which 5 were waited for; matrix products, arithmetic and copies ran while one was open for 0% of the time, Pallas kernels for 1%

profile of v9, /device:TPU:1, one launch (start us, length us, event | category | flops | bytes accessed | tf_op | source)
XLA Modules:
  0.0 74.6 jit_solution(3464157203592464584)
XLA Ops:
  0.6 1.6 %shard_map.58 = (bf16[48,768]{1,0:T(8,128)(2,1)}, bf16[48,768]{1,0:T(8,128)(2,1)S(1)}) custom-call(bf16[32,768]{1,0:T(8,128)(2,1)} %img_hbm.1, bf16[32,768]{1,0:T(8,128)(2,1)} %txt_hbm.1, s32[1,32]{1,0:T(1,128)} %bitcast.2), custom_call_target="tpu_custom_call" | custom-call | tf_op jit(solution)/shard_map/pallas_call | solution.py:347
  2.2 3.3 %collective-permute-start = (bf16[48,768]{1,0:T(8,128)(2,1)S(1)}, bf16[48,768]{1,0:T(8,128)(2,1)}, u32[]{:S(2)}, u32[]{:S(2)}) collective-permute-start(bf16[48,768]{1,0:T(8,128)(2,1)S(1)} %get-tuple-element.121), channel_id=1, source_target_pairs={{0,1},{1,0},{2,3},{3,2},{4,5},{5,4},{6,7},{7,6},{8,9},{9,8},{10,11... | collective-permute-start | bytes 221192 | tf_op jit(solution)/shard_map/ppermute | solution.py:330
  5.5 1.0 %collective-permute-done = bf16[48,768]{1,0:T(8,128)(2,1)} collective-permute-done((bf16[48,768]{1,0:T(8,128)(2,1)S(1)}, bf16[48,768]{1,0:T(8,128)(2,1)}, u32[]{:S(2)}, u32[]{:S(2)}) %collective-permute-start) | collective-permute-done | bytes 73760 | tf_op jit(solution)/shard_map/ppermute | solution.py:330
  6.6 22.7 %conditional.3 = (bf16[8,400,128]{2,1,0:T(8,128)(2,1)S(1)}, bf16[8,400,128]{2,1,0:T(8,128)(2,1)S(1)}) conditional(s32[]{:T(128)} %convert_element_type.2, (bf16[48,768]{1,0:T(8,128)(2,1)}, bf16[48,768]{1,0:T(8,128)(2,1)}) %tuple.30, (bf16[48,768]{1,0:T(8,128)(2,1)}, bf16[48,768]{1,0:T(8,128)(2,1)}) %tuple.31), branch_computations={%region_0.0_spmd, %region_1.0_spmd} | conditional | bytes 6553616 | solution.py:370
  6.6 1.1 %branch_0_fun.4 = bf16[8,400,128]{2,1,0:T(8,128)(2,1)S(1)} custom-call(bf16[48,768]{1,0:T(8,128)(2,1)} %get-tuple-element.64.first, bf16[48,768]{1,0:T(8,128)(2,1)} %get-tuple-element.65.second), custom_call_target="tpu_custom_call" | custom-call | tf_op jit(solution)/shard_map/cond/branch_0_fun/pallas_call | solution.py:367
  7.6 21.6 %all_to_all.24 = bf16[8,400,128]{2,1,0:T(8,128)(2,1)S(1)} all-to-all(bf16[8,400,128]{2,1,0:T(8,128)(2,1)S(1)} %branch_0_fun.4), channel_id=1, replica_groups=mesh['z'=8,'y'=4,'x'=4,'c'=2] {'z'}, dimensions={0} | all-to-all | bytes 1638400 | tf_op jit(solution)/shard_map/cond/branch_0_fun/all_to_all | solution.py:326
  29.2 0.1 copy.11
  29.3 0.3 collective-permute-start.1
  29.6 0.3 collective-permute-start.2
  29.9 1.8 %collective-permute-done.1.y_ref = bf16[8,400,128]{2,1,0:T(8,128)(2,1)S(1)} collective-permute-done((bf16[8,400,128]{2,1,0:T(8,128)(2,1)S(1)}, bf16[8,400,128]{2,1,0:T(8,128)(2,1)S(1)}, u32[]{:S(2)}, u32[]{:S(2)}) %collective-permute-start.1) | collective-permute-done | bytes 819232 | tf_op jit(solution)/shard_map/ppermute | solution.py:330
  31.7 0.5 shard_map.59
  32.2 0.6 collective-permute-done.2
  32.9 16.3 %conditional.4 = (bf16[8,400,128]{2,1,0:T(8,128)(2,1)S(1)}, f32[8,128]{1,0:T(8,128)S(1)}, f32[8,128]{1,0:T(8,128)S(1)}) conditional(s32[]{:T(128)} %convert_element_type.2, (bf16[8,400,128]{2,1,0:T(8,128)(2,1)S(1)}, bf16[8,400,128]{2,1,0:T(8,128)(2,1)S(1)}, bf16[8,400,128]{2,1,0:T(8,128)(2,1)S(1)}, f32[8,128]{1,0:T(8,128)S(1)}, ...), branch_computations={%region_2.0_spmd, %region_4.0_spmd} | conditional | flops 15360 | bytes 200732 | solution.py:390
  32.9 1.6 %branch_0_fun.5 = (bf16[8,400,128]{2,1,0:T(8,128)(2,1)S(1)}, f32[8,8,128]{2,1,0:T(8,128)S(1)}, f32[8,128]{1,0:T(8,128)S(1)}) custom-call(bf16[8,400,128]{2,1,0:T(8,128)(2,1)S(1)} %get-tuple-element.68.free_ref, bf16[8,400,128]{2,1,0:T(8,128)(2,1)S(1)} %get-tuple-element.69.x1_ref, ...), custom_call_target="tpu_custom_call", output_to_operand_aliasing={{0}: (0, {})} | custom-call | tf_op jit(solution)/shard_map/cond/branch_0_fun/pallas_call | solution.py:382
  34.4 14.7 %all_to_all.26 = f32[8,8,128]{2,1,0:T(8,128)S(1)} all-to-all(f32[8,8,128]{2,1,0:T(8,128)S(1)} %get-tuple-element.76), channel_id=1, replica_groups=mesh['z'=8,'y'=4,'x'=4,'c'=2] {'z'}, dimensions={0} | all-to-all | bytes 65536 | tf_op jit(solution)/shard_map/cond/branch_0_fun/all_to_all | solution.py:326
  49.1 0.1 collective-permute-start.3
  49.2 1.2 %collective-permute-done.3 = f32[8,128]{1,0:T(8,128)S(1)} collective-permute-done((f32[8,128]{1,0:T(8,128)S(1)}, f32[8,128]{1,0:T(8,128)S(1)}, u32[]{:S(2)}, u32[]{:S(2)}) %collective-permute-start.3) | collective-permute-done | bytes 4128 | tf_op jit(solution)/shard_map/ppermute | solution.py:330
  50.4 21.8 %conditional.5 = ((f32[32,768]{1,0:T(8,128)S(1)}, f32[40,768]{1,0:T(8,128)S(1)}, f32[8,128]{1,0:T(8,128)S(1)})) conditional(s32[]{:T(128)} %convert_element_type.2, (bf16[8,128,128]{2,1,0:T(8,128)(2,1)S(1)}, bf16[8,400,128]{2,1,0:T(8,128)(2,1)S(1)}, f32[8,128]{1,0:T(8,128)S(1)}, f32[8,128]{1,0:T(8,128)S(1)}, f32[8,128]{1,0:T(8,128)S(1)}, ...), branch_computations={%region_6.0_spmd, %region_7.0_spmd} | conditional | bytes 3276808 | solution.py:407
  50.4 1.2 %branch_0_fun.6 = s16[8,400,128]{2,1,0:T(8,128)(2,1)S(1)} custom-call(bf16[8,128,128]{2,1,0:T(8,128)(2,1)S(1)} %get-tuple-element.87.first_ref, bf16[8,400,128]{2,1,0:T(8,128)(2,1)S(1)} %get-tuple-element.88.second_ref, f32[8,128]{1,0:T(8,128)S(1)} %get-tuple-element.89.match_ref, f32[8,128]{1,0:T(8,128)S(1)} %get-tuple-element.90.mine_ref, ...), custom_call_target="tpu_custom_call" | custom-call | tf_op jit(solution)/shard_map/cond/branch_0_fun/pallas_call | solution.py:398
  51.6 19.4 %all_to_all.28.parts = s16[8,400,128]{2,1,0:T(8,128)(2,1)S(1)} all-to-all(s16[8,400,128]{2,1,0:T(8,128)(2,1)S(1)} %branch_0_fun.6), channel_id=1, replica_groups=mesh['z'=8,'y'=4,'x'=4,'c'=2] {'z'}, dimensions={0} | all-to-all | bytes 1638400 | tf_op jit(solution)/shard_map/cond/branch_0_fun/all_to_all | solution.py:326
  70.9 1.3 %branch_0_fun.7 = (f32[32,768]{1,0:T(8,128)S(1)}, f32[40,768]{1,0:T(8,128)S(1)}, f32[8,128]{1,0:T(8,128)S(1)}) custom-call(bf16[48,768]{1,0:T(8,128)(2,1)} %get-tuple-element.85.first, bf16[48,768]{1,0:T(8,128)(2,1)} %get-tuple-element.86.second, s16[8,400,128]{2,1,0:T(8,128)(2,1)S(1)} %all_to_all.28.parts), custom_call_target="tpu_custom_call" | custom-call | tf_op jit(solution)/shard_map/cond/branch_0_fun/pallas_call | solution.py:402
  72.2 0.7 collective-permute-start.4
  72.9 1.0 %collective-permute-done.4.recv_ref = f32[40,768]{1,0:T(8,128)S(1)} collective-permute-done((f32[40,768]{1,0:T(8,128)S(1)}, f32[40,768]{1,0:T(8,128)S(1)}, u32[]{:S(2)}, u32[]{:S(2)}) %collective-permute-start.4) | collective-permute-done | bytes 122912 | tf_op jit(solution)/shard_map/ppermute | solution.py:330
  73.9 0.7 shard_map.60
  (1 shorter events, 0.0 us)
Async XLA Ops:
  2.2 4.4 %collective-permute-start = (bf16[48,768]{1,0:T(8,128)(2,1)S(1)}, bf16[48,768]{1,0:T(8,128)(2,1)}, u32[]{:S(2)}, u32[]{:S(2)}) collective-permute-start(bf16[48,768]{1,0:T(8,128)(2,1)S(1)} %get-tuple-element.121), channel_id=1, source_target_pairs={{0,1},{1,0},{2,3},{3,2},{4,5},{5,4},{6,7},{7,6},{8,9},{9,8},{10,11... | collective-permute-start | bytes 221192 | tf_op jit(solution)/shard_map/ppermute | solution.py:330
  29.3 2.4 %collective-permute-start.1 = (bf16[8,400,128]{2,1,0:T(8,128)(2,1)S(1)}, bf16[8,400,128]{2,1,0:T(8,128)(2,1)S(1)}, u32[]{:S(2)}, u32[]{:S(2)}) collective-permute-start(bf16[8,400,128]{2,1,0:T(8,128)(2,1)S(1)} %get-tuple-element.123.x_ref), channel_id=1, source_target_pairs={{0,1},{1,0},{2,3},{3,2},{4,5},{5,4},{6,7},{7,6},{8,9},{9,8},{10,11... | collective-permute-start | bytes 2457608 | tf_op jit(solution)/shard_map/ppermute | solution.py:330
  29.6 3.3 %collective-permute-start.2 = (bf16[8,400,128]{2,1,0:T(8,128)(2,1)S(1)}, bf16[8,400,128]{2,1,0:T(8,128)(2,1)S(1)}, u32[]{:S(2)}, u32[]{:S(2)}) collective-permute-start(bf16[8,400,128]{2,1,0:T(8,128)(2,1)S(1)} %get-tuple-element.125), channel_id=1, source_target_pairs={{0,1},{1,0},{2,3},{3,2},{4,5},{5,4},{6,7},{7,6},{8,9},{9,8},{10,11... | collective-permute-start | bytes 2457608 | tf_op jit(solution)/shard_map/ppermute | solution.py:330
  49.1 1.2 %collective-permute-start.3 = (f32[8,128]{1,0:T(8,128)S(1)}, f32[8,128]{1,0:T(8,128)S(1)}, u32[]{:S(2)}, u32[]{:S(2)}) collective-permute-start(f32[8,128]{1,0:T(8,128)S(1)} %get-tuple-element.130), channel_id=1, source_target_pairs={{0,1},{1,0},{2,3},{3,2},{4,5},{5,4},{6,7},{7,6},{8,9},{9,8},{10,11... | collective-permute-start | bytes 12296 | tf_op jit(solution)/shard_map/ppermute | solution.py:330
  72.2 1.7 %collective-permute-start.4 = (f32[40,768]{1,0:T(8,128)S(1)}, f32[40,768]{1,0:T(8,128)S(1)}, u32[]{:S(2)}, u32[]{:S(2)}) collective-permute-start(f32[40,768]{1,0:T(8,128)S(1)} %get-tuple-element.133), channel_id=1, source_target_pairs={{0,1},{1,0},{2,3},{3,2},{4,5},{5,4},{6,7},{7,6},{8,9},{9,8},{10,11... | collective-permute-start | bytes 368648 | tf_op jit(solution)/shard_map/ppermute | solution.py:330

commit v10 on v6

--- a/solution.py
+++ b/solution.py
@@ -12,7 +12,7 @@
 f32 = jnp.float32
 bf16 = jnp.bfloat16
 NT = (((1,), (1,)), ((), ()))
-PLANE, LINE = ("y", "x"), "z"
+PLANE, LINE = ("x", "y"), "z"
 EXTRA = 16
 
 

time: 72.3 us -> 72.2 us (level)
  no operation moved by 1% of the time
where the time goes in v10:
time: 72.2 us; the launch traced here: 71.9 us
  blocking collectives  55.3 us (77%)
  waiting for transfers between devices  6.31 us (9%)
  Pallas kernels  5.12 us (7%)
  starting transfers between devices  4.42 us (6%)
    all_to_all x3, blocking collectives, exchange(): return lax.all_to_all(x, axes, 0, 0)  55.3 us
    ppermute x4, waiting for transfers between devices, swap(): return lax.ppermute(x, 'c', [(0, 1), (1, 0)])  6.31 us
    ppermute x4, starting transfers between devices, swap(): return lax.ppermute(x, 'c', [(0, 1), (1, 0)])  4.42 us
    pallas_call x1, Pallas kernels, sums(): call(functools.partial(scores_kernel, images, rows), [((n_plane, packed,...  1.81 us
  transfers between devices with their start and end apart: 4, of which 4 were waited for; matrix products, arithmetic and copies ran while one was open for 0% of the time, Pallas kernels for 0%

profile of v10, /device:TPU:1, one launch (start us, length us, event | category | flops | bytes accessed | tf_op | source)
XLA Modules:
  0.0 71.9 jit_solution(647769568901265596)
XLA Ops:
  0.6 0.9 %shard_map.58 = (bf16[48,768]{1,0:T(8,128)(2,1)S(1)}, bf16[48,768]{1,0:T(8,128)(2,1)S(1)}) custom-call(bf16[32,768]{1,0:T(8,128)(2,1)} %img_hbm.1, bf16[32,768]{1,0:T(8,128)(2,1)} %txt_hbm.1, s32[1,32]{1,0:T(1,128)} %bitcast.2), custom_call_target="tpu_custom_call" | custom-call | tf_op jit(solution)/shard_map/pallas_call | solution.py:302
  1.6 3.3 %collective-permute-start = (bf16[48,768]{1,0:T(8,128)(2,1)S(1)}, bf16[48,768]{1,0:T(8,128)(2,1)S(1)}, u32[]{:S(2)}, u32[]{:S(2)}) collective-permute-start(bf16[48,768]{1,0:T(8,128)(2,1)S(1)} %get-tuple-element.89), channel_id=1, source_target_pairs={{0,1},{1,0},{2,3},{3,2},{4,5},{5,4},{6,7},{7,6},{8,9},{9,8},{10,11... | collective-permute-start | bytes 221192 | tf_op jit(solution)/shard_map/ppermute | solution.py:285
  4.9 0.9 %collective-permute-done = bf16[48,768]{1,0:T(8,128)(2,1)S(1)} collective-permute-done((bf16[48,768]{1,0:T(8,128)(2,1)S(1)}, bf16[48,768]{1,0:T(8,128)(2,1)S(1)}, u32[]{:S(2)}, u32[]{:S(2)}) %collective-permute-start) | collective-permute-done | bytes 73760 | tf_op jit(solution)/shard_map/ppermute | solution.py:285
  5.8 21.9 %conditional.3 = (bf16[16,400,128]{2,1,0:T(8,128)(2,1)S(1)}) conditional(s32[]{:T(128)} %convert_element_type.4, (bf16[48,768]{1,0:T(8,128)(2,1)S(1)}, bf16[48,768]{1,0:T(8,128)(2,1)S(1)}) %tuple.28, (bf16[48,768]{1,0:T(8,128)(2,1)S(1)}, bf16[48,768]{1,0:T(8,128)(2,1)S(1)}) %tuple.29), branch_computations={%region_0.1_spmd, %region_1.2_spmd} | conditional | bytes 4096010 | solution.py:324
  5.8 0.1 branch_0_fun.4
  6.0 21.6 %all_to_all.24 = bf16[8,400,128]{2,1,0:T(8,128)(2,1)S(1)} all-to-all(bf16[8,400,128]{2,1,0:T(8,128)(2,1)S(1)} %branch_0_fun.4), channel_id=1, replica_groups=mesh['z'=8,'y'=4,'x'=4,'c'=2] {'z'}, dimensions={0} | all-to-all | bytes 1638400 | tf_op jit(solution)/shard_map/cond/branch_0_fun/all_to_all | solution.py:281
  27.5 0.2 pad.3
  27.7 0.1 collective-permute-start.1
  27.8 3.5 %collective-permute-done.1 = bf16[16,400,128]{2,1,0:T(8,128)(2,1)S(1)} collective-permute-done((bf16[16,400,128]{2,1,0:T(8,128)(2,1)S(1)}, bf16[16,400,128]{2,1,0:T(8,128)(2,1)S(1)}, u32[]{:S(2)}, u32[]{:S(2)}) %collective-permute-start.1) | collective-permute-done | bytes 1638432 | tf_op jit(solution)/shard_map/ppermute | solution.py:285
  31.3 16.1 %conditional.4 = (bf16[16,400,128]{2,1,0:T(8,128)(2,1)S(1)}, f32[8,128]{1,0:T(8,128)S(1)}, f32[8,128]{1,0:T(8,128)S(1)}) conditional(s32[]{:T(128)} %convert_element_type.4, (bf16[16,400,128]{2,1,0:T(8,128)(2,1)S(1)}, bf16[16,400,128]{2,1,0:T(8,128)(2,1)S(1)}) %tuple.30, (bf16[16,400,128]{2,1,0:T(8,128)(2,1)S(1)}, ...), branch_computations={%region_2.4_spmd, %region_4.6_spmd} | conditional | flops 15360 | bytes 200732 | solution.py:337
  31.3 1.8 %branch_0_fun.5 = (bf16[16,400,128]{2,1,0:T(8,128)(2,1)S(1)}, f32[8,8,128]{2,1,0:T(8,128)S(1)}, f32[8,128]{1,0:T(8,128)S(1)}) custom-call(bf16[16,400,128]{2,1,0:T(8,128)(2,1)S(1)} %get-tuple-element.51.x_ref, bf16[16,400,128]{2,1,0:T(8,128)(2,1)S(1)} %get-tuple-element.52.y_ref), custom_call_target="tpu_custom_call", output_to_operand_aliasing={{0}: (0, {})} | custom-call | tf_op jit(solution)/shard_map/cond/branch_0_fun/pallas_call | solution.py:328
  33.1 14.3 %all_to_all.26 = f32[8,8,128]{2,1,0:T(8,128)S(1)} all-to-all(f32[8,8,128]{2,1,0:T(8,128)S(1)} %get-tuple-element.55), channel_id=1, replica_groups=mesh['z'=8,'y'=4,'x'=4,'c'=2] {'z'}, dimensions={0} | all-to-all | bytes 65536 | tf_op jit(solution)/shard_map/cond/branch_0_fun/all_to_all | solution.py:281
  47.4 0.3 collective-permute-start.2
  47.7 0.9 %collective-permute-done.2 = f32[8,128]{1,0:T(8,128)S(1)} collective-permute-done((f32[8,128]{1,0:T(8,128)S(1)}, f32[8,128]{1,0:T(8,128)S(1)}, u32[]{:S(2)}, u32[]{:S(2)}) %collective-permute-start.2) | collective-permute-done | bytes 4128 | tf_op jit(solution)/shard_map/ppermute | solution.py:285
  48.6 21.0 %conditional.5 = ((f32[32,768]{1,0:T(8,128)S(1)}, f32[40,768]{1,0:T(8,128)S(1)}, f32[8,128]{1,0:T(8,128)S(1)})) conditional(s32[]{:T(128)} %convert_element_type.4, (bf16[16,400,128]{2,1,0:T(8,128)(2,1)S(1)}, bf16[16,400,128]{2,1,0:T(8,128)(2,1)S(1)}, f32[8,128]{1,0:T(8,128)S(1)}, f32[8,128]{1,0:T(8,128)S(1)}, f32[8,128]{1,0:T(8,128)S(1)}, ...), branch_computations={%region_6.7_spmd, %region_7.8_spmd} | conditional | bytes 3276808 | solution.py:354
  48.6 1.2 %branch_0_fun.6 = s16[8,400,128]{2,1,0:T(8,128)(2,1)S(1)} custom-call(bf16[16,400,128]{2,1,0:T(8,128)(2,1)S(1)} %get-tuple-element.63.y_ref, bf16[16,400,128]{2,1,0:T(8,128)(2,1)S(1)} %get-tuple-element.64.e_ref, f32[8,128]{1,0:T(8,128)S(1)} %get-tuple-element.65.match_ref, f32[8,128]{1,0:T(8,128)S(1)} %get-tuple-element.66.mine_ref, ...), custom_call_target="tpu_custom_call" | custom-call | tf_op jit(solution)/shard_map/cond/branch_0_fun/pallas_call | solution.py:345
  49.8 19.4 %all_to_all.28.parts = s16[8,400,128]{2,1,0:T(8,128)(2,1)S(1)} all-to-all(s16[8,400,128]{2,1,0:T(8,128)(2,1)S(1)} %branch_0_fun.6), channel_id=1, replica_groups=mesh['z'=8,'y'=4,'x'=4,'c'=2] {'z'}, dimensions={0} | all-to-all | bytes 1638400 | tf_op jit(solution)/shard_map/cond/branch_0_fun/all_to_all | solution.py:281
  69.2 0.3 branch_0_fun.7
  69.6 0.7 collective-permute-start.3
  70.3 1.0 %collective-permute-done.3.recv_ref = f32[40,768]{1,0:T(8,128)S(1)} collective-permute-done((f32[40,768]{1,0:T(8,128)S(1)}, f32[40,768]{1,0:T(8,128)S(1)}, u32[]{:S(2)}, u32[]{:S(2)}) %collective-permute-start.3) | collective-permute-done | bytes 122912 | tf_op jit(solution)/shard_map/ppermute | solution.py:285
  71.2 0.7 shard_map.59
  (1 shorter events, 0.0 us)
Async XLA Ops:
  1.6 4.2 %collective-permute-start = (bf16[48,768]{1,0:T(8,128)(2,1)S(1)}, bf16[48,768]{1,0:T(8,128)(2,1)S(1)}, u32[]{:S(2)}, u32[]{:S(2)}) collective-permute-start(bf16[48,768]{1,0:T(8,128)(2,1)S(1)} %get-tuple-element.89), channel_id=1, source_target_pairs={{0,1},{1,0},{2,3},{3,2},{4,5},{5,4},{6,7},{7,6},{8,9},{9,8},{10,11... | collective-permute-start | bytes 221192 | tf_op jit(solution)/shard_map/ppermute | solution.py:285
  27.7 3.6 %collective-permute-start.1 = (bf16[16,400,128]{2,1,0:T(8,128)(2,1)S(1)}, bf16[16,400,128]{2,1,0:T(8,128)(2,1)S(1)}, u32[]{:S(2)}, u32[]{:S(2)}) collective-permute-start(bf16[16,400,128]{2,1,0:T(8,128)(2,1)S(1)} %get-tuple-element.112), channel_id=1, source_target_pairs={{0,1},{1,0},{2,3},{3,2},{4,5},{5,4},{6,7},{7,6},{8,9},{9,8},{10,11... | collective-permute-start | bytes 4915208 | tf_op jit(solution)/shard_map/ppermute | solution.py:285
  47.4 1.2 %collective-permute-start.2 = (f32[8,128]{1,0:T(8,128)S(1)}, f32[8,128]{1,0:T(8,128)S(1)}, u32[]{:S(2)}, u32[]{:S(2)}) collective-permute-start(f32[8,128]{1,0:T(8,128)S(1)} %get-tuple-element.93), channel_id=1, source_target_pairs={{0,1},{1,0},{2,3},{3,2},{4,5},{5,4},{6,7},{7,6},{8,9},{9,8},{10,11... | collective-permute-start | bytes 12296 | tf_op jit(solution)/shard_map/ppermute | solution.py:285
  69.6 1.7 %collective-permute-start.3 = (f32[40,768]{1,0:T(8,128)S(1)}, f32[40,768]{1,0:T(8,128)S(1)}, u32[]{:S(2)}, u32[]{:S(2)}) collective-permute-start(f32[40,768]{1,0:T(8,128)S(1)} %get-tuple-element.96), channel_id=1, source_target_pairs={{0,1},{1,0},{2,3},{3,2},{4,5},{5,4},{6,7},{7,6},{8,9},{9,8},{10,11... | collective-permute-start | bytes 368648 | tf_op jit(solution)/shard_map/ppermute | solution.py:285

commit v11 on v6

--- a/solution.py
+++ b/solution.py
@@ -198,6 +198,20 @@
     rest = [jnp.zeros((EXTRA - 2 - width // 128, 128), jnp.int32)]
     row_inv = f32(1.0) / mine_ref[:nx]
     y = unpack(y_ref, 0, ny * per, rows, width)
+    def store(b):
+        steps = []
+        for k in range(width // 128):
+            q, t = encode(
+                gs[b * 2 // blocks][
+                    b % (blocks // 2) * rows : (b % (blocks // 2) + 1) * rows,
+                    k * 128 : (k + 1) * 128,
+                ]
+            )
+            out_ref[b, k * rows : (k + 1) * rows, :] = q.astype(jnp.int16)
+            steps.append(t)
+        tile = jnp.concatenate(steps + share + rest, axis=0)
+        out_ref[b, packed - EXTRA :, :] = tile.astype(jnp.int16)
+
     gs = []
     ds = []
     for r in range(nx):
@@ -214,19 +228,8 @@
         if (r + 1) % (nx // 2) == 0:
             gs.append(jnp.dot(jnp.concatenate(ds, axis=0), y, preferred_element_type=f32))
             ds = []
-    for b in range(blocks):
-        steps = []
-        for k in range(width // 128):
-            q, t = encode(
-                gs[b * 2 // blocks][
-                    b % (blocks // 2) * rows : (b % (blocks // 2) + 1) * rows,
-                    k * 128 : (k + 1) * 128,
-                ]
-            )
-            out_ref[b, k * rows : (k + 1) * rows, :] = q.astype(jnp.int16)
-            steps.append(t)
-        tile = jnp.concatenate(steps + share + rest, axis=0)
-        out_ref[b, packed - EXTRA :, :] = tile.astype(jnp.int16)
+            for b in range((len(gs) - 1) * blocks // 2, len(gs) * blocks // 2):
+                store(b)
 
 
 def finish_kernel(scale, keep_first, first, second, parts, keep_ref, send_ref, share_ref):

time: 72.3 us -> 72.3 us (level)
  no operation moved by 1% of the time
where the time goes in v11:
time: 72.3 us; the launch traced here: 72 us
  blocking collectives  55.3 us (76%)
  waiting for transfers between devices  6.43 us (9%)
  Pallas kernels  5.12 us (7%)
  starting transfers between devices  4.32 us (6%)
    all_to_all x3, blocking collectives, exchange(): return lax.all_to_all(x, axes, 0, 0)  55.3 us
    ppermute x4, waiting for transfers between devices, swap(): return lax.ppermute(x, 'c', [(0, 1), (1, 0)])  6.43 us
    ppermute x4, starting transfers between devices, swap(): return lax.ppermute(x, 'c', [(0, 1), (1, 0)])  4.32 us
    pallas_call x1, Pallas kernels, sums(): call(functools.partial(scores_kernel, images, rows), [((n_plane, packed,...  1.81 us
  transfers between devices with their start and end apart: 4, of which 4 were waited for; matrix products, arithmetic and copies ran while one was open for 0% of the time, Pallas kernels for 0%

profile of v11, /device:TPU:1, one launch (start us, length us, event | category | flops | bytes accessed | tf_op | source)
XLA Modules:
  0.0 72.0 jit_solution(12840626010865957701)
XLA Ops:
  0.6 0.9 %shard_map.58 = (bf16[48,768]{1,0:T(8,128)(2,1)S(1)}, bf16[48,768]{1,0:T(8,128)(2,1)S(1)}) custom-call(bf16[32,768]{1,0:T(8,128)(2,1)} %img_hbm.1, bf16[32,768]{1,0:T(8,128)(2,1)} %txt_hbm.1, s32[1,32]{1,0:T(1,128)} %bitcast.2), custom_call_target="tpu_custom_call" | custom-call | tf_op jit(solution)/shard_map/pallas_call | solution.py:305
  1.6 3.3 %collective-permute-start = (bf16[48,768]{1,0:T(8,128)(2,1)S(1)}, bf16[48,768]{1,0:T(8,128)(2,1)S(1)}, u32[]{:S(2)}, u32[]{:S(2)}) collective-permute-start(bf16[48,768]{1,0:T(8,128)(2,1)S(1)} %get-tuple-element.89), channel_id=1, source_target_pairs={{0,1},{1,0},{2,3},{3,2},{4,5},{5,4},{6,7},{7,6},{8,9},{9,8},{10,11... | collective-permute-start | bytes 221192 | tf_op jit(solution)/shard_map/ppermute | solution.py:288
  4.9 0.9 %collective-permute-done = bf16[48,768]{1,0:T(8,128)(2,1)S(1)} collective-permute-done((bf16[48,768]{1,0:T(8,128)(2,1)S(1)}, bf16[48,768]{1,0:T(8,128)(2,1)S(1)}, u32[]{:S(2)}, u32[]{:S(2)}) %collective-permute-start) | collective-permute-done | bytes 73760 | tf_op jit(solution)/shard_map/ppermute | solution.py:288
  5.8 21.9 %conditional.3 = (bf16[16,400,128]{2,1,0:T(8,128)(2,1)S(1)}) conditional(s32[]{:T(128)} %convert_element_type.4, (bf16[48,768]{1,0:T(8,128)(2,1)S(1)}, bf16[48,768]{1,0:T(8,128)(2,1)S(1)}) %tuple.28, (bf16[48,768]{1,0:T(8,128)(2,1)S(1)}, bf16[48,768]{1,0:T(8,128)(2,1)S(1)}) %tuple.29), branch_computations={%region_0.1_spmd, %region_1.2_spmd} | conditional | bytes 4096010 | solution.py:327
  5.8 0.1 branch_0_fun.4
  6.0 21.6 %all_to_all.24 = bf16[8,400,128]{2,1,0:T(8,128)(2,1)S(1)} all-to-all(bf16[8,400,128]{2,1,0:T(8,128)(2,1)S(1)} %branch_0_fun.4), channel_id=1, replica_groups=mesh['z'=8,'y'=4,'x'=4,'c'=2] {'z'}, dimensions={0} | all-to-all | bytes 1638400 | tf_op jit(solution)/shard_map/cond/branch_0_fun/all_to_all | solution.py:284
  27.5 0.2 pad.3
  27.7 0.1 collective-permute-start.1
  27.8 3.5 %collective-permute-done.1 = bf16[16,400,128]{2,1,0:T(8,128)(2,1)S(1)} collective-permute-done((bf16[16,400,128]{2,1,0:T(8,128)(2,1)S(1)}, bf16[16,400,128]{2,1,0:T(8,128)(2,1)S(1)}, u32[]{:S(2)}, u32[]{:S(2)}) %collective-permute-start.1) | collective-permute-done | bytes 1638432 | tf_op jit(solution)/shard_map/ppermute | solution.py:288
  31.3 16.2 %conditional.4 = (bf16[16,400,128]{2,1,0:T(8,128)(2,1)S(1)}, f32[8,128]{1,0:T(8,128)S(1)}, f32[8,128]{1,0:T(8,128)S(1)}) conditional(s32[]{:T(128)} %convert_element_type.4, (bf16[16,400,128]{2,1,0:T(8,128)(2,1)S(1)}, bf16[16,400,128]{2,1,0:T(8,128)(2,1)S(1)}) %tuple.30, (bf16[16,400,128]{2,1,0:T(8,128)(2,1)S(1)}, ...), branch_computations={%region_2.4_spmd, %region_4.6_spmd} | conditional | flops 15360 | bytes 200732 | solution.py:340
  31.3 1.8 %branch_0_fun.5 = (bf16[16,400,128]{2,1,0:T(8,128)(2,1)S(1)}, f32[8,8,128]{2,1,0:T(8,128)S(1)}, f32[8,128]{1,0:T(8,128)S(1)}) custom-call(bf16[16,400,128]{2,1,0:T(8,128)(2,1)S(1)} %get-tuple-element.51.x_ref, bf16[16,400,128]{2,1,0:T(8,128)(2,1)S(1)} %get-tuple-element.52.y_ref), custom_call_target="tpu_custom_call", output_to_operand_aliasing={{0}: (0, {})} | custom-call | tf_op jit(solution)/shard_map/cond/branch_0_fun/pallas_call | solution.py:331
  33.1 14.4 %all_to_all.26 = f32[8,8,128]{2,1,0:T(8,128)S(1)} all-to-all(f32[8,8,128]{2,1,0:T(8,128)S(1)} %get-tuple-element.55), channel_id=1, replica_groups=mesh['z'=8,'y'=4,'x'=4,'c'=2] {'z'}, dimensions={0} | all-to-all | bytes 65536 | tf_op jit(solution)/shard_map/cond/branch_0_fun/all_to_all | solution.py:284
  47.5 0.2 collective-permute-start.2
  47.7 1.1 %collective-permute-done.2 = f32[8,128]{1,0:T(8,128)S(1)} collective-permute-done((f32[8,128]{1,0:T(8,128)S(1)}, f32[8,128]{1,0:T(8,128)S(1)}, u32[]{:S(2)}, u32[]{:S(2)}) %collective-permute-start.2) | collective-permute-done | bytes 4128 | tf_op jit(solution)/shard_map/ppermute | solution.py:288
  48.8 20.9 %conditional.5 = ((f32[32,768]{1,0:T(8,128)S(1)}, f32[40,768]{1,0:T(8,128)S(1)}, f32[8,128]{1,0:T(8,128)S(1)})) conditional(s32[]{:T(128)} %convert_element_type.4, (bf16[16,400,128]{2,1,0:T(8,128)(2,1)S(1)}, bf16[16,400,128]{2,1,0:T(8,128)(2,1)S(1)}, f32[8,128]{1,0:T(8,128)S(1)}, f32[8,128]{1,0:T(8,128)S(1)}, f32[8,128]{1,0:T(8,128)S(1)}, ...), branch_computations={%region_6.7_spmd, %region_7.8_spmd} | conditional | bytes 3276808 | solution.py:357
  48.8 1.2 %branch_0_fun.6 = s16[8,400,128]{2,1,0:T(8,128)(2,1)S(1)} custom-call(bf16[16,400,128]{2,1,0:T(8,128)(2,1)S(1)} %get-tuple-element.63.y_ref, bf16[16,400,128]{2,1,0:T(8,128)(2,1)S(1)} %get-tuple-element.64.e_ref, f32[8,128]{1,0:T(8,128)S(1)} %get-tuple-element.65.match_ref, f32[8,128]{1,0:T(8,128)S(1)} %get-tuple-element.66.mine_ref, ...), custom_call_target="tpu_custom_call" | custom-call | tf_op jit(solution)/shard_map/cond/branch_0_fun/pallas_call | solution.py:348
  49.9 19.4 %all_to_all.28.parts = s16[8,400,128]{2,1,0:T(8,128)(2,1)S(1)} all-to-all(s16[8,400,128]{2,1,0:T(8,128)(2,1)S(1)} %branch_0_fun.6), channel_id=1, replica_groups=mesh['z'=8,'y'=4,'x'=4,'c'=2] {'z'}, dimensions={0} | all-to-all | bytes 1638400 | tf_op jit(solution)/shard_map/cond/branch_0_fun/all_to_all | solution.py:284
  69.3 0.3 branch_0_fun.7
  69.7 0.7 collective-permute-start.3
  70.4 1.0 %collective-permute-done.3.recv_ref = f32[40,768]{1,0:T(8,128)S(1)} collective-permute-done((f32[40,768]{1,0:T(8,128)S(1)}, f32[40,768]{1,0:T(8,128)S(1)}, u32[]{:S(2)}, u32[]{:S(2)}) %collective-permute-start.3) | collective-permute-done | bytes 122912 | tf_op jit(solution)/shard_map/ppermute | solution.py:288
  71.3 0.7 shard_map.59
  (1 shorter events, 0.0 us)
Async XLA Ops:
  1.6 4.2 %collective-permute-start = (bf16[48,768]{1,0:T(8,128)(2,1)S(1)}, bf16[48,768]{1,0:T(8,128)(2,1)S(1)}, u32[]{:S(2)}, u32[]{:S(2)}) collective-permute-start(bf16[48,768]{1,0:T(8,128)(2,1)S(1)} %get-tuple-element.89), channel_id=1, source_target_pairs={{0,1},{1,0},{2,3},{3,2},{4,5},{5,4},{6,7},{7,6},{8,9},{9,8},{10,11... | collective-permute-start | bytes 221192 | tf_op jit(solution)/shard_map/ppermute | solution.py:288
  27.7 3.6 %collective-permute-start.1 = (bf16[16,400,128]{2,1,0:T(8,128)(2,1)S(1)}, bf16[16,400,128]{2,1,0:T(8,128)(2,1)S(1)}, u32[]{:S(2)}, u32[]{:S(2)}) collective-permute-start(bf16[16,400,128]{2,1,0:T(8,128)(2,1)S(1)} %get-tuple-element.112), channel_id=1, source_target_pairs={{0,1},{1,0},{2,3},{3,2},{4,5},{5,4},{6,7},{7,6},{8,9},{9,8},{10,11... | collective-permute-start | bytes 4915208 | tf_op jit(solution)/shard_map/ppermute | solution.py:288
  47.5 1.2 %collective-permute-start.2 = (f32[8,128]{1,0:T(8,128)S(1)}, f32[8,128]{1,0:T(8,128)S(1)}, u32[]{:S(2)}, u32[]{:S(2)}) collective-permute-start(f32[8,128]{1,0:T(8,128)S(1)} %get-tuple-element.93), channel_id=1, source_target_pairs={{0,1},{1,0},{2,3},{3,2},{4,5},{5,4},{6,7},{7,6},{8,9},{9,8},{10,11... | collective-permute-start | bytes 12296 | tf_op jit(solution)/shard_map/ppermute | solution.py:288
  69.7 1.7 %collective-permute-start.3 = (f32[40,768]{1,0:T(8,128)S(1)}, f32[40,768]{1,0:T(8,128)S(1)}, u32[]{:S(2)}, u32[]{:S(2)}) collective-permute-start(f32[40,768]{1,0:T(8,128)S(1)} %get-tuple-element.96), channel_id=1, source_target_pairs={{0,1},{1,0},{2,3},{3,2},{4,5},{5,4},{6,7},{7,6},{8,9},{9,8},{10,11... | collective-permute-start | bytes 368648 | tf_op jit(solution)/shard_map/ppermute | solution.py:288
